TPU v7x, 32 devices: a whole 2x2x4 slice. The times are simulated.
32 devices in a mesh: segment: 4 (over y, x), expert: 4 (over z), dp: 2 (over core).
Axes of the slice: x: 2, y: 2, z: 4, core: 2. Of those that a mesh axis runs over, the one named last changes fastest.
Arguments:
- activations: bfloat16 [4, 256, 8, 512], P('segment', ('expert', 'dp')), may hold values from -6 to 6
- upstream: bfloat16 [4, 256, 8, 512], P('segment', ('expert', 'dp')), may hold values from -6 to 6
- routes: int32 [4, 256, 2], P('segment', ('expert', 'dp')), may hold values from 0 to 3, all different within a row; in each aligned block of 32 rows (0 to 31, 32 to 63, ..., all dimensions but the last counted through in order) at most 32 rows name the same one
- gate_codes: int32 [4, 256, 2], P('segment', ('expert', 'dp')), may hold values from 1 to 32767
- weights: bfloat16 [4, 4, 9, 64, 512], P('segment', 'expert'), may hold values from -0.25 to 0.25
Outputs:
- input_grad: bfloat16 [4, 256, 8, 512], P('segment', ('expert', 'dp'))
- weight_grad: float32 [4, 4, 9, 64, 512], P('segment', 'expert')
Inputs may be any that keep to these rules, and one draw needn't show every extreme that they name: `routes`: the two experts of a tile differ; the 32 tiles of one device name each expert at most 32 times, and on some devices one expert exactly 32 times.
All inputs are finite; a program needn't handle non-finite values.
Results may differ from a plain program's by a relative error of at most 0.004.
Values may be sent and summed in bfloat16 or wider, within the bound.
No kernel may reach another device: no remote copies, remote signals or barrier semaphores. Data moves between devices by JAX's collectives and lax.ppermute only.
A program may use at most 64 MiB of HBM per device.

v0:
```python
import jax
import jax.numpy as jnp
import numpy as np
from jax import lax
from jax.sharding import PartitionSpec as P

TH = 4
TW = 2


def shifted(array, axis, by):
    count = lax.axis_size(axis)
    return lax.ppermute(array, axis, [(i, (i + by) % count) for i in range(count)])


def offsets_table():
    cell_count = TH * TW
    table = np.zeros((cell_count, cell_count, 9), np.float32)
    for source_cell in range(cell_count):
        for target_cell in range(cell_count):
            row_step = target_cell // TW - source_cell // TW
            col_step = target_cell % TW - source_cell % TW
            if abs(row_step) <= 1 and abs(col_step) <= 1:
                table[source_cell, target_cell, (row_step + 1) * 3 + col_step + 1] = 1.0
    return table


def by_group(rows, group_width):
    tile_count = rows.shape[0]
    cell_count = rows.shape[1]
    group_count = rows.shape[2] // group_width
    split = rows.reshape(tile_count, cell_count, group_count, group_width).transpose(2, 0, 1, 3)
    return split.reshape(group_count, tile_count, cell_count * group_width)


def transpose_conv(scaled_grads, weight):
    tile_count = scaled_grads.shape[0]
    cell_count = scaled_grads.shape[1]
    group_width = weight.shape[1]
    channels = weight.shape[2]
    group_count = channels // group_width
    selector = jnp.asarray(offsets_table(), jnp.bfloat16)
    split_weight = weight.reshape(9, group_width, group_count, group_width)
    blocks = jnp.einsum(
        "pqt,tcgo->gpoqc", selector, split_weight, preferred_element_type=jnp.float32
    )
    blocks = blocks.astype(jnp.bfloat16).reshape(
        group_count, cell_count * group_width, cell_count * group_width
    )
    grouped = by_group(scaled_grads, group_width)
    result = jnp.einsum("gnk,gkm->gnm", grouped, blocks, preferred_element_type=jnp.float32)
    result = result.reshape(group_count, tile_count, cell_count, group_width).transpose(1, 2, 0, 3)
    return result.reshape(tile_count, cell_count, channels)


def weight_corr(inputs, scaled_grads, group_width):
    cell_count = inputs.shape[1]
    channels = inputs.shape[2]
    group_count = channels // group_width
    grouped_inputs = by_group(inputs, group_width)
    grouped_grads = by_group(scaled_grads, group_width)
    moments = jnp.einsum(
        "gnk,gnm->gkm", grouped_inputs, grouped_grads, preferred_element_type=jnp.float32
    )
    moments = moments.reshape(group_count, cell_count, group_width, cell_count, group_width)
    selector = jnp.asarray(offsets_table(), jnp.float32)
    taps = jnp.einsum("gpcqo,qpt->tcgo", moments, selector, precision=lax.Precision.HIGHEST)
    return taps.reshape(9, group_width, channels)


def body(activations, upstream, routes, gate_codes, weights):
    incoming = shifted(upstream, "segment", -1)[0]
    inputs = activations[0]
    route_ids = routes[0]
    code_values = gate_codes[0].astype(jnp.float32)
    kernel = weights[0, 0]
    group_width = kernel.shape[1]
    per_device = inputs.shape[0]
    cell_count = inputs.shape[1]
    channels = inputs.shape[2]
    experts = lax.axis_size("expert")
    capacity = max(2, 4 * per_device // experts)
    gate_share = code_values / jnp.sum(code_values, axis=1, keepdims=True)
    scaled_grads = (gate_share[:, :, None, None] * incoming[:, None].astype(jnp.float32)).astype(
        jnp.bfloat16
    )
    grad_rows = scaled_grads.reshape(2 * per_device, cell_count * channels)
    input_rows = jnp.repeat(inputs, 2, axis=0).reshape(2 * per_device, cell_count * channels)
    flat_expert = route_ids.reshape(-1)
    matches = (flat_expert[:, None] == jnp.arange(experts, dtype=jnp.int32)[None, :]).astype(
        jnp.int32
    )
    earlier = jnp.cumsum(matches, axis=0) - matches
    slot_rank = jnp.sum(earlier * matches, axis=1)
    slot_place = flat_expert * capacity + slot_rank
    chooser = (
        slot_place[None, :] == jnp.arange(experts * capacity, dtype=jnp.int32)[:, None]
    ).astype(jnp.bfloat16)

    def pack_slots(rows):
        packed = jnp.dot(chooser, rows, preferred_element_type=jnp.float32).astype(jnp.bfloat16)
        return packed.reshape(experts, capacity, cell_count, channels)

    inputs_recv, grads_recv = (
        lax.all_to_all(pack_slots(input_rows), "expert", split_axis=0, concat_axis=0, tiled=True),
        lax.all_to_all(pack_slots(grad_rows), "expert", split_axis=0, concat_axis=0, tiled=True),
    )
    flat_grads = grads_recv.reshape(experts * capacity, cell_count, channels)
    answers = transpose_conv(flat_grads, kernel).astype(jnp.bfloat16)
    returned = lax.all_to_all(
        answers.reshape(experts, capacity, cell_count, channels),
        "expert",
        split_axis=0,
        concat_axis=0,
        tiled=True,
    )
    flat_inputs = inputs_recv.reshape(experts * capacity, cell_count, channels)
    local_grad = weight_corr(flat_inputs, flat_grads, group_width)
    flat_answers = returned.reshape(experts * capacity, cell_count * channels)
    per_route = jnp.dot(chooser.T, flat_answers, preferred_element_type=jnp.float32).reshape(
        per_device, 2, cell_count, channels
    )
    input_grad = (incoming.astype(jnp.float32) + per_route[:, 0] + per_route[:, 1]).astype(
        jnp.bfloat16
    )
    total_grad = lax.psum(local_grad, "dp") / per_device
    return (input_grad[None], total_grad[None, None])


def solution(mesh):
    placed = (
        P("segment", ("expert", "dp"), None, None),
        P("segment", ("expert", "dp"), None, None),
        P("segment", ("expert", "dp"), None),
        P("segment", ("expert", "dp"), None),
        P("segment", "expert", None, None, None),
    )
    return jax.shard_map(
        body,
        mesh=mesh,
        in_specs=placed,
        out_specs=(
            P("segment", ("expert", "dp"), None, None),
            P("segment", "expert", None, None, None),
        ),
        check_vma=False,
    )
```

profile of v0, /device:TPU:19, one launch (start us, length us, event | category | flops | bytes accessed | tf_op | source)
XLA Modules:
  0.0 169.3 jit_solution(13103199921764056042)
XLA Ops:
  10.0 1.4 copy.46
  11.4 4.6 %all-to-all-start.2 = ((bf16[4,32,8,512]{3,2,1,0:T(8,128)(2,1)}), bf16[4,32,8,512]{3,2,1,0:T(8,128)(2,1)S(1)}, u32[]{:S(2)}, u32[]{:S(2)}) async-start(bf16[4,32,8,512]{3,2,1,0:T(8,128)(2,1)} %bitcast.54), calls=%async_computation.2 | async-start | bytes 2097152 | tf_op jit(solution)/shard_map/all_to_all | solution.py:105
  16.9 6.8 %collective-permute-done = bf16[1,32,8,512]{3,1,2,0:T(8,128)(2,1)S(1)} collective-permute-done((bf16[1,32,8,512]{3,1,2,0:T(8,128)(2,1)S(1)}, bf16[1,32,8,512]{3,1,2,0:T(8,128)(2,1)S(1)}, u32[]{:S(2)}, u32[]{:S(2)}) %collective-permute-start) | collective-permute-done | bytes 262176 | tf_op jit(solution)/shard_map/ppermute | solution.py:13
  25.3 1.4 copy.43
  26.6 11.6 %all-to-all-done.2 = bf16[4,32,8,512]{3,2,1,0:T(8,128)(2,1)S(1)} async-done(((bf16[4,32,8,512]{3,2,1,0:T(8,128)(2,1)}), bf16[4,32,8,512]{3,2,1,0:T(8,128)(2,1)S(1)}, u32[]{:S(2)}, u32[]{:S(2)}) %all-to-all-start.2) | async-done | bytes 1048608 | tf_op jit(solution)/shard_map/all_to_all | solution.py:105
  38.3 7.2 %all-to-all-start = ((bf16[4,32,8,512]{3,2,1,0:T(8,128)(2,1)}), bf16[4,32,8,512]{3,2,1,0:T(8,128)(2,1)}, u32[]{:S(2)}, u32[]{:S(2)}) async-start(bf16[4,32,8,512]{3,2,1,0:T(8,128)(2,1)} %bitcast.41), calls=%async_computation | async-start | bytes 2097152 | tf_op jit(solution)/shard_map/all_to_all | solution.py:106
  46.1 5.5 %convert_bitcast_fusion = bf16[8,8,64,8,64]{2,3,0,4,1:T(8,128)(2,1)} fusion(bf16[8,8,9,1,1]{2,1,4,3,0:T(8,128)(2,1)S(1)} %copy-done.6, bf16[9,64,8,64]{3,2,1,0:T(8,128)(2,1)S(1)} %reshape_squeeze.7), kind=kOutput, calls=%fused_computation | convolution fusion | flops 39845888 | bytes 4785280 | tf_op jit(solution)/shard_map/pqt,tcgo->gpoqc/dot_general | solution.py:44
  51.6 15.0 %copy.26 = bf16[8,8,64,8,64]{4,3,2,1,0:T(8,128)(2,1)} copy(bf16[8,8,64,8,64]{2,3,0,4,1:T(8,128)(2,1)} %convert_bitcast_fusion) | data formatting | bytes 8388608 | tf_op jit(solution)/shard_map/convert_element_type | solution.py:47
  66.6 11.8 %reshape.104 = bf16[8,512,512]{2,1,0:T(8,128)(2,1)} reshape(bf16[8,8,64,8,64]{4,3,2,1,0:T(8,128)(2,1)} %copy.26) | data formatting | bytes 8388608 | tf_op jit(solution)/shard_map/reshape | solution.py:47
  79.6 2.9 %copy.31 = bf16[8,128,8,64]{1,3,2,0:T(8,128)(2,1)} copy(bf16[8,128,8,64]{3,0,2,1:T(8,128)(2,1)S(1)} %bitcast.91) | data formatting | bytes 2097152 | tf_op jit(solution)/shard_map/transpose | solution.py:32
  82.5 2.8 %reshape_reshape.10 = bf16[128,8,8,64]{3,2,1,0:T(8,128)(2,1)S(1)} reshape(bf16[4,32,8,512]{3,2,1,0:T(8,128)(2,1)} %all-to-all-done) | data formatting | bytes 2097152 | tf_op jit(solution)/shard_map/reshape;reshape | solution.py:32
  85.3 2.1 %copy.24 = bf16[8,128,8,64]{1,3,2,0:T(8,128)(2,1)S(1)} copy(bf16[8,128,8,64]{3,0,2,1:T(8,128)(2,1)S(1)} %bitcast.92) | data formatting | bytes 2097152 | tf_op jit(solution)/shard_map/transpose | solution.py:32
  87.4 3.0 %convolution_convert_fusion.2 = bf16[8,128,512]{2,1,0:T(8,128)(2,1)S(1)} fusion(bf16[8,128,512]{1,2,0:T(8,128)(2,1)S(1)} %bitcast.89, bf16[8,512,512]{2,1,0:T(8,128)(2,1)} %reshape.104), kind=kOutput, calls=%fused_computation.6 | convolution fusion | flops 537395200 | bytes 6291456 | tf_op jit(solution)/shard_map/gnk,gkm->gnm/dot_general | solution.py:51
  90.4 1.3 copy.28
  91.7 3.9 %copy.29 = bf16[128,8,8,64]{3,2,1,0:T(8,128)(2,1)S(1)} copy(bf16[128,8,8,64]{0,3,1,2:T(8,128)(2,1)} %bitcast.94) | data formatting | bytes 2097152 | tf_op jit(solution)/shard_map/convert_element_type | solution.py:109
  95.7 2.1 %convert_element_type.76 = bf16[4,32,8,512]{3,2,1,0:T(8,128)(2,1)} reshape(bf16[128,8,8,64]{3,2,1,0:T(8,128)(2,1)S(1)} %copy.29) | data formatting | bytes 2097152 | tf_op jit(solution)/shard_map/convert_element_type | solution.py:109
  97.8 4.7 %all-to-all-start.1 = ((bf16[4,32,8,512]{3,2,1,0:T(8,128)(2,1)}), bf16[4,32,8,512]{3,2,1,0:T(8,128)(2,1)S(1)}, u32[]{:S(2)}, u32[]{:S(2)}) async-start(bf16[4,32,8,512]{3,2,1,0:T(8,128)(2,1)} %convert_element_type.76), calls=%async_computation.1 | async-start | bytes 2097152 | tf_op jit(solution)/shard_map/all_to_all | solution.py:110
  102.4 4.5 %fusion.13 = f32[8,512,512]{2,1,0:T(8,128)} fusion(bf16[8,128,512]{1,2,0:T(8,128)(2,1)S(1)} %bitcast.93, bf16[8,128,512]{1,2,0:T(8,128)(2,1)S(1)} %bitcast.90), kind=kOutput, calls=%fused_computation.30 | convolution fusion | flops 536870912 | bytes 10485760 | tf_op jit(solution)/shard_map/gnk,gnm->gkm/dot_general | solution.py:62
  106.9 12.9 %reshape.108 = f32[8,8,64,8,64]{4,3,2,1,0:T(8,128)} reshape(f32[8,512,512]{2,1,0:T(8,128)} %fusion.13) | data formatting | bytes 16777216 | tf_op jit(solution)/shard_map/reshape | solution.py:65
  119.8 11.4 %convolution_bitcast_fusion = f32[9,64,8,64]{3,0,1,2:T(8,128)S(1)} fusion(f32[8,8,64,8,64]{4,3,2,1,0:T(8,128)} %reshape.108, f32[8,8,9,1,1]{2,0,1,4,3:T(8,128)S(1)} %copy-done.5), kind=kOutput, calls=%fused_computation.3 | convolution fusion | flops 226492416 | bytes 9570560 | tf_op jit(solution)/shard_map/gpcqo,qpt->tcgo/dot_general | solution.py:67
  131.2 1.4 copy.34
  132.6 1.6 reshape.109
  134.4 23.0 %all-reduce.2.cloned.1.call-done = f32[9,64,512]{2,1,0:T(8,128)} async-done(((f32[9,64,512]{2,1,0:T(8,128)}), f32[9,64,512]{2,1,0:T(8,128)}) %all-reduce.2.cloned.1.call-update) | async-done | bytes 1179664 | tf_op jit(solution)/shard_map/psum | solution.py:126
  157.4 2.4 %multiply_bitcast_fusion = f32[1,1,9,64,512]{4,3,2,1,0:T(8,128)} fusion(f32[9,64,512]{2,1,0:T(8,128)} %all-reduce.2.cloned.1.call-done), kind=kLoop, calls=%fused_computation.7 | loop fusion | flops 294912 | bytes 2359296 | tf_op jit(solution)/shard_map/broadcast_in_dim | solution.py:127
  (55 shorter events, 9.7 us)
Async XLA Ops:
  10.0 6.0 %copy-start.4 = (bf16[1,32,8,512]{3,2,1,0:T(8,128)(2,1)S(1)}, bf16[1,32,8,512]{3,2,1,0:T(8,128)(2,1)}, u32[]{:S(2)}) copy-start(bf16[1,32,8,512]{3,2,1,0:T(8,128)(2,1)} %param.8) | copy-start | bytes 786436
  10.0 6.4 %copy-start.8 = (s32[1,32,2]{1,2,0:T(2,128)S(1)}, s32[1,32,2]{1,2,0:T(2,128)}, u32[]{:S(2)}) copy-start(s32[1,32,2]{1,2,0:T(2,128)} %param.10) | copy-start | bytes 772
  11.4 26.9 %all-to-all-start.2 = ((bf16[4,32,8,512]{3,2,1,0:T(8,128)(2,1)}), bf16[4,32,8,512]{3,2,1,0:T(8,128)(2,1)S(1)}, u32[]{:S(2)}, u32[]{:S(2)}) async-start(bf16[4,32,8,512]{3,2,1,0:T(8,128)(2,1)} %bitcast.54), calls=%async_computation.2 | async-start | bytes 2097152 | tf_op jit(solution)/shard_map/all_to_all | solution.py:105
  16.1 7.5 %collective-permute-start = (bf16[1,32,8,512]{3,1,2,0:T(8,128)(2,1)S(1)}, bf16[1,32,8,512]{3,1,2,0:T(8,128)(2,1)S(1)}, u32[]{:S(2)}, u32[]{:S(2)}) collective-permute-start(bf16[1,32,8,512]{3,1,2,0:T(8,128)(2,1)S(1)} %copy.19), channel_id=1, source_target_pairs={{0,24},{8,0},{16,8},{24,16},{1,25},{9,1},{17,9},{25,17},{2,26},{10... | collective-permute-start | bytes 786440 | tf_op jit(solution)/shard_map/ppermute | solution.py:13
  23.6 1.1 copy-start.1
  25.3 20.2 %copy-start.3 = (bf16[1,1,9,64,512]{4,3,2,1,0:T(8,128)(2,1)S(1)}, bf16[1,1,9,64,512]{4,3,2,1,0:T(8,128)(2,1)}, u32[]{:S(2)}) copy-start(bf16[1,1,9,64,512]{4,3,2,1,0:T(8,128)(2,1)} %param.11) | copy-start | bytes 1769476
  26.6 19.5 %copy-start.6 = (bf16[8,8,9,1,1]{2,1,4,3,0:T(8,128)(2,1)S(1)}, bf16[8,8,9,1,1]{2,1,4,3,0:T(8,128)(2,1)}, u32[]{:S(2)}) copy-start(bf16[8,8,9,1,1]{2,1,4,3,0:T(8,128)(2,1)} %constant.24) | copy-start | bytes 3460
  38.3 44.2 %all-to-all-start = ((bf16[4,32,8,512]{3,2,1,0:T(8,128)(2,1)}), bf16[4,32,8,512]{3,2,1,0:T(8,128)(2,1)}, u32[]{:S(2)}, u32[]{:S(2)}) async-start(bf16[4,32,8,512]{3,2,1,0:T(8,128)(2,1)} %bitcast.41), calls=%async_computation | async-start | bytes 2097152 | tf_op jit(solution)/shard_map/all_to_all | solution.py:106
  97.7 4.7 %copy-start = (bf16[8,128,8,64]{1,3,2,0:T(8,128)(2,1)S(1)}, bf16[8,128,8,64]{1,3,2,0:T(8,128)(2,1)}, u32[]{:S(2)}) copy-start(bf16[8,128,8,64]{1,3,2,0:T(8,128)(2,1)} %copy.31) | copy-start | bytes 3145732
  97.8 62.1 %all-to-all-start.1 = ((bf16[4,32,8,512]{3,2,1,0:T(8,128)(2,1)}), bf16[4,32,8,512]{3,2,1,0:T(8,128)(2,1)S(1)}, u32[]{:S(2)}, u32[]{:S(2)}) async-start(bf16[4,32,8,512]{3,2,1,0:T(8,128)(2,1)} %convert_element_type.76), calls=%async_computation.1 | async-start | bytes 2097152 | tf_op jit(solution)/shard_map/all_to_all | solution.py:110
  102.4 55.0 %all-reduce.2.cloned.1.call-start = ((), (), s32[]{:S(2)}) async-start(), calls=%async_computation.3 | async-start | bytes 2359296 | tf_op jit(solution)/shard_map/psum | solution.py:126
  106.9 12.9 %copy-start.5 = (f32[8,8,9,1,1]{2,0,1,4,3:T(8,128)S(1)}, f32[8,8,9,1,1]{2,0,1,4,3:T(8,128)}, u32[]{:S(2)}) copy-start(f32[8,8,9,1,1]{2,0,1,4,3:T(8,128)} %constant.25) | copy-start | bytes 6916
  132.6 1.8 %copy-start.7 = (s32[1,32,2]{1,2,0:T(2,128)S(1)}, s32[1,32,2]{1,2,0:T(2,128)}, u32[]{:S(2)}) copy-start(s32[1,32,2]{1,2,0:T(2,128)} %param.9) | copy-start | bytes 772
  160.2 1.2 copy-start.2
Sparse Core Ops, SparseCore 0:
  134.3 23.0 all-reduce.1
where the time goes:
time: 172 us; the launch traced here: 169 us
  local copies, waits for them, and re-layouts  67.9 us (39%)
  waiting for transfers between devices  41.5 us (24%)
  matrix products  25.8 us (15%)
  starting transfers between devices  16.8 us (10%)
  between operations  14.3 us (8%)
  other arithmetic  3 us (2%)
    psum x1, waiting for transfers between devices, body(): total_grad = lax.psum(local_grad, 'dp') / per_device  23 us
    convert_element_type x1, local copies, waits for them, and re-layouts, transpose_conv(): blocks.astype(jnp.bfloat16)  15 us
    reshape x1, local copies, waits for them, and re-layouts, weight_corr(): moments.reshape(group_count, cell_count, group_width, cell_count, group_w...  12.9 us
    reshape x1, local copies, waits for them, and re-layouts, transpose_conv(): blocks.astype(jnp.bfloat16)  11.8 us
    all_to_all x1, waiting for transfers between devices, body(): lax.all_to_all(pack_slots(input_rows), 'expert', split_axis=0, concat_axi...  11.6 us
    dot_general x1, matrix products, weight_corr(): jnp.einsum('gpcqo,qpt->tcgo', moments, selector, precision=lax.Precision....  11.4 us
    convert_element_type x3, local copies, waits for them, and re-layouts, body(): answers = transpose_conv(flat_grads, kernel).astype(jnp.bfloat16)  7.34 us
    all_to_all x1, starting transfers between devices, body(): lax.all_to_all(pack_slots(grad_rows), 'expert', split_axis=0, concat_axis...  7.2 us
  transfers between devices with their start and end apart: 5, of which 3 were waited for; matrix products, arithmetic and copies ran while one was open for 44% of the time, Pallas kernels for 0%

commit v1 on v0

--- a/solution.py
+++ b/solution.py
@@ -2,6 +2,8 @@
 import jax.numpy as jnp
 import numpy as np
 from jax import lax
+from jax.experimental import pallas as pl
+from jax.experimental.pallas import tpu as pltpu
 from jax.sharding import PartitionSpec as P
 
 TH = 4
@@ -127,6 +129,236 @@
     return (input_grad[None], total_grad[None, None])
 
 
+LINE = 4
+NEAR_PAIRS = [(0, 1), (1, 0), (2, 3), (3, 2)]
+INNER_PAIRS = [(1, 2), (2, 1)]
+SWAP = [(0, 1), (1, 0)]
+VMEM_LIMIT = 56 * 1024 * 1024
+
+
+def fits_line(mesh):
+    return mesh.shape["expert"] == LINE and mesh.shape["dp"] == 2
+
+
+def cell_order():
+    return [row * TW + col for col in range(TW) for row in range(TH)]
+
+
+def own_gates(info, expert):
+    codes = info[2:4].astype(jnp.float32)
+    hits = jnp.where(info[0:2] == expert, codes, 0.0)
+    return (hits[0:1] + hits[1:2]) / (codes[0:1] + codes[1:2])
+
+
+def gate_columns(info_ref, experts):
+    rows = [own_gates(info_ref[...], expert) for expert in experts]
+    count = rows[0].shape[1]
+    table = jnp.concatenate(rows + [jnp.zeros((8 - len(rows), count), jnp.float32)], axis=0)
+    table = jnp.concatenate([table, jnp.zeros((8, 128 - count), jnp.float32)], axis=1)
+    return table.T[:count]
+
+
+def slot_experts():
+    me = lax.axis_index("expert")
+    outer = (me == 0) | (me == 3)
+    mid = jnp.where(outer, 2, 3)
+    far = 5 - mid
+    return [me, me ^ 1, me ^ mid, me ^ far]
+
+
+def partial_kernel(
+    grad_a, grad_b, act_a, act_b, info_a, info_b, scaled_ref, own_ref, near_ref, mid_ref, far_ref, wide, cells, turned
+):
+    tiles = info_a.shape[1]
+    block = 2 * tiles
+    width = grad_a.shape[1]
+    column = TH * block
+    strips = width // 128
+    for at, ref in enumerate((grad_a, grad_b, act_a, act_b)):
+        for strip in range(strips):
+            wide[at * strips + strip] = ref[:, pl.ds(strip * 128, 128)].astype(jnp.float32)
+
+    def cell_rows(at, cell):
+        pieces = [wide[at * strips + strip, pl.ds(cell, tiles, stride=TH * TW), :] for strip in range(strips)]
+        return jnp.concatenate(pieces, axis=1)
+
+    experts = slot_experts()
+    gates_a = gate_columns(info_a, experts)
+    gates_b = gate_columns(info_b, experts)
+    order = cell_order()
+    for place, cell in enumerate(order):
+        part_a = cell_rows(0, cell)
+        part_b = cell_rows(1, cell)
+        for slot in range(4):
+            both = jnp.concatenate(
+                [part_a * gates_a[:, slot : slot + 1], part_b * gates_b[:, slot : slot + 1]], axis=0
+            )
+            scaled_ref[slot, pl.ds(place * block, block), :] = both.astype(jnp.bfloat16)
+        act_rows = jnp.concatenate([cell_rows(2, cell), cell_rows(3, cell)], axis=0)
+        cells[pl.ds(place * block, block), :] = act_rows.astype(jnp.bfloat16)
+    empty = jnp.zeros((block, width), jnp.bfloat16)
+    for col in range(TW):
+        rows = cells[pl.ds(col * column, column), :]
+        turned[1, :, pl.ds(col * column, column)] = rows.T
+        turned[2, :, pl.ds(col * column, column)] = jnp.concatenate([rows[block:], empty], axis=0).T
+        turned[0, :, pl.ds(col * column, column)] = jnp.concatenate([empty, rows[:-block]], axis=0).T
+    low_half = lax.broadcasted_iota(jnp.int32, (64, 128), 1) < 64
+    for slot, ref in ((3, far_ref), (2, mid_ref), (1, near_ref), (0, own_ref)):
+        for row_off in (-1, 0, 1):
+            for col_off in (-1, 0, 1):
+                lhs = turned[row_off + 1]
+                rhs = scaled_ref[slot]
+                if col_off == 1:
+                    lhs, rhs = lhs[:, column:], rhs[:column]
+                if col_off == -1:
+                    lhs, rhs = lhs[:, :column], rhs[column:]
+                full = jnp.dot(lhs, rhs, preferred_element_type=jnp.float32)
+                tap = (row_off + 1) * 3 + col_off + 1
+                for pair in range(width // 128):
+                    base = pair * 128
+                    piece = jnp.where(
+                        low_half,
+                        full[base : base + 64, base : base + 128],
+                        full[base + 64 : base + 128, base : base + 128],
+                    )
+                    ref[tap, :, pl.ds(base, 128)] = piece.astype(ref.dtype)
+
+
+def answer_kernel(scaled_ref, own_ref, near_ref, mid_ref, far_ref, grad_a, grad_b, out_a, out_b, total, spread):
+    width = grad_a.shape[1]
+    tiles = grad_a.shape[0] // (TH * TW)
+    block = 2 * tiles
+    lane_group = lax.broadcasted_iota(jnp.int32, (64, width), 1) // 64
+    masks = [jnp.where(lane_group == g, 1.0, 0.0).astype(jnp.bfloat16) for g in range(width // 64)]
+    total[...] = jnp.zeros_like(total)
+    for slot, ref in enumerate((own_ref, near_ref, mid_ref, far_ref)):
+        for row_off in (-1, 0, 1):
+            for col_off in (-1, 0, 1):
+                tap = (row_off + 1) * 3 + col_off + 1
+                kernel = ref[tap]
+                blocks = jnp.concatenate([kernel * mask for mask in masks], axis=0)
+                first = max(0, -row_off)
+                rows = (TH - abs(row_off)) * block
+                for col in range(TW):
+                    if not 0 <= col + col_off < TW:
+                        continue
+                    source = (col * TH + first) * block
+                    target = ((col + col_off) * TH + first + row_off) * block
+                    total[pl.ds(target, rows), :] += lax.dot_general(
+                        scaled_ref[slot, pl.ds(source, rows), :],
+                        blocks,
+                        (((1,), (1,)), ((), ())),
+                        preferred_element_type=jnp.float32,
+                    )
+    for at, (grad, out) in enumerate(((grad_a, out_a), (grad_b, out_b))):
+        for place, cell in enumerate(cell_order()):
+            for strip in range(width // 128):
+                spread[strip, pl.ds(cell, tiles, stride=TH * TW), :] = total[
+                    pl.ds(place * block + at * tiles, tiles), pl.ds(strip * 128, 128)
+                ]
+        for strip in range(width // 128):
+            lanes = pl.ds(strip * 128, 128)
+            out[:, lanes] = (grad[:, lanes].astype(jnp.float32) + spread[strip]).astype(jnp.bfloat16)
+
+
+def on_vmem(count):
+    return [pl.BlockSpec(memory_space=pltpu.VMEM)] * count
+
+
+def weights_travel(activations, upstream, routes, gate_codes, weights):
+    me = lax.axis_index("expert")
+    core = lax.axis_index("dp")
+    inner = (me == 1) | (me == 2)
+    per_device, cell_count, channels = activations.shape[1:]
+    rows = per_device * cell_count
+    width = channels // 2
+    kernel = weights[0, 0]
+    taps, group_width = kernel.shape[0], kernel.shape[1]
+    sections = lax.axis_size("segment")
+
+    def half(array, which):
+        return lax.dynamic_slice_in_dim(array, which * width, width, array.ndim - 1)
+
+    def along(array, pairs):
+        return lax.ppermute(array, "expert", pairs)
+
+    def from_next(array, flip):
+        pairs = []
+        for s in range(sections):
+            for d in range(2):
+                pairs.append((2 * ((s + 1) % sections) + d, 2 * s + (1 - d if flip else d)))
+        return lax.ppermute(array, ("segment", "dp"), pairs)
+
+    upstream_rows = upstream[0].reshape(rows, channels)
+    act_rows = activations[0].reshape(rows, channels)
+    info = jnp.concatenate([routes[0].T, gate_codes[0].T], axis=0)
+    my_weights = half(kernel, core)
+    inner_weights = along(my_weights, INNER_PAIRS)
+    near_weights = along(my_weights, NEAR_PAIRS)
+    grad_a = from_next(half(upstream_rows, core), False)
+    grad_b = from_next(half(upstream_rows, 1 - core), True)
+    act_a = half(act_rows, core)
+    act_b = lax.ppermute(half(act_rows, 1 - core), "dp", SWAP)
+    info_b = lax.ppermute(info, "dp", SWAP)
+
+    part = jax.ShapeDtypeStruct((taps, group_width, width), jnp.bfloat16)
+    scaled, own_part, near_part, mid_part, far_part = pl.pallas_call(
+        partial_kernel,
+        out_shape=(
+            jax.ShapeDtypeStruct((4, 2 * rows, width), jnp.bfloat16),
+            jax.ShapeDtypeStruct((taps, group_width, width), jnp.float32),
+            part,
+            part,
+            part,
+        ),
+        in_specs=on_vmem(6),
+        out_specs=tuple(on_vmem(5)),
+        scratch_shapes=[
+            pltpu.VMEM((4 * (width // 128), rows, 128), jnp.float32),
+            pltpu.VMEM((2 * rows, width), jnp.bfloat16),
+            pltpu.VMEM((3, width, 2 * rows), jnp.bfloat16),
+        ],
+        compiler_params=pltpu.CompilerParams(vmem_limit_bytes=VMEM_LIMIT),
+        cost_estimate=pl.CostEstimate(flops=3_000_000_000, bytes_accessed=3_000_000, transcendentals=0),
+    )(grad_a, grad_b, act_a, act_b, info, info_b)
+
+    cross_weights = along(near_weights, INNER_PAIRS)
+    first_swap = along(jnp.where(inner, inner_weights, far_part), NEAR_PAIRS)
+    second_swap = along(jnp.where(inner, cross_weights, mid_part), NEAR_PAIRS)
+    far_sum = along(far_part + first_swap, INNER_PAIRS)
+    mid_sum = along(mid_part + second_swap, INNER_PAIRS)
+    last_swap = along(near_part + far_sum, NEAR_PAIRS)
+
+    mid_weights = jnp.where(inner, inner_weights, first_swap)
+    far_weights = jnp.where(inner, cross_weights, second_swap)
+    answer = jax.ShapeDtypeStruct((rows, width), jnp.bfloat16)
+    grad_own, grad_other = pl.pallas_call(
+        answer_kernel,
+        out_shape=(answer, answer),
+        in_specs=on_vmem(7),
+        out_specs=tuple(on_vmem(2)),
+        scratch_shapes=[
+            pltpu.VMEM((2 * rows, width), jnp.float32),
+            pltpu.VMEM((width // 128, rows, 128), jnp.float32),
+        ],
+        compiler_params=pltpu.CompilerParams(vmem_limit_bytes=VMEM_LIMIT),
+        cost_estimate=pl.CostEstimate(flops=3_000_000_000, bytes_accessed=3_000_000, transcendentals=0),
+    )(scaled, my_weights, near_weights, mid_weights, far_weights, grad_a, grad_b)
+    grad_back = lax.ppermute(grad_other, "dp", SWAP)
+
+    def whole(mine, other):
+        return jnp.where(
+            core == 0, jnp.concatenate([mine, other], axis=-1), jnp.concatenate([other, mine], axis=-1)
+        )
+
+    input_grad = whole(grad_own, grad_back).reshape(per_device, cell_count, channels)
+    kernel_sum = own_part + last_swap.astype(jnp.float32) + mid_sum.astype(jnp.float32)
+    kernel_mine = kernel_sum.astype(jnp.bfloat16)
+    kernel_other = lax.ppermute(kernel_mine, "dp", SWAP)
+    weight_grad = whole(kernel_mine, kernel_other).astype(jnp.float32) / per_device
+    return (input_grad[None], weight_grad[None, None])
+
+
 def solution(mesh):
     placed = (
         P("segment", ("expert", "dp"), None, None),
@@ -135,8 +367,9 @@
         P("segment", ("expert", "dp"), None),
         P("segment", "expert", None, None, None),
     )
+    step = weights_travel if fits_line(mesh) else body
     return jax.shard_map(
-        body,
+        step,
         mesh=mesh,
         in_specs=placed,
         out_specs=(

time: 172 us -> 59.3 us (0.34); the launches traced: 169 us -> 58.8 us
  local copies, waits for them, and re-layouts: 67.9 us -> 3.44 us
  matrix products: 25.8 us -> 0 us
  waiting for transfers between devices: 41.5 us -> 19 us
  between operations: 14.3 us -> 0.84 us
  Pallas kernels: 0 us -> 8.63 us
  starting transfers between devices: 16.8 us -> 21.1 us
  other arithmetic: 3 us -> 5.75 us
    reshape x3 -> x0, local copies, waits for them, and re-layouts: 26.3 us -> none  [the longest x1 12.9 us: weight_corr(): moments.reshape(group_count, cell_count, group_width, cell_count, group_w...]
    dot_general x7 -> x0, matrix products: 25.8 us -> none  [the longest x1 11.4 us: weight_corr(): jnp.einsum('gpcqo,qpt->tcgo', moments, selector, precision=lax.Precision....]
    psum x1 -> x0, waiting for transfers between devices: 23 us -> none  [body(): total_grad = lax.psum(local_grad, 'dp') / per_device]
    convert_element_type x7 -> x0, local copies, waits for them, and re-layouts: 22.9 us -> none  [the longest x1 15 us: transpose_conv(): blocks.astype(jnp.bfloat16)]
    ppermute x1 -> x14, starting transfers between devices: 0.31 us -> 21.1 us  [the longest x8 13.3 us: along(): return lax.ppermute(array, 'expert', pairs)]
    all_to_all x3 -> x0, starting transfers between devices: 16.5 us -> none  [the longest x1 7.2 us: body(): lax.all_to_all(pack_slots(grad_rows), 'expert', split_axis=0, concat_axis...]
    ppermute x1 -> x14, waiting for transfers between devices: 6.78 us -> 19 us  [the longest x8 16.5 us: along(): return lax.ppermute(array, 'expert', pairs)]
    all_to_all x3 -> x0, waiting for transfers between devices: 11.6 us -> none  [the longest x1 11.6 us: body(): lax.all_to_all(pack_slots(input_rows), 'expert', split_axis=0, concat_axi...]
  transfers between devices with their start and end apart: 5 -> 14, of which waited for: 3 -> 10; matrix products, arithmetic and copies ran while one was open for 44% -> 10% of each run, Pallas kernels for 0% -> 15%
where the time goes in v1:
time: 59.3 us; the launch traced here: 58.8 us
  starting transfers between devices  21.1 us (36%)
  waiting for transfers between devices  19 us (32%)
  Pallas kernels  8.63 us (15%)
  other arithmetic  5.75 us (10%)
  local copies, waits for them, and re-layouts  3.44 us (6%)
  between operations  0.84 us (1%)
    ppermute x8, waiting for transfers between devices, along(): return lax.ppermute(array, 'expert', pairs)  16.5 us
    ppermute x8, starting transfers between devices, along(): return lax.ppermute(array, 'expert', pairs)  13.3 us
    pallas_call x1, Pallas kernels, weights_travel(): pl.pallas_call(answer_kernel, out_shape=(answer, answer), in_specs=on_vme...  4.47 us
    pallas_call x1, Pallas kernels, weights_travel(): pl.pallas_call(partial_kernel, out_shape=(jax.ShapeDtypeStruct((4, 2 * ro...  4.15 us
    ppermute x1, starting transfers between devices, weights_travel(): kernel_other = lax.ppermute(kernel_mine, 'dp', SWAP)  3.61 us
    ppermute x2, starting transfers between devices, from_next(): return lax.ppermute(array, ('segment', 'dp'), pairs)  3.31 us
    dynamic_slice x3, local copies, waits for them, and re-layouts, half(): return lax.dynamic_slice_in_dim(array, which * width, width, array.ndim - 1)  2.71 us
    select_n x1, other arithmetic, whole(): jnp.where(core == 0, jnp.concatenate([mine, other], axis=-1), jnp.concate...  1.75 us
  transfers between devices with their start and end apart: 14, of which 10 were waited for; matrix products, arithmetic and copies ran while one was open for 10% of the time, Pallas kernels for 15%

profile of v1, /device:TPU:19, one launch (start us, length us, event | category | flops | bytes accessed | tf_op | source)
XLA Modules:
  0.0 58.8 jit_solution(3773132468918017337)
XLA Ops:
  0.7 1.0 %constant_dynamic-slice_fusion.2 = (bf16[256,256]{1,0:T(8,128)(2,1)S(1)}, bf16[256,256]{1,0:T(8,128)(2,1)S(1)}) fusion(bf16[256,512]{1,0:T(8,128)(2,1)} %bitcast.16, s32[]{:T(128)S(6)} %select_n.61, s32[]{:T(128)S(6)} %select_n.60), kind=kLoop, calls=%fused_computation.12 | loop fusion | bytes 524296 | tf_op jit(solution)/shard_map/dynamic_slice | solution.py:280
  2.0 3.0 %collective-permute-start.1 = (bf16[256,256]{1,0:T(8,128)(2,1)S(1)}, bf16[256,256]{1,0:T(8,128)(2,1)S(1)}, u32[]{:S(2)}, u32[]{:S(2)}) collective-permute-start(bf16[256,256]{1,0:T(8,128)(2,1)S(1)} %get-tuple-element.22), channel_id=1, source_target_pairs={{8,1},{9,0},{16,9},{17,8},{24,17},{25,16},{0,25},{1,24},{10,3},{11... | collective-permute-start | bytes 393224 | tf_op jit(solution)/shard_map/ppermute | solution.py:290
  5.0 1.6 %constant_dynamic-slice_fusion = (bf16[256,256]{1,0:T(8,128)(2,1)S(1)}, bf16[256,256]{1,0:T(8,128)(2,1)}) fusion(bf16[256,512]{1,0:T(8,128)(2,1)} %bitcast.17, s32[]{:T(128)S(6)} %select_n.61, s32[]{:T(128)S(6)} %select_n.60), kind=kLoop, calls=%fused_computation.10 | loop fusion | bytes 524296 | tf_op jit(solution)/shard_map/dynamic_slice | solution.py:280
  6.7 2.1 %collective-permute-start.5 = (bf16[9,64,256]{2,1,0:T(8,128)(2,1)S(1)}, bf16[9,64,256]{2,1,0:T(8,128)(2,1)S(1)}, u32[]{:S(2)}, u32[]{:S(2)}) collective-permute-start(bf16[9,64,256]{2,1,0:T(8,128)(2,1)S(1)} %dynamic-slice_bitcast_fusion.own_ref), channel_id=1, source_target_pairs={{2,4},{4,2},{3,5},{5,3},{10,12},{12,10},{11,13},{13,11},{18,20},{2... | collective-permute-start | bytes 884744 | tf_op jit(solution)/shard_map/ppermute | solution.py:283
  8.9 0.9 %collective-permute-start.3 = (s32[4,32]{1,0:T(4,128)S(1)}, s32[4,32]{1,0:T(4,128)S(1)}, u32[]{:S(2)}, u32[]{:S(2)}) collective-permute-start(s32[4,32]{1,0:T(4,128)S(1)} %pad_add_fusion.info_a), channel_id=1, source_target_pairs={{0,1},{1,0},{2,3},{3,2},{4,5},{5,4},{6,7},{7,6},{8,9},{9,8},{10,11... | collective-permute-start | bytes 1544 | tf_op jit(solution)/shard_map/ppermute | solution.py:302
  9.7 0.8 %collective-permute-done.3.info_b = s32[4,32]{1,0:T(4,128)S(1)} collective-permute-done((s32[4,32]{1,0:T(4,128)S(1)}, s32[4,32]{1,0:T(4,128)S(1)}, u32[]{:S(2)}, u32[]{:S(2)}) %collective-permute-start.3) | collective-permute-done | bytes 544 | tf_op jit(solution)/shard_map/ppermute | solution.py:302
  11.4 4.2 %shard_map.68 = (bf16[4,512,256]{2,1,0:T(8,128)(2,1)}, f32[9,64,256]{2,1,0:T(8,128)}, bf16[9,64,256]{2,1,0:T(8,128)(2,1)}, bf16[9,64,256]{2,1,0:T(8,128)(2,1)}, bf16[9,64,256]{2,1,0:T(8,128)(2,1)}) custom-call(bf16[256,256]{1,0:T(8,128)(2,1)} %copy-done.9, bf16[256,256]{1,0:T(8,128)(2,1)} %copy-done.10, bf16[256,256]{1,0:T(8,128)(2,1)} %get-tuple-element.21.act_a, ...), custom_call_target="tpu_custom_call" | custom-call | flops 3000000000 | bytes 3000000 | tf_op jit(solution)/shard_map/pallas_call | solution.py:305
  15.6 1.1 %collective-permute-done.5 = bf16[9,64,256]{2,1,0:T(8,128)(2,1)S(1)} collective-permute-done((bf16[9,64,256]{2,1,0:T(8,128)(2,1)S(1)}, bf16[9,64,256]{2,1,0:T(8,128)(2,1)S(1)}, u32[]{:S(2)}, u32[]{:S(2)}) %collective-permute-start.5) | collective-permute-done | bytes 294944 | tf_op jit(solution)/shard_map/ppermute | solution.py:283
  16.7 1.3 %collective-permute-start.6 = (bf16[9,64,256]{2,1,0:T(8,128)(2,1)S(1)}, bf16[9,64,256]{2,1,0:T(8,128)(2,1)S(1)}, u32[]{:S(2)}, u32[]{:S(2)}) collective-permute-start(bf16[9,64,256]{2,1,0:T(8,128)(2,1)S(1)} %broadcast_select_fusion.3), channel_id=1, source_target_pairs={{0,2},{2,0},{4,6},{6,4},{1,3},{3,1},{5,7},{7,5},{8,10},{10,8},{12,... | collective-permute-start | bytes 884744 | tf_op jit(solution)/shard_map/ppermute | solution.py:283
  18.8 3.2 %collective-permute-start.7 = (bf16[9,64,256]{2,1,0:T(8,128)(2,1)S(1)}, bf16[9,64,256]{2,1,0:T(8,128)(2,1)S(1)}, u32[]{:S(2)}, u32[]{:S(2)}) collective-permute-start(bf16[9,64,256]{2,1,0:T(8,128)(2,1)S(1)} %collective-permute-done.4.near_ref), channel_id=1, source_target_pairs={{2,4},{4,2},{3,5},{5,3},{10,12},{12,10},{11,13},{13,11},{18,20},{2... | collective-permute-start | bytes 884744 | tf_op jit(solution)/shard_map/ppermute | solution.py:283
  22.0 2.0 %collective-permute-done.6 = bf16[9,64,256]{2,1,0:T(8,128)(2,1)S(1)} collective-permute-done((bf16[9,64,256]{2,1,0:T(8,128)(2,1)S(1)}, bf16[9,64,256]{2,1,0:T(8,128)(2,1)S(1)}, u32[]{:S(2)}, u32[]{:S(2)}) %collective-permute-start.6) | collective-permute-done | bytes 294944 | tf_op jit(solution)/shard_map/ppermute | solution.py:283
  24.0 1.7 %fusion = (bf16[9,64,256]{2,1,0:T(8,128)(2,1)S(1)}, bf16[9,64,256]{2,1,0:T(8,128)(2,1)}) fusion(bf16[9,64,256]{2,1,0:T(8,128)(2,1)} %get-tuple-element.10, bf16[9,64,256]{2,1,0:T(8,128)(2,1)S(1)} %collective-permute-done.6, bf16[9,64,256]{2,1,0:T(8,128)(2,1)S(1)} %collective-permute-done.5, pred[]{:T(512)S(6)} %or.3), kind=kLoop, calls=%fused_computation.14 | loop fusion | flops 294912 | bytes 1474561 | tf_op jit(solution)/shard_map/add | solution.py:328
  25.8 4.4 %collective-permute-start.10 = (bf16[9,64,256]{2,1,0:T(8,128)(2,1)S(1)}, bf16[9,64,256]{2,1,0:T(8,128)(2,1)S(1)}, u32[]{:S(2)}, u32[]{:S(2)}) collective-permute-start(bf16[9,64,256]{2,1,0:T(8,128)(2,1)S(1)} %get-tuple-element.16), channel_id=1, source_target_pairs={{2,4},{4,2},{3,5},{5,3},{10,12},{12,10},{11,13},{13,11},{18,20},{2... | collective-permute-start | bytes 884744 | tf_op jit(solution)/shard_map/ppermute | solution.py:283
  30.3 5.7 %collective-permute-done.10 = bf16[9,64,256]{2,1,0:T(8,128)(2,1)S(1)} collective-permute-done((bf16[9,64,256]{2,1,0:T(8,128)(2,1)S(1)}, bf16[9,64,256]{2,1,0:T(8,128)(2,1)S(1)}, u32[]{:S(2)}, u32[]{:S(2)}) %collective-permute-start.10) | collective-permute-done | bytes 294944 | tf_op jit(solution)/shard_map/ppermute | solution.py:283
  36.2 1.3 %collective-permute-done.8 = bf16[9,64,256]{2,1,0:T(8,128)(2,1)S(1)} collective-permute-done((bf16[9,64,256]{2,1,0:T(8,128)(2,1)S(1)}, bf16[9,64,256]{2,1,0:T(8,128)(2,1)S(1)}, u32[]{:S(2)}, u32[]{:S(2)}) %collective-permute-start.8) | collective-permute-done | bytes 294944 | tf_op jit(solution)/shard_map/ppermute | solution.py:283
  37.5 0.8 %fusion.1 = (bf16[9,64,256]{2,1,0:T(8,128)(2,1)S(1)}, bf16[9,64,256]{2,1,0:T(8,128)(2,1)}) fusion(bf16[9,64,256]{2,1,0:T(8,128)(2,1)S(1)} %copy-done.1, bf16[9,64,256]{2,1,0:T(8,128)(2,1)S(1)} %collective-permute-done.8, bf16[9,64,256]{2,1,0:T(8,128)(2,1)S(1)} %collective-permute-done.7, pred[]{:T(512)S(6)} %or.3), kind=kLoop, calls=%fused_computation.15 | loop fusion | flops 294912 | bytes 1474561 | tf_op jit(solution)/shard_map/add | solution.py:329
  38.3 2.2 %collective-permute-start.12 = (bf16[9,64,256]{2,1,0:T(8,128)(2,1)S(1)}, bf16[9,64,256]{2,1,0:T(8,128)(2,1)S(1)}, u32[]{:S(2)}, u32[]{:S(2)}) collective-permute-start(bf16[9,64,256]{2,1,0:T(8,128)(2,1)S(1)} %get-tuple-element.18), channel_id=1, source_target_pairs={{2,4},{4,2},{3,5},{5,3},{10,12},{12,10},{11,13},{13,11},{18,20},{2... | collective-permute-start | bytes 884744 | tf_op jit(solution)/shard_map/ppermute | solution.py:283
  40.5 3.0 %collective-permute-done.11 = bf16[9,64,256]{2,1,0:T(8,128)(2,1)S(1)} collective-permute-done((bf16[9,64,256]{2,1,0:T(8,128)(2,1)S(1)}, bf16[9,64,256]{2,1,0:T(8,128)(2,1)S(1)}, u32[]{:S(2)}, u32[]{:S(2)}) %collective-permute-start.11) | collective-permute-done | bytes 294944 | tf_op jit(solution)/shard_map/ppermute | solution.py:283
  43.5 2.6 %collective-permute-done.12 = bf16[9,64,256]{2,1,0:T(8,128)(2,1)S(1)} collective-permute-done((bf16[9,64,256]{2,1,0:T(8,128)(2,1)S(1)}, bf16[9,64,256]{2,1,0:T(8,128)(2,1)S(1)}, u32[]{:S(2)}, u32[]{:S(2)}) %collective-permute-start.12) | collective-permute-done | bytes 294944 | tf_op jit(solution)/shard_map/ppermute | solution.py:283
  46.2 3.6 %collective-permute-start.13 = (bf16[9,64,256]{2,1,0:T(8,128)(2,1)S(1)}, bf16[9,64,256]{2,1,0:T(8,128)(2,1)S(1)}, u32[]{:S(2)}, u32[]{:S(2)}) collective-permute-start(bf16[9,64,256]{2,1,0:T(8,128)(2,1)S(1)} %add_convert_fusion), channel_id=1, source_target_pairs={{0,1},{1,0},{2,3},{3,2},{4,5},{5,4},{6,7},{7,6},{8,9},{9,8},{10,11... | collective-permute-start | bytes 884744 | tf_op jit(solution)/shard_map/ppermute | solution.py:357
  49.8 4.5 %shard_map.69 = (bf16[256,256]{1,0:T(8,128)(2,1)}, bf16[256,256]{1,0:T(8,128)(2,1)}) custom-call(bf16[4,512,256]{2,1,0:T(8,128)(2,1)} %get-tuple-element.9.scaled_ref, bf16[9,64,256]{2,1,0:T(8,128)(2,1)} %copy-done.4, bf16[9,64,256]{2,1,0:T(8,128)(2,1)} %copy-done.8, bf16[9,64,256]{2,1,0:T(8,128)(2,1)} %get-tuple-element.17.mid_ref, ...), custom_call_target="tpu_custom_call" | custom-call | flops 3000000000 | bytes 3000000 | tf_op jit(solution)/shard_map/pallas_call | solution.py:335
  54.3 1.5 %collective-permute-done.9 = bf16[256,256]{1,0:T(8,128)(2,1)S(1)} collective-permute-done((bf16[256,256]{1,0:T(8,128)(2,1)}, bf16[256,256]{1,0:T(8,128)(2,1)S(1)}, u32[]{:S(2)}, u32[]{:S(2)}) %collective-permute-start.9) | collective-permute-done | bytes 131104 | tf_op jit(solution)/shard_map/ppermute | solution.py:347
  55.8 1.8 %maximum_select_fusion.1 = bf16[1,32,8,512]{3,2,1,0:T(8,128)(2,1)} fusion(bf16[1,32,8,256]{3,2,1,0:T(8,128)(2,1)S(1)} %bitcast.19, bf16[1,32,8,256]{3,2,1,0:T(8,128)(2,1)} %bitcast.18, pred[]{:T(512)S(6)} %eq.10), kind=kLoop, calls=%fused_computation.8 | loop fusion | flops 1179648 | bytes 524289 | tf_op jit(solution)/shard_map/jit(_where)/select_n | solution.py:350
  57.6 1.2 %convert_multiply_fusion = f32[1,1,9,64,512]{4,3,2,1,0:T(8,128)} fusion(bf16[1,1,9,64,256]{4,3,2,1,0:T(8,128)(2,1)S(1)} %bitcast.15, bf16[1,1,9,64,256]{4,3,2,1,0:T(8,128)(2,1)S(1)} %bitcast.14, pred[]{:T(512)S(6)} %eq.10), kind=kLoop, calls=%fused_computation | loop fusion | flops 3244032 | bytes 1769473 | tf_op jit(solution)/shard_map/div | solution.py:358
  (44 shorter events, 2.4 us)
Async XLA Ops:
  0.6 6.1 %copy-start = (bf16[1,1,9,64,512]{4,3,2,1,0:T(8,128)(2,1)S(1)}, bf16[1,1,9,64,512]{4,3,2,1,0:T(8,128)(2,1)}, u32[]{:S(2)}) copy-start(bf16[1,1,9,64,512]{4,3,2,1,0:T(8,128)(2,1)} %param.9) | copy-start | bytes 1769476
  0.6 8.2 %copy-start.7 = (s32[1,32,2]{1,2,0:T(2,128)S(1)}, s32[1,32,2]{1,2,0:T(2,128)}, u32[]{:S(2)}) copy-start(s32[1,32,2]{1,2,0:T(2,128)} %param.7) | copy-start | bytes 772
  0.7 8.2 %copy-start.6 = (s32[1,32,2]{1,2,0:T(2,128)S(1)}, s32[1,32,2]{1,2,0:T(2,128)}, u32[]{:S(2)}) copy-start(s32[1,32,2]{1,2,0:T(2,128)} %param.8) | copy-start | bytes 772
  1.7 8.8 %collective-permute-start = (bf16[256,256]{1,0:T(8,128)(2,1)S(1)}, bf16[256,256]{1,0:T(8,128)(2,1)S(1)}, u32[]{:S(2)}, u32[]{:S(2)}) collective-permute-start(bf16[256,256]{1,0:T(8,128)(2,1)S(1)} %get-tuple-element.23), channel_id=1, source_target_pairs={{8,0},{9,1},{16,8},{17,9},{24,16},{25,17},{0,24},{1,25},{10,2},{11... | collective-permute-start | bytes 393224 | tf_op jit(solution)/shard_map/ppermute | solution.py:290
  2.0 8.7 %collective-permute-start.1 = (bf16[256,256]{1,0:T(8,128)(2,1)S(1)}, bf16[256,256]{1,0:T(8,128)(2,1)S(1)}, u32[]{:S(2)}, u32[]{:S(2)}) collective-permute-start(bf16[256,256]{1,0:T(8,128)(2,1)S(1)} %get-tuple-element.22), channel_id=1, source_target_pairs={{8,1},{9,0},{16,9},{17,8},{24,17},{25,16},{0,25},{1,24},{10,3},{11... | collective-permute-start | bytes 393224 | tf_op jit(solution)/shard_map/ppermute | solution.py:290
  6.7 4.0 %collective-permute-start.2 = (bf16[256,256]{1,0:T(8,128)(2,1)S(1)}, bf16[256,256]{1,0:T(8,128)(2,1)S(1)}, u32[]{:S(2)}, u32[]{:S(2)}) collective-permute-start(bf16[256,256]{1,0:T(8,128)(2,1)S(1)} %get-tuple-element.20), channel_id=1, source_target_pairs={{0,1},{1,0},{2,3},{3,2},{4,5},{5,4},{6,7},{7,6},{8,9},{9,8},{10,11... | collective-permute-start | bytes 393224 | tf_op jit(solution)/shard_map/ppermute | solution.py:301
  6.7 8.8 %copy-start.4 = (bf16[9,64,256]{2,1,0:T(8,128)(2,1)}, bf16[9,64,256]{2,1,0:T(8,128)(2,1)S(1)}, u32[]{:S(2)}) copy-start(bf16[9,64,256]{2,1,0:T(8,128)(2,1)S(1)} %dynamic-slice_bitcast_fusion.own_ref) | copy-start | bytes 884740
  6.7 10.0 %collective-permute-start.5 = (bf16[9,64,256]{2,1,0:T(8,128)(2,1)S(1)}, bf16[9,64,256]{2,1,0:T(8,128)(2,1)S(1)}, u32[]{:S(2)}, u32[]{:S(2)}) collective-permute-start(bf16[9,64,256]{2,1,0:T(8,128)(2,1)S(1)} %dynamic-slice_bitcast_fusion.own_ref), channel_id=1, source_target_pairs={{2,4},{4,2},{3,5},{5,3},{10,12},{12,10},{11,13},{13,11},{18,20},{2... | collective-permute-start | bytes 884744 | tf_op jit(solution)/shard_map/ppermute | solution.py:283
  8.8 1.9 %copy-start.5 = (s32[4,32]{1,0:T(4,128)}, s32[4,32]{1,0:T(4,128)S(1)}, u32[]{:S(2)}) copy-start(s32[4,32]{1,0:T(4,128)S(1)} %pad_add_fusion.info_a) | copy-start | bytes 1540
  8.9 1.7 %collective-permute-start.3 = (s32[4,32]{1,0:T(4,128)S(1)}, s32[4,32]{1,0:T(4,128)S(1)}, u32[]{:S(2)}, u32[]{:S(2)}) collective-permute-start(s32[4,32]{1,0:T(4,128)S(1)} %pad_add_fusion.info_a), channel_id=1, source_target_pairs={{0,1},{1,0},{2,3},{3,2},{4,5},{5,4},{6,7},{7,6},{8,9},{9,8},{10,11... | collective-permute-start | bytes 1544 | tf_op jit(solution)/shard_map/ppermute | solution.py:302
  10.5 8.3 %collective-permute-start.4 = (bf16[9,64,256]{2,1,0:T(8,128)(2,1)S(1)}, bf16[9,64,256]{2,1,0:T(8,128)(2,1)S(1)}, u32[]{:S(2)}, u32[]{:S(2)}) collective-permute-start(bf16[9,64,256]{2,1,0:T(8,128)(2,1)S(1)} %dynamic-slice_bitcast_fusion.own_ref), channel_id=1, source_target_pairs={{0,2},{2,0},{4,6},{6,4},{1,3},{3,1},{5,7},{7,5},{8,10},{10,8},{12,... | collective-permute-start | bytes 884744 | tf_op jit(solution)/shard_map/ppermute | solution.py:283
  10.7 0.7 %copy-start.11 = (bf16[256,256]{1,0:T(8,128)(2,1)}, bf16[256,256]{1,0:T(8,128)(2,1)S(1)}, u32[]{:S(2)}) copy-start(bf16[256,256]{1,0:T(8,128)(2,1)S(1)} %collective-permute-done.2.act_b) | copy-start | bytes 393220
  16.7 13.5 %copy-start.1 = (bf16[9,64,256]{2,1,0:T(8,128)(2,1)S(1)}, bf16[9,64,256]{2,1,0:T(8,128)(2,1)}, u32[]{:S(2)}) copy-start(bf16[9,64,256]{2,1,0:T(8,128)(2,1)} %get-tuple-element.11) | copy-start | bytes 884740
  16.7 19.3 %copy-start.3 = (bf16[9,64,256]{2,1,0:T(8,128)(2,1)S(1)}, bf16[9,64,256]{2,1,0:T(8,128)(2,1)}, u32[]{:S(2)}) copy-start(bf16[9,64,256]{2,1,0:T(8,128)(2,1)} %get-tuple-element.15) | copy-start | bytes 884740
  16.7 7.3 %collective-permute-start.6 = (bf16[9,64,256]{2,1,0:T(8,128)(2,1)S(1)}, bf16[9,64,256]{2,1,0:T(8,128)(2,1)S(1)}, u32[]{:S(2)}, u32[]{:S(2)}) collective-permute-start(bf16[9,64,256]{2,1,0:T(8,128)(2,1)S(1)} %broadcast_select_fusion.3), channel_id=1, source_target_pairs={{0,2},{2,0},{4,6},{6,4},{1,3},{3,1},{5,7},{7,5},{8,10},{10,8},{12,... | collective-permute-start | bytes 884744 | tf_op jit(solution)/shard_map/ppermute | solution.py:283
  18.8 11.5 %copy-start.8 = (bf16[9,64,256]{2,1,0:T(8,128)(2,1)}, bf16[9,64,256]{2,1,0:T(8,128)(2,1)S(1)}, u32[]{:S(2)}) copy-start(bf16[9,64,256]{2,1,0:T(8,128)(2,1)S(1)} %collective-permute-done.4.near_ref) | copy-start | bytes 884740
  18.8 11.4 %collective-permute-start.7 = (bf16[9,64,256]{2,1,0:T(8,128)(2,1)S(1)}, bf16[9,64,256]{2,1,0:T(8,128)(2,1)S(1)}, u32[]{:S(2)}, u32[]{:S(2)}) collective-permute-start(bf16[9,64,256]{2,1,0:T(8,128)(2,1)S(1)} %collective-permute-done.4.near_ref), channel_id=1, source_target_pairs={{2,4},{4,2},{3,5},{5,3},{10,12},{12,10},{11,13},{13,11},{18,20},{2... | collective-permute-start | bytes 884744 | tf_op jit(solution)/shard_map/ppermute | solution.py:283
  25.8 10.2 %collective-permute-start.10 = (bf16[9,64,256]{2,1,0:T(8,128)(2,1)S(1)}, bf16[9,64,256]{2,1,0:T(8,128)(2,1)S(1)}, u32[]{:S(2)}, u32[]{:S(2)}) collective-permute-start(bf16[9,64,256]{2,1,0:T(8,128)(2,1)S(1)} %get-tuple-element.16), channel_id=1, source_target_pairs={{2,4},{4,2},{3,5},{5,3},{10,12},{12,10},{11,13},{13,11},{18,20},{2... | collective-permute-start | bytes 884744 | tf_op jit(solution)/shard_map/ppermute | solution.py:283
  30.3 7.3 %collective-permute-start.8 = (bf16[9,64,256]{2,1,0:T(8,128)(2,1)S(1)}, bf16[9,64,256]{2,1,0:T(8,128)(2,1)S(1)}, u32[]{:S(2)}, u32[]{:S(2)}) collective-permute-start(bf16[9,64,256]{2,1,0:T(8,128)(2,1)S(1)} %broadcast_select_fusion.1), channel_id=1, source_target_pairs={{0,2},{2,0},{4,6},{6,4},{1,3},{3,1},{5,7},{7,5},{8,10},{10,8},{12,... | collective-permute-start | bytes 884744 | tf_op jit(solution)/shard_map/ppermute | solution.py:283
  36.0 10.0 %copy-start.2 = (f32[9,64,256]{2,1,0:T(8,128)S(1)}, f32[9,64,256]{2,1,0:T(8,128)}, u32[]{:S(2)}) copy-start(f32[9,64,256]{2,1,0:T(8,128)} %get-tuple-element.14) | copy-start | bytes 1769476
  36.1 7.4 %collective-permute-start.11 = (bf16[9,64,256]{2,1,0:T(8,128)(2,1)S(1)}, bf16[9,64,256]{2,1,0:T(8,128)(2,1)S(1)}, u32[]{:S(2)}, u32[]{:S(2)}) collective-permute-start(bf16[9,64,256]{2,1,0:T(8,128)(2,1)S(1)} %add.27), channel_id=1, source_target_pairs={{0,2},{2,0},{4,6},{6,4},{1,3},{3,1},{5,7},{7,5},{8,10},{10,8},{12,... | collective-permute-start | bytes 884744 | tf_op jit(solution)/shard_map/ppermute | solution.py:283
  38.3 7.8 %collective-permute-start.12 = (bf16[9,64,256]{2,1,0:T(8,128)(2,1)S(1)}, bf16[9,64,256]{2,1,0:T(8,128)(2,1)S(1)}, u32[]{:S(2)}, u32[]{:S(2)}) collective-permute-start(bf16[9,64,256]{2,1,0:T(8,128)(2,1)S(1)} %get-tuple-element.18), channel_id=1, source_target_pairs={{2,4},{4,2},{3,5},{5,3},{10,12},{12,10},{11,13},{13,11},{18,20},{2... | collective-permute-start | bytes 884744 | tf_op jit(solution)/shard_map/ppermute | solution.py:283
  46.2 11.4 %collective-permute-start.13 = (bf16[9,64,256]{2,1,0:T(8,128)(2,1)S(1)}, bf16[9,64,256]{2,1,0:T(8,128)(2,1)S(1)}, u32[]{:S(2)}, u32[]{:S(2)}) collective-permute-start(bf16[9,64,256]{2,1,0:T(8,128)(2,1)S(1)} %add_convert_fusion), channel_id=1, source_target_pairs={{0,1},{1,0},{2,3},{3,2},{4,5},{5,4},{6,7},{7,6},{8,9},{9,8},{10,11... | collective-permute-start | bytes 884744 | tf_op jit(solution)/shard_map/ppermute | solution.py:357
  54.3 1.6 %collective-permute-start.9 = (bf16[256,256]{1,0:T(8,128)(2,1)}, bf16[256,256]{1,0:T(8,128)(2,1)S(1)}, u32[]{:S(2)}, u32[]{:S(2)}) collective-permute-start(bf16[256,256]{1,0:T(8,128)(2,1)} %get-tuple-element.13), channel_id=1, source_target_pairs={{0,1},{1,0},{2,3},{3,2},{4,5},{5,4},{6,7},{7,6},{8,9},{9,8},{10,11... | collective-permute-start | bytes 393224 | tf_op jit(solution)/shard_map/ppermute | solution.py:347
  (3 other events, 1.9 us)

commit v2 on v1

--- a/solution.py
+++ b/solution.py
@@ -130,14 +130,24 @@
 
 
 LINE = 4
+CORES = 2
 NEAR_PAIRS = [(0, 1), (1, 0), (2, 3), (3, 2)]
-INNER_PAIRS = [(1, 2), (2, 1)]
 SWAP = [(0, 1), (1, 0)]
-VMEM_LIMIT = 56 * 1024 * 1024
+VMEM_LIMIT = 16 * 1024 * 1024
+
+
+def inner_pairs():
+    crossing = {1: 2, 2: 1}
+    pairs = []
+    for e in range(LINE):
+        for d in range(CORES):
+            target = (crossing[e], d) if e in crossing else (e, 1 - d)
+            pairs.append((CORES * e + d, CORES * target[0] + target[1]))
+    return pairs
 
 
 def fits_line(mesh):
-    return mesh.shape["expert"] == LINE and mesh.shape["dp"] == 2
+    return mesh.shape["expert"] == LINE and mesh.shape["dp"] == CORES
 
 
 def cell_order():
@@ -166,9 +176,7 @@
     return [me, me ^ 1, me ^ mid, me ^ far]
 
 
-def partial_kernel(
-    grad_a, grad_b, act_a, act_b, info_a, info_b, scaled_ref, own_ref, near_ref, mid_ref, far_ref, wide, cells, turned
-):
+def prepare_kernel(grad_a, grad_b, act_a, act_b, info_a, info_b, scaled_ref, turned, far_ref, wide, cells):
     tiles = info_a.shape[1]
     block = 2 * tiles
     width = grad_a.shape[1]
@@ -185,8 +193,7 @@
     experts = slot_experts()
     gates_a = gate_columns(info_a, experts)
     gates_b = gate_columns(info_b, experts)
-    order = cell_order()
-    for place, cell in enumerate(order):
+    for place, cell in enumerate(cell_order()):
         part_a = cell_rows(0, cell)
         part_b = cell_rows(1, cell)
         for slot in range(4):
@@ -202,36 +209,43 @@
         turned[1, :, pl.ds(col * column, column)] = rows.T
         turned[2, :, pl.ds(col * column, column)] = jnp.concatenate([rows[block:], empty], axis=0).T
         turned[0, :, pl.ds(col * column, column)] = jnp.concatenate([empty, rows[:-block]], axis=0).T
+    kernel_gradient(turned, scaled_ref, 3, far_ref)
+
+
+def kernel_gradient(turned, scaled_ref, slot, ref):
+    width, column = turned.shape[1], turned.shape[2] // TW
     low_half = lax.broadcasted_iota(jnp.int32, (64, 128), 1) < 64
-    for slot, ref in ((3, far_ref), (2, mid_ref), (1, near_ref), (0, own_ref)):
-        for row_off in (-1, 0, 1):
-            for col_off in (-1, 0, 1):
-                lhs = turned[row_off + 1]
-                rhs = scaled_ref[slot]
-                if col_off == 1:
-                    lhs, rhs = lhs[:, column:], rhs[:column]
-                if col_off == -1:
-                    lhs, rhs = lhs[:, :column], rhs[column:]
-                full = jnp.dot(lhs, rhs, preferred_element_type=jnp.float32)
-                tap = (row_off + 1) * 3 + col_off + 1
-                for pair in range(width // 128):
-                    base = pair * 128
-                    piece = jnp.where(
-                        low_half,
-                        full[base : base + 64, base : base + 128],
-                        full[base + 64 : base + 128, base : base + 128],
-                    )
-                    ref[tap, :, pl.ds(base, 128)] = piece.astype(ref.dtype)
-
-
-def answer_kernel(scaled_ref, own_ref, near_ref, mid_ref, far_ref, grad_a, grad_b, out_a, out_b, total, spread):
-    width = grad_a.shape[1]
-    tiles = grad_a.shape[0] // (TH * TW)
-    block = 2 * tiles
+    for row_off in (-1, 0, 1):
+        for col_off in (-1, 0, 1):
+            lhs = turned[row_off + 1]
+            rhs = scaled_ref[slot]
+            if col_off == 1:
+                lhs, rhs = lhs[:, column:], rhs[:column]
+            if col_off == -1:
+                lhs, rhs = lhs[:, :column], rhs[column:]
+            full = jnp.dot(lhs, rhs, preferred_element_type=jnp.float32)
+            tap = (row_off + 1) * 3 + col_off + 1
+            for pair in range(width // 128):
+                base = pair * 128
+                piece = jnp.where(
+                    low_half,
+                    full[base : base + 64, base : base + 128],
+                    full[base + 64 : base + 128, base : base + 128],
+                )
+                ref[tap, :, pl.ds(base, 128)] = piece.astype(ref.dtype)
+
+
+def partial_kernel(scaled_ref, turned, mid_ref, near_ref, own_ref):
+    for slot, ref in ((2, mid_ref), (1, near_ref), (0, own_ref)):
+        kernel_gradient(turned, scaled_ref, slot, ref)
+
+
+def add_answers(scaled_ref, slots, kernels, total):
+    width = total.shape[1]
+    block = total.shape[0] // (TH * TW)
     lane_group = lax.broadcasted_iota(jnp.int32, (64, width), 1) // 64
     masks = [jnp.where(lane_group == g, 1.0, 0.0).astype(jnp.bfloat16) for g in range(width // 64)]
-    total[...] = jnp.zeros_like(total)
-    for slot, ref in enumerate((own_ref, near_ref, mid_ref, far_ref)):
+    for slot, ref in zip(slots, kernels):
         for row_off in (-1, 0, 1):
             for col_off in (-1, 0, 1):
                 tap = (row_off + 1) * 3 + col_off + 1
@@ -250,19 +264,43 @@
                         (((1,), (1,)), ((), ())),
                         preferred_element_type=jnp.float32,
                     )
+
+
+def early_answer_kernel(scaled_ref, own_ref, near_ref, mid_ref, total):
+    total[...] = jnp.zeros_like(total)
+    add_answers(scaled_ref, (0, 1, 2), (own_ref, near_ref, mid_ref), total)
+
+
+def late_answer_kernel(scaled_ref, far_ref, early, grad_a, grad_b, out_a, out_b, total, spread):
+    tiles = grad_a.shape[0] // (TH * TW)
+    block = 2 * tiles
+    strips = grad_a.shape[1] // 128
+    total[...] = early[...]
+    add_answers(scaled_ref, (3,), (far_ref,), total)
     for at, (grad, out) in enumerate(((grad_a, out_a), (grad_b, out_b))):
-        for place, cell in enumerate(cell_order()):
-            for strip in range(width // 128):
+        for strip in range(strips):
+            lanes = pl.ds(strip * 128, 128)
+            for place, cell in enumerate(cell_order()):
                 spread[strip, pl.ds(cell, tiles, stride=TH * TW), :] = total[
-                    pl.ds(place * block + at * tiles, tiles), pl.ds(strip * 128, 128)
+                    pl.ds(place * block + at * tiles, tiles), lanes
                 ]
-        for strip in range(width // 128):
-            lanes = pl.ds(strip * 128, 128)
             out[:, lanes] = (grad[:, lanes].astype(jnp.float32) + spread[strip]).astype(jnp.bfloat16)
 
 
 def on_vmem(count):
     return [pl.BlockSpec(memory_space=pltpu.VMEM)] * count
+
+
+def local_call(kernel, outs, scratch, flops, *operands):
+    return pl.pallas_call(
+        kernel,
+        out_shape=tuple(outs),
+        in_specs=on_vmem(len(operands)),
+        out_specs=tuple(on_vmem(len(outs))),
+        scratch_shapes=scratch,
+        compiler_params=pltpu.CompilerParams(vmem_limit_bytes=VMEM_LIMIT),
+        cost_estimate=pl.CostEstimate(flops=flops, bytes_accessed=2_000_000, transcendentals=0),
+    )(*operands)
 
 
 def weights_travel(activations, upstream, routes, gate_codes, weights):
@@ -279,8 +317,11 @@
     def half(array, which):
         return lax.dynamic_slice_in_dim(array, which * width, width, array.ndim - 1)
 
-    def along(array, pairs):
-        return lax.ppermute(array, "expert", pairs)
+    def near(array):
+        return lax.ppermute(array, "expert", NEAR_PAIRS)
+
+    def across(array):
+        return lax.ppermute(array, ("expert", "dp"), inner_pairs())
 
     def from_next(array, flip):
         pairs = []
@@ -289,12 +330,13 @@
                 pairs.append((2 * ((s + 1) % sections) + d, 2 * s + (1 - d if flip else d)))
         return lax.ppermute(array, ("segment", "dp"), pairs)
 
+    info = jnp.concatenate([routes[0].T, gate_codes[0].T], axis=0)
+    my_weights = half(kernel, core)
+    my_weights, upstream = lax.optimization_barrier((my_weights, upstream))
     upstream_rows = upstream[0].reshape(rows, channels)
     act_rows = activations[0].reshape(rows, channels)
-    info = jnp.concatenate([routes[0].T, gate_codes[0].T], axis=0)
-    my_weights = half(kernel, core)
-    inner_weights = along(my_weights, INNER_PAIRS)
-    near_weights = along(my_weights, NEAR_PAIRS)
+    inner_weights = across(my_weights)
+    near_weights = near(my_weights)
     grad_a = from_next(half(upstream_rows, core), False)
     grad_b = from_next(half(upstream_rows, 1 - core), True)
     act_a = half(act_rows, core)
@@ -302,48 +344,54 @@
     info_b = lax.ppermute(info, "dp", SWAP)
 
     part = jax.ShapeDtypeStruct((taps, group_width, width), jnp.bfloat16)
-    scaled, own_part, near_part, mid_part, far_part = pl.pallas_call(
-        partial_kernel,
-        out_shape=(
+    scaled, turned, far_part = local_call(
+        prepare_kernel,
+        (
             jax.ShapeDtypeStruct((4, 2 * rows, width), jnp.bfloat16),
-            jax.ShapeDtypeStruct((taps, group_width, width), jnp.float32),
-            part,
-            part,
+            jax.ShapeDtypeStruct((3, width, 2 * rows), jnp.bfloat16),
             part,
         ),
-        in_specs=on_vmem(6),
-        out_specs=tuple(on_vmem(5)),
-        scratch_shapes=[
+        [
             pltpu.VMEM((4 * (width // 128), rows, 128), jnp.float32),
             pltpu.VMEM((2 * rows, width), jnp.bfloat16),
-            pltpu.VMEM((3, width, 2 * rows), jnp.bfloat16),
         ],
-        compiler_params=pltpu.CompilerParams(vmem_limit_bytes=VMEM_LIMIT),
-        cost_estimate=pl.CostEstimate(flops=3_000_000_000, bytes_accessed=3_000_000, transcendentals=0),
-    )(grad_a, grad_b, act_a, act_b, info, info_b)
-
-    cross_weights = along(near_weights, INNER_PAIRS)
-    first_swap = along(jnp.where(inner, inner_weights, far_part), NEAR_PAIRS)
-    second_swap = along(jnp.where(inner, cross_weights, mid_part), NEAR_PAIRS)
-    far_sum = along(far_part + first_swap, INNER_PAIRS)
-    mid_sum = along(mid_part + second_swap, INNER_PAIRS)
-    last_swap = along(near_part + far_sum, NEAR_PAIRS)
+        800_000_000,
+        grad_a, grad_b, act_a, act_b, info, info_b,
+    )
+    cross_weights = across(near_weights)
+    first_swap = near(jnp.where(inner, inner_weights, far_part))
+    mid_part, near_part, own_part = local_call(
+        partial_kernel,
+        (part, part, jax.ShapeDtypeStruct((taps, group_width, width), jnp.float32)),
+        [],
+        1_200_000_000,
+        scaled, turned,
+    )
+    second_swap = near(jnp.where(inner, cross_weights, mid_part))
+    far_sum = across(far_part + first_swap)
+    mid_sum = across(mid_part + second_swap)
+    last_swap = near(jnp.where(inner, near_part + far_sum, near_part))
 
     mid_weights = jnp.where(inner, inner_weights, first_swap)
     far_weights = jnp.where(inner, cross_weights, second_swap)
+    (early,) = local_call(
+        early_answer_kernel,
+        (jax.ShapeDtypeStruct((2 * rows, width), jnp.float32),),
+        [],
+        1_200_000_000,
+        scaled, my_weights, near_weights, mid_weights,
+    )
     answer = jax.ShapeDtypeStruct((rows, width), jnp.bfloat16)
-    grad_own, grad_other = pl.pallas_call(
-        answer_kernel,
-        out_shape=(answer, answer),
-        in_specs=on_vmem(7),
-        out_specs=tuple(on_vmem(2)),
-        scratch_shapes=[
+    grad_own, grad_other = local_call(
+        late_answer_kernel,
+        (answer, answer),
+        [
             pltpu.VMEM((2 * rows, width), jnp.float32),
             pltpu.VMEM((width // 128, rows, 128), jnp.float32),
         ],
-        compiler_params=pltpu.CompilerParams(vmem_limit_bytes=VMEM_LIMIT),
-        cost_estimate=pl.CostEstimate(flops=3_000_000_000, bytes_accessed=3_000_000, transcendentals=0),
-    )(scaled, my_weights, near_weights, mid_weights, far_weights, grad_a, grad_b)
+        500_000_000,
+        scaled, far_weights, early, grad_a, grad_b,
+    )
     grad_back = lax.ppermute(grad_other, "dp", SWAP)
 
     def whole(mine, other):
@@ -352,7 +400,8 @@
         )
 
     input_grad = whole(grad_own, grad_back).reshape(per_device, cell_count, channels)
-    kernel_sum = own_part + last_swap.astype(jnp.float32) + mid_sum.astype(jnp.float32)
+    last_swap, input_grad = lax.optimization_barrier((last_swap, input_grad))
+    kernel_sum = own_part + last_swap.astype(jnp.float32) + jnp.where(inner, mid_sum, 0).astype(jnp.float32)
     kernel_mine = kernel_sum.astype(jnp.bfloat16)
     kernel_other = lax.ppermute(kernel_mine, "dp", SWAP)
     weight_grad = whole(kernel_mine, kernel_other).astype(jnp.float32) / per_device

time: 59.3 us -> 47.8 us (0.81)
  the two profiles are of different devices: /device:TPU:19 before, /device:TPU:0 now
where the time goes in v2:
time: 47.8 us; the launch traced here: 47.7 us
  starting transfers between devices  20.1 us (42%)
  waiting for transfers between devices  17 us (36%)
  Pallas kernels  4.61 us (10%)
  other arithmetic  3.07 us (6%)
  local copies, waits for them, and re-layouts  2.08 us (4%)
  between operations  0.82 us (2%)
    ppermute x4, starting transfers between devices, near(): return lax.ppermute(array, 'expert', NEAR_PAIRS)  16 us
    ppermute x4, waiting for transfers between devices, near(): return lax.ppermute(array, 'expert', NEAR_PAIRS)  8.59 us
    ppermute x2, waiting for transfers between devices, from_next(): return lax.ppermute(array, ('segment', 'dp'), pairs)  5.54 us
    pallas_call x4, Pallas kernels, local_call(): pl.pallas_call(kernel, out_shape=tuple(outs), in_specs=on_vmem(len(operan...  4.61 us
    ppermute x2, starting transfers between devices, from_next(): return lax.ppermute(array, ('segment', 'dp'), pairs)  3.11 us
    ppermute x1, waiting for transfers between devices, weights_travel(): kernel_other = lax.ppermute(kernel_mine, 'dp', SWAP)  1.57 us
    ppermute x1, waiting for transfers between devices, weights_travel(): grad_back = lax.ppermute(grad_other, 'dp', SWAP)  1.33 us
    div x1, other arithmetic, weights_travel(): whole(kernel_mine, kernel_other).astype(jnp.float32) / per_device  1.22 us
  transfers between devices with their start and end apart: 14, of which 6 were waited for; matrix products, arithmetic and copies ran while one was open for 6% of the time, Pallas kernels for 10%

profile of v2, /device:TPU:0, one launch (start us, length us, event | category | flops | bytes accessed | tf_op | source)
XLA Modules:
  0.0 47.7 jit_solution(27363220812448875)
XLA Ops:
  0.7 1.0 %copy-done = bf16[1,1,9,64,512]{4,3,2,1,0:T(8,128)(2,1)S(1)} copy-done((bf16[1,1,9,64,512]{4,3,2,1,0:T(8,128)(2,1)S(1)}, bf16[1,1,9,64,512]{4,3,2,1,0:T(8,128)(2,1)}, u32[]{:S(2)}) %copy-start) | copy-done | bytes 589848
  1.7 3.1 %collective-permute-start.8 = (bf16[9,64,256]{2,1,0:T(8,128)(2,1)S(1)}, bf16[9,64,256]{2,1,0:T(8,128)(2,1)S(1)}, u32[]{:S(2)}, u32[]{:S(2)}) collective-permute-start(bf16[9,64,256]{2,1,0:T(8,128)(2,1)S(1)} %dynamic-slice_bitcast_fusion.own_ref), channel_id=1, source_target_pairs={{0,2},{2,0},{4,6},{6,4},{1,3},{3,1},{5,7},{7,5},{8,10},{10,8},{12,... | collective-permute-start | bytes 884744 | tf_op jit(solution)/shard_map/ppermute | solution.py:321
  4.8 0.7 %pad_add_fusion.info_a = s32[4,32]{1,0:T(4,128)S(1)} fusion(s32[2,32]{1,0:T(2,128)} %bitcast.22, s32[2,32]{1,0:T(2,128)} %bitcast.23), kind=kLoop, calls=%fused_computation.10 | loop fusion | flops 128 | bytes 1024 | tf_op jit(solution)/shard_map/concatenate | solution.py:333
  5.5 0.5 %collective-permute-start.3 = (s32[4,32]{1,0:T(4,128)S(1)}, s32[4,32]{1,0:T(4,128)S(1)}, u32[]{:S(2)}, u32[]{:S(2)}) collective-permute-start(s32[4,32]{1,0:T(4,128)S(1)} %pad_add_fusion.info_a), channel_id=1, source_target_pairs={{0,1},{1,0},{2,3},{3,2},{4,5},{5,4},{6,7},{7,6},{8,9},{9,8},{10,11... | collective-permute-start | bytes 1544 | tf_op jit(solution)/shard_map/ppermute | solution.py:344
  6.0 1.0 %constant_dynamic-slice_fusion = (bf16[256,256]{1,0:T(8,128)(2,1)S(1)}, bf16[256,256]{1,0:T(8,128)(2,1)S(1)}) fusion(bf16[256,512]{1,0:T(8,128)(2,1)} %bitcast.19, s32[]{:T(128)S(6)} %select_n.65, s32[]{:T(128)S(6)} %select_n.64), kind=kLoop, calls=%fused_computation.11 | loop fusion | bytes 524296 | tf_op jit(solution)/shard_map/dynamic_slice | solution.py:318
  7.0 0.1 collective-permute-start.2
  7.1 2.6 %collective-permute-start.1 = (bf16[256,256]{1,0:T(8,128)(2,1)S(1)}, bf16[256,256]{1,0:T(8,128)(2,1)S(1)}, u32[]{:S(2)}, u32[]{:S(2)}) collective-permute-start(bf16[256,256]{1,0:T(8,128)(2,1)S(1)} %get-tuple-element.32), channel_id=1, source_target_pairs={{8,1},{9,0},{16,9},{17,8},{24,17},{25,16},{0,25},{1,24},{10,3},{11... | collective-permute-start | bytes 393224 | tf_op jit(solution)/shard_map/ppermute | solution.py:331
  9.7 0.5 %collective-permute-start = (bf16[256,256]{1,0:T(8,128)(2,1)S(1)}, bf16[256,256]{1,0:T(8,128)(2,1)S(1)}, u32[]{:S(2)}, u32[]{:S(2)}) collective-permute-start(bf16[256,256]{1,0:T(8,128)(2,1)S(1)} %get-tuple-element.33), channel_id=1, source_target_pairs={{8,0},{9,1},{16,8},{17,9},{24,16},{25,17},{0,24},{1,25},{10,2},{11... | collective-permute-start | bytes 393224 | tf_op jit(solution)/shard_map/ppermute | solution.py:331
  10.3 3.3 %collective-permute-done.1.grad_b = bf16[256,256]{1,0:T(8,128)(2,1)S(1)} collective-permute-done((bf16[256,256]{1,0:T(8,128)(2,1)S(1)}, bf16[256,256]{1,0:T(8,128)(2,1)S(1)}, u32[]{:S(2)}, u32[]{:S(2)}) %collective-permute-start.1) | collective-permute-done | bytes 131104 | tf_op jit(solution)/shard_map/ppermute | solution.py:331
  13.6 2.2 %collective-permute-done.grad_a = bf16[256,256]{1,0:T(8,128)(2,1)S(1)} collective-permute-done((bf16[256,256]{1,0:T(8,128)(2,1)S(1)}, bf16[256,256]{1,0:T(8,128)(2,1)S(1)}, u32[]{:S(2)}, u32[]{:S(2)}) %collective-permute-start) | collective-permute-done | bytes 131104 | tf_op jit(solution)/shard_map/ppermute | solution.py:331
  15.8 0.9 %shard_map.68 = (bf16[4,512,256]{2,1,0:T(8,128)(2,1)S(1)}, bf16[3,256,512]{2,1,0:T(8,128)(2,1)S(1)}, bf16[9,64,256]{2,1,0:T(8,128)(2,1)S(1)}) custom-call(bf16[256,256]{1,0:T(8,128)(2,1)S(1)} %collective-permute-done.grad_a, bf16[256,256]{1,0:T(8,128)(2,1)S(1)} %collective-permute-done.1.grad_b, bf16[256,256]{1,0:T(8,128)(2,1)S(1)} %get-tuple-element.31.act_a, ...), custom_call_target="tpu_custom_call" | custom-call | flops 800000000 | bytes 2000000 | tf_op jit(solution)/shard_map/pallas_call | solution.py:295
  16.8 3.2 %collective-permute-start.5 = (bf16[9,64,256]{2,1,0:T(8,128)(2,1)S(1)}, bf16[9,64,256]{2,1,0:T(8,128)(2,1)S(1)}, u32[]{:S(2)}, u32[]{:S(2)}) collective-permute-start(bf16[9,64,256]{2,1,0:T(8,128)(2,1)S(1)} %broadcast_select_fusion.3), channel_id=1, source_target_pairs={{0,2},{2,0},{4,6},{6,4},{1,3},{3,1},{5,7},{7,5},{8,10},{10,8},{12,... | collective-permute-start | bytes 884744 | tf_op jit(solution)/shard_map/ppermute | solution.py:321
  20.0 1.4 %shard_map.69 = (bf16[9,64,256]{2,1,0:T(8,128)(2,1)S(1)}, bf16[9,64,256]{2,1,0:T(8,128)(2,1)S(1)}, f32[9,64,256]{2,1,0:T(8,128)S(1)}) custom-call(bf16[4,512,256]{2,1,0:T(8,128)(2,1)S(1)} %get-tuple-element.15.scaled_ref, bf16[3,256,512]{2,1,0:T(8,128)(2,1)S(1)} %get-tuple-element.16.turned), custom_call_target="tpu_custom_call" | custom-call | flops 1200000000 | bytes 2000000 | tf_op jit(solution)/shard_map/pallas_call | solution.py:295
  21.5 7.3 %collective-permute-start.10 = (bf16[9,64,256]{2,1,0:T(8,128)(2,1)S(1)}, bf16[9,64,256]{2,1,0:T(8,128)(2,1)S(1)}, u32[]{:S(2)}, u32[]{:S(2)}) collective-permute-start(bf16[9,64,256]{2,1,0:T(8,128)(2,1)S(1)} %broadcast_select_fusion.2), channel_id=1, source_target_pairs={{0,2},{2,0},{4,6},{6,4},{1,3},{3,1},{5,7},{7,5},{8,10},{10,8},{12,... | collective-permute-start | bytes 884744 | tf_op jit(solution)/shard_map/ppermute | solution.py:321
  29.0 1.6 %shard_map.70.early = f32[512,256]{1,0:T(8,128)S(1)} custom-call(bf16[4,512,256]{2,1,0:T(8,128)(2,1)S(1)} %get-tuple-element.15.scaled_ref, bf16[9,64,256]{2,1,0:T(8,128)(2,1)S(1)} %dynamic-slice_bitcast_fusion.own_ref, bf16[9,64,256]{2,1,0:T(8,128)(2,1)S(1)} %collective-permute-done.8.near_ref, bf16[9,64,256]{2,1,0:T(8,128)(2,1)S(1)} %get-tuple-element.28.mid_ref), custom_call_target="tpu_custom_call" | custom-call | flops 1200000000 | bytes 2000000 | tf_op jit(solution)/shard_map/pallas_call | solution.py:295
  30.5 4.5 %collective-permute-done.10 = bf16[9,64,256]{2,1,0:T(8,128)(2,1)S(1)} collective-permute-done((bf16[9,64,256]{2,1,0:T(8,128)(2,1)S(1)}, bf16[9,64,256]{2,1,0:T(8,128)(2,1)S(1)}, u32[]{:S(2)}, u32[]{:S(2)}) %collective-permute-start.10) | collective-permute-done | bytes 294944 | tf_op jit(solution)/shard_map/ppermute | solution.py:321
  35.2 2.4 %collective-permute-start.7 = (bf16[9,64,256]{2,1,0:T(8,128)(2,1)S(1)}, bf16[9,64,256]{2,1,0:T(8,128)(2,1)S(1)}, u32[]{:S(2)}, u32[]{:S(2)}) collective-permute-start(bf16[9,64,256]{2,1,0:T(8,128)(2,1)S(1)} %add_select_fusion), channel_id=1, source_target_pairs={{0,2},{2,0},{4,6},{6,4},{1,3},{3,1},{5,7},{7,5},{8,10},{10,8},{12,... | collective-permute-start | bytes 884744 | tf_op jit(solution)/shard_map/ppermute | solution.py:321
  37.6 0.7 %shard_map.71 = (bf16[256,256]{1,0:T(8,128)(2,1)S(1)}, bf16[256,256]{1,0:T(8,128)(2,1)S(1)}) custom-call(bf16[4,512,256]{2,1,0:T(8,128)(2,1)S(1)} %get-tuple-element.15.scaled_ref, bf16[9,64,256]{2,1,0:T(8,128)(2,1)S(1)} %get-tuple-element.27.far_ref, f32[512,256]{1,0:T(8,128)S(1)} %shard_map.70.early, bf16[256,256]{1,0:T(8,128)(2,1)S(1)} %collective-permute-done.grad_a, ...), custom_call_target="tpu_custom_call" | custom-call | flops 500000000 | bytes 2000000 | tf_op jit(solution)/shard_map/pallas_call | solution.py:295
  38.4 1.3 %collective-permute-done.11 = bf16[256,256]{1,0:T(8,128)(2,1)S(1)} collective-permute-done((bf16[256,256]{1,0:T(8,128)(2,1)S(1)}, bf16[256,256]{1,0:T(8,128)(2,1)S(1)}, u32[]{:S(2)}, u32[]{:S(2)}) %collective-permute-start.11) | collective-permute-done | bytes 131104 | tf_op jit(solution)/shard_map/ppermute | solution.py:395
  39.7 0.8 %maximum_select_fusion.1 = bf16[32,8,512]{2,1,0:T(8,128)(2,1)} fusion(bf16[32,8,256]{2,1,0:T(8,128)(2,1)S(1)} %bitcast.21, bf16[32,8,256]{2,1,0:T(8,128)(2,1)S(1)} %bitcast.15, pred[]{:T(512)S(6)} %eq.12), kind=kLoop, calls=%fused_computation.9 | loop fusion | flops 1179648 | bytes 524289 | tf_op jit(solution)/shard_map/jit(_where)/select_n | solution.py:398
  40.6 4.1 %collective-permute-done.7 = bf16[9,64,256]{2,1,0:T(8,128)(2,1)S(1)} collective-permute-done((bf16[9,64,256]{2,1,0:T(8,128)(2,1)S(1)}, bf16[9,64,256]{2,1,0:T(8,128)(2,1)S(1)}, u32[]{:S(2)}, u32[]{:S(2)}) %collective-permute-start.7) | collective-permute-done | bytes 294944 | tf_op jit(solution)/shard_map/ppermute | solution.py:321
  44.7 0.1 add_convert_fusion
  44.9 1.6 %collective-permute-done.13 = bf16[9,64,256]{2,1,0:T(8,128)(2,1)S(1)} collective-permute-done((bf16[9,64,256]{2,1,0:T(8,128)(2,1)S(1)}, bf16[9,64,256]{2,1,0:T(8,128)(2,1)S(1)}, u32[]{:S(2)}, u32[]{:S(2)}) %collective-permute-start.13) | collective-permute-done | bytes 294944 | tf_op jit(solution)/shard_map/ppermute | solution.py:406
  46.4 1.2 %convert_multiply_fusion = f32[1,1,9,64,512]{4,3,2,1,0:T(8,128)} fusion(bf16[1,1,9,64,256]{4,3,2,1,0:T(8,128)(2,1)S(1)} %bitcast.17, bf16[1,1,9,64,256]{4,3,2,1,0:T(8,128)(2,1)S(1)} %bitcast.16, pred[]{:T(512)S(6)} %eq.12), kind=kLoop, calls=%fused_computation | loop fusion | flops 3244032 | bytes 1769473 | tf_op jit(solution)/shard_map/div | solution.py:407
  (24 shorter events, 0.6 us)
Async XLA Ops:
  0.6 1.1 %copy-start = (bf16[1,1,9,64,512]{4,3,2,1,0:T(8,128)(2,1)S(1)}, bf16[1,1,9,64,512]{4,3,2,1,0:T(8,128)(2,1)}, u32[]{:S(2)}) copy-start(bf16[1,1,9,64,512]{4,3,2,1,0:T(8,128)(2,1)} %param.9) | copy-start | bytes 1769476
  0.6 6.5 %copy-start.1 = (bf16[1,32,8,512]{3,2,1,0:T(8,128)(2,1)S(1)}, bf16[1,32,8,512]{3,2,1,0:T(8,128)(2,1)}, u32[]{:S(2)}) copy-start(bf16[1,32,8,512]{3,2,1,0:T(8,128)(2,1)} %param.6) | copy-start | bytes 786436
  1.7 15.0 %collective-permute-start.8 = (bf16[9,64,256]{2,1,0:T(8,128)(2,1)S(1)}, bf16[9,64,256]{2,1,0:T(8,128)(2,1)S(1)}, u32[]{:S(2)}, u32[]{:S(2)}) collective-permute-start(bf16[9,64,256]{2,1,0:T(8,128)(2,1)S(1)} %dynamic-slice_bitcast_fusion.own_ref), channel_id=1, source_target_pairs={{0,2},{2,0},{4,6},{6,4},{1,3},{3,1},{5,7},{7,5},{8,10},{10,8},{12,... | collective-permute-start | bytes 884744 | tf_op jit(solution)/shard_map/ppermute | solution.py:321
  4.8 12.0 %collective-permute-start.4 = (bf16[9,64,256]{2,1,0:T(8,128)(2,1)S(1)}, bf16[9,64,256]{2,1,0:T(8,128)(2,1)S(1)}, u32[]{:S(2)}, u32[]{:S(2)}) collective-permute-start(bf16[9,64,256]{2,1,0:T(8,128)(2,1)S(1)} %dynamic-slice_bitcast_fusion.own_ref), channel_id=1, source_target_pairs={{0,1},{1,0},{2,4},{3,5},{4,2},{5,3},{6,7},{7,6},{8,9},{9,8},{10,12... | collective-permute-start | bytes 884744 | tf_op jit(solution)/shard_map/ppermute | solution.py:324
  5.5 4.2 %collective-permute-start.3 = (s32[4,32]{1,0:T(4,128)S(1)}, s32[4,32]{1,0:T(4,128)S(1)}, u32[]{:S(2)}, u32[]{:S(2)}) collective-permute-start(s32[4,32]{1,0:T(4,128)S(1)} %pad_add_fusion.info_a), channel_id=1, source_target_pairs={{0,1},{1,0},{2,3},{3,2},{4,5},{5,4},{6,7},{7,6},{8,9},{9,8},{10,11... | collective-permute-start | bytes 1544 | tf_op jit(solution)/shard_map/ppermute | solution.py:344
  7.0 3.2 %collective-permute-start.2 = (bf16[256,256]{1,0:T(8,128)(2,1)S(1)}, bf16[256,256]{1,0:T(8,128)(2,1)S(1)}, u32[]{:S(2)}, u32[]{:S(2)}) collective-permute-start(bf16[256,256]{1,0:T(8,128)(2,1)S(1)} %get-tuple-element.30), channel_id=1, source_target_pairs={{0,1},{1,0},{2,3},{3,2},{4,5},{5,4},{6,7},{7,6},{8,9},{9,8},{10,11... | collective-permute-start | bytes 393224 | tf_op jit(solution)/shard_map/ppermute | solution.py:343
  7.1 6.4 %collective-permute-start.1 = (bf16[256,256]{1,0:T(8,128)(2,1)S(1)}, bf16[256,256]{1,0:T(8,128)(2,1)S(1)}, u32[]{:S(2)}, u32[]{:S(2)}) collective-permute-start(bf16[256,256]{1,0:T(8,128)(2,1)S(1)} %get-tuple-element.32), channel_id=1, source_target_pairs={{8,1},{9,0},{16,9},{17,8},{24,17},{25,16},{0,25},{1,24},{10,3},{11... | collective-permute-start | bytes 393224 | tf_op jit(solution)/shard_map/ppermute | solution.py:331
  9.7 6.1 %collective-permute-start = (bf16[256,256]{1,0:T(8,128)(2,1)S(1)}, bf16[256,256]{1,0:T(8,128)(2,1)S(1)}, u32[]{:S(2)}, u32[]{:S(2)}) collective-permute-start(bf16[256,256]{1,0:T(8,128)(2,1)S(1)} %get-tuple-element.33), channel_id=1, source_target_pairs={{8,0},{9,1},{16,8},{17,9},{24,16},{25,17},{0,24},{1,25},{10,2},{11... | collective-permute-start | bytes 393224 | tf_op jit(solution)/shard_map/ppermute | solution.py:331
  16.7 4.7 %collective-permute-start.9 = (bf16[9,64,256]{2,1,0:T(8,128)(2,1)S(1)}, bf16[9,64,256]{2,1,0:T(8,128)(2,1)S(1)}, u32[]{:S(2)}, u32[]{:S(2)}) collective-permute-start(bf16[9,64,256]{2,1,0:T(8,128)(2,1)S(1)} %collective-permute-done.8.near_ref), channel_id=1, source_target_pairs={{0,1},{1,0},{2,4},{3,5},{4,2},{5,3},{6,7},{7,6},{8,9},{9,8},{10,12... | collective-permute-start | bytes 884744 | tf_op jit(solution)/shard_map/ppermute | solution.py:324
  16.8 12.0 %collective-permute-start.5 = (bf16[9,64,256]{2,1,0:T(8,128)(2,1)S(1)}, bf16[9,64,256]{2,1,0:T(8,128)(2,1)S(1)}, u32[]{:S(2)}, u32[]{:S(2)}) collective-permute-start(bf16[9,64,256]{2,1,0:T(8,128)(2,1)S(1)} %broadcast_select_fusion.3), channel_id=1, source_target_pairs={{0,2},{2,0},{4,6},{6,4},{1,3},{3,1},{5,7},{7,5},{8,10},{10,8},{12,... | collective-permute-start | bytes 884744 | tf_op jit(solution)/shard_map/ppermute | solution.py:321
  21.5 13.5 %collective-permute-start.10 = (bf16[9,64,256]{2,1,0:T(8,128)(2,1)S(1)}, bf16[9,64,256]{2,1,0:T(8,128)(2,1)S(1)}, u32[]{:S(2)}, u32[]{:S(2)}) collective-permute-start(bf16[9,64,256]{2,1,0:T(8,128)(2,1)S(1)} %broadcast_select_fusion.2), channel_id=1, source_target_pairs={{0,2},{2,0},{4,6},{6,4},{1,3},{3,1},{5,7},{7,5},{8,10},{10,8},{12,... | collective-permute-start | bytes 884744 | tf_op jit(solution)/shard_map/ppermute | solution.py:321
  28.9 6.3 %collective-permute-start.6 = (bf16[9,64,256]{2,1,0:T(8,128)(2,1)S(1)}, bf16[9,64,256]{2,1,0:T(8,128)(2,1)S(1)}, u32[]{:S(2)}, u32[]{:S(2)}) collective-permute-start(bf16[9,64,256]{2,1,0:T(8,128)(2,1)S(1)} %get-tuple-element.29), channel_id=1, source_target_pairs={{0,1},{1,0},{2,4},{3,5},{4,2},{5,3},{6,7},{7,6},{8,9},{9,8},{10,12... | collective-permute-start | bytes 884744 | tf_op jit(solution)/shard_map/ppermute | solution.py:324
  35.1 9.6 %collective-permute-start.12 = (bf16[9,64,256]{2,1,0:T(8,128)(2,1)S(1)}, bf16[9,64,256]{2,1,0:T(8,128)(2,1)S(1)}, u32[]{:S(2)}, u32[]{:S(2)}) collective-permute-start(bf16[9,64,256]{2,1,0:T(8,128)(2,1)S(1)} %get-tuple-element.26), channel_id=1, source_target_pairs={{0,1},{1,0},{2,4},{3,5},{4,2},{5,3},{6,7},{7,6},{8,9},{9,8},{10,12... | collective-permute-start | bytes 884744 | tf_op jit(solution)/shard_map/ppermute | solution.py:324
  35.2 9.5 %collective-permute-start.7 = (bf16[9,64,256]{2,1,0:T(8,128)(2,1)S(1)}, bf16[9,64,256]{2,1,0:T(8,128)(2,1)S(1)}, u32[]{:S(2)}, u32[]{:S(2)}) collective-permute-start(bf16[9,64,256]{2,1,0:T(8,128)(2,1)S(1)} %add_select_fusion), channel_id=1, source_target_pairs={{0,2},{2,0},{4,6},{6,4},{1,3},{3,1},{5,7},{7,5},{8,10},{10,8},{12,... | collective-permute-start | bytes 884744 | tf_op jit(solution)/shard_map/ppermute | solution.py:321
  38.3 1.4 %collective-permute-start.11 = (bf16[256,256]{1,0:T(8,128)(2,1)S(1)}, bf16[256,256]{1,0:T(8,128)(2,1)S(1)}, u32[]{:S(2)}, u32[]{:S(2)}) collective-permute-start(bf16[256,256]{1,0:T(8,128)(2,1)S(1)} %get-tuple-element.22), channel_id=1, source_target_pairs={{0,1},{1,0},{2,3},{3,2},{4,5},{5,4},{6,7},{7,6},{8,9},{9,8},{10,11... | collective-permute-start | bytes 393224 | tf_op jit(solution)/shard_map/ppermute | solution.py:395
  44.8 1.6 %collective-permute-start.13 = (bf16[9,64,256]{2,1,0:T(8,128)(2,1)S(1)}, bf16[9,64,256]{2,1,0:T(8,128)(2,1)S(1)}, u32[]{:S(2)}, u32[]{:S(2)}) collective-permute-start(bf16[9,64,256]{2,1,0:T(8,128)(2,1)S(1)} %add_convert_fusion), channel_id=1, source_target_pairs={{0,1},{1,0},{2,3},{3,2},{4,5},{5,4},{6,7},{7,6},{8,9},{9,8},{10,11... | collective-permute-start | bytes 884744 | tf_op jit(solution)/shard_map/ppermute | solution.py:406

commit v3 on v2

--- a/solution.py
+++ b/solution.py
@@ -1,3 +1,5 @@
+import functools
+
 import jax
 import jax.numpy as jnp
 import numpy as np
@@ -287,6 +289,42 @@
             out[:, lanes] = (grad[:, lanes].astype(jnp.float32) + spread[strip]).astype(jnp.bfloat16)
 
 
+def place_half_kernel(scale, side, core_ref, half_ref, *refs):
+    out, staged, done = refs[-3:]
+    taps, _, width = half_ref.shape
+    at = core_ref[0] if side == 0 else 1 - core_ref[0]
+    lanes = pl.ds(pl.multiple_of(at * width, width), width)
+    copies = []
+    for tap in range(taps):
+        staged[tap] = half_ref[tap].astype(jnp.float32) * scale
+        copies.append(pltpu.make_async_copy(staged.at[tap], out.at[tap, :, lanes], done.at[tap]))
+        copies[-1].start()
+    for copy in copies:
+        copy.wait()
+
+
+def place_half(scale, side, core_at, half, begun=None):
+    taps, group_width, width = half.shape
+    specs = [pl.BlockSpec(memory_space=pltpu.SMEM)] + on_vmem(1)
+    operands = [core_at, half]
+    if begun is not None:
+        specs.append(pl.BlockSpec(memory_space=pl.ANY))
+        operands.append(begun)
+    return pl.pallas_call(
+        functools.partial(place_half_kernel, scale, side),
+        out_shape=jax.ShapeDtypeStruct((taps, group_width, 2 * width), jnp.float32),
+        in_specs=specs,
+        out_specs=pl.BlockSpec(memory_space=pl.ANY),
+        scratch_shapes=[
+            pltpu.VMEM((taps, group_width, width), jnp.float32),
+            pltpu.SemaphoreType.DMA((taps,)),
+        ],
+        input_output_aliases={} if begun is None else {2: 0},
+        compiler_params=pltpu.CompilerParams(vmem_limit_bytes=VMEM_LIMIT),
+        cost_estimate=pl.CostEstimate(flops=1000, bytes_accessed=1000, transcendentals=0),
+    )(*operands)
+
+
 def on_vmem(count):
     return [pl.BlockSpec(memory_space=pltpu.VMEM)] * count
 
@@ -299,7 +337,7 @@
         out_specs=tuple(on_vmem(len(outs))),
         scratch_shapes=scratch,
         compiler_params=pltpu.CompilerParams(vmem_limit_bytes=VMEM_LIMIT),
-        cost_estimate=pl.CostEstimate(flops=flops, bytes_accessed=2_000_000, transcendentals=0),
+        cost_estimate=pl.CostEstimate(flops=1000, bytes_accessed=1000, transcendentals=0),
     )(*operands)
 
 
@@ -310,8 +348,7 @@
     per_device, cell_count, channels = activations.shape[1:]
     rows = per_device * cell_count
     width = channels // 2
-    kernel = weights[0, 0]
-    taps, group_width = kernel.shape[0], kernel.shape[1]
+    taps, group_width = weights.shape[2:4]
     sections = lax.axis_size("segment")
 
     def half(array, which):
@@ -323,25 +360,20 @@
     def across(array):
         return lax.ppermute(array, ("expert", "dp"), inner_pairs())
 
-    def from_next(array, flip):
-        pairs = []
-        for s in range(sections):
-            for d in range(2):
-                pairs.append((2 * ((s + 1) % sections) + d, 2 * s + (1 - d if flip else d)))
-        return lax.ppermute(array, ("segment", "dp"), pairs)
+    def from_next(array):
+        return lax.ppermute(array, "segment", [((s + 1) % sections, s) for s in range(sections)])
 
     info = jnp.concatenate([routes[0].T, gate_codes[0].T], axis=0)
-    my_weights = half(kernel, core)
-    my_weights, upstream = lax.optimization_barrier((my_weights, upstream))
-    upstream_rows = upstream[0].reshape(rows, channels)
+    info_b = lax.ppermute(info, "dp", SWAP)
+    grad_rows = from_next(upstream[0].reshape(rows, channels))
+    my_weights = half(weights[0, 0], core)
+    inner_weights = across(my_weights)
     act_rows = activations[0].reshape(rows, channels)
-    inner_weights = across(my_weights)
-    near_weights = near(my_weights)
-    grad_a = from_next(half(upstream_rows, core), False)
-    grad_b = from_next(half(upstream_rows, 1 - core), True)
     act_a = half(act_rows, core)
     act_b = lax.ppermute(half(act_rows, 1 - core), "dp", SWAP)
-    info_b = lax.ppermute(info, "dp", SWAP)
+    near_weights = near(my_weights)
+    grad_a = half(grad_rows, core)
+    grad_b = lax.ppermute(half(grad_rows, 1 - core), "dp", SWAP)
 
     part = jax.ShapeDtypeStruct((taps, group_width, width), jnp.bfloat16)
     scaled, turned, far_part = local_call(
@@ -358,6 +390,7 @@
         800_000_000,
         grad_a, grad_b, act_a, act_b, info, info_b,
     )
+    near_weights, far_part = lax.optimization_barrier((near_weights, far_part))
     cross_weights = across(near_weights)
     first_swap = near(jnp.where(inner, inner_weights, far_part))
     mid_part, near_part, own_part = local_call(
@@ -367,6 +400,7 @@
         1_200_000_000,
         scaled, turned,
     )
+    first_swap, mid_part = lax.optimization_barrier((first_swap, mid_part))
     second_swap = near(jnp.where(inner, cross_weights, mid_part))
     far_sum = across(far_part + first_swap)
     mid_sum = across(mid_part + second_swap)
@@ -404,7 +438,9 @@
     kernel_sum = own_part + last_swap.astype(jnp.float32) + jnp.where(inner, mid_sum, 0).astype(jnp.float32)
     kernel_mine = kernel_sum.astype(jnp.bfloat16)
     kernel_other = lax.ppermute(kernel_mine, "dp", SWAP)
-    weight_grad = whole(kernel_mine, kernel_other).astype(jnp.float32) / per_device
+    core_at = jnp.reshape(core, (1,)).astype(jnp.int32)
+    begun = place_half(1.0 / per_device, 0, core_at, kernel_mine)
+    weight_grad = place_half(1.0 / per_device, 1, core_at, kernel_other, begun)
     return (input_grad[None], weight_grad[None, None])
 
 

time: 47.8 us -> 42.3 us (0.88)
  the two profiles are of different devices: /device:TPU:0 before, /device:TPU:19 now
where the time goes in v3:
time: 42.3 us; the launch traced here: 42.1 us
  waiting for transfers between devices  19.2 us (45%)
  starting transfers between devices  12.8 us (30%)
  Pallas kernels  6.37 us (15%)
  local copies, waits for them, and re-layouts  1.77 us (4%)
  other arithmetic  1.17 us (3%)
  between operations  0.76 us (2%)
    ppermute x4, waiting for transfers between devices, near(): return lax.ppermute(array, 'expert', NEAR_PAIRS)  6.9 us
    ppermute x4, waiting for transfers between devices, across(): return lax.ppermute(array, ('expert', 'dp'), inner_pairs())  6.04 us
    ppermute x4, starting transfers between devices, near(): return lax.ppermute(array, 'expert', NEAR_PAIRS)  4.74 us
    pallas_call x4, Pallas kernels, local_call(): pl.pallas_call(kernel, out_shape=tuple(outs), in_specs=on_vmem(len(operan...  4.6 us
    ppermute x1, waiting for transfers between devices, from_next(): lax.ppermute(array, 'segment', [((s + 1) % sections, s) for s in range(se...  3.83 us
    ppermute x1, starting transfers between devices, weights_travel(): kernel_other = lax.ppermute(kernel_mine, 'dp', SWAP)  2.57 us
    ppermute x1, starting transfers between devices, weights_travel(): grad_back = lax.ppermute(grad_other, 'dp', SWAP)  2.55 us
    pallas_call x2, Pallas kernels, place_half(): pl.pallas_call(functools.partial(place_half_kernel, scale, side), out_sha...  1.77 us
  transfers between devices with their start and end apart: 14, of which 9 were waited for; matrix products, arithmetic and copies ran while one was open for 5% of the time, Pallas kernels for 13%

profile of v3, /device:TPU:19, one launch (start us, length us, event | category | flops | bytes accessed | tf_op | source)
XLA Modules:
  0.0 42.1 jit_solution(7419753735122006626)
XLA Ops:
  1.0 0.7 %copy-done = bf16[1,1,9,64,512]{4,3,2,1,0:T(8,128)(2,1)S(1)} copy-done((bf16[1,1,9,64,512]{4,3,2,1,0:T(8,128)(2,1)S(1)}, bf16[1,1,9,64,512]{4,3,2,1,0:T(8,128)(2,1)}, u32[]{:S(2)}) %copy-start) | copy-done | bytes 589848
  2.0 1.8 %collective-permute-start.4 = (bf16[9,64,256]{2,1,0:T(8,128)(2,1)S(1)}, bf16[9,64,256]{2,1,0:T(8,128)(2,1)S(1)}, u32[]{:S(2)}, u32[]{:S(2)}) collective-permute-start(bf16[9,64,256]{2,1,0:T(8,128)(2,1)S(1)} %dynamic-slice_bitcast_fusion.own_ref), channel_id=1, source_target_pairs={{0,2},{2,0},{4,6},{6,4},{1,3},{3,1},{5,7},{7,5},{8,10},{10,8},{12,... | collective-permute-start | bytes 884744 | tf_op jit(solution)/shard_map/ppermute | solution.py:358
  3.8 1.0 %constant_dynamic-slice_fusion = (bf16[256,256]{1,0:T(8,128)(2,1)S(1)}, bf16[256,256]{1,0:T(8,128)(2,1)S(1)}) fusion(bf16[256,512]{1,0:T(8,128)(2,1)} %bitcast.18, s32[]{:T(128)S(6)} %select_n.50, s32[]{:T(128)S(6)} %select_n.49), kind=kLoop, calls=%fused_computation.9 | loop fusion | bytes 524296 | tf_op jit(solution)/shard_map/dynamic_slice | solution.py:355
  4.8 0.4 collective-permute-start.2
  5.2 3.8 %collective-permute-done = bf16[256,512]{1,0:T(8,128)(2,1)S(1)} collective-permute-done((bf16[256,512]{1,0:T(8,128)(2,1)}, bf16[256,512]{1,0:T(8,128)(2,1)S(1)}, u32[]{:S(2)}, u32[]{:S(2)}) %collective-permute-start) | collective-permute-done | bytes 262176 | tf_op jit(solution)/shard_map/ppermute | solution.py:364
  9.0 1.6 %collective-permute-start.1 = (bf16[256,256]{1,0:T(8,128)(2,1)S(1)}, bf16[256,256]{1,0:T(8,128)(2,1)S(1)}, u32[]{:S(2)}, u32[]{:S(2)}) collective-permute-start(bf16[256,256]{1,0:T(8,128)(2,1)S(1)} %get-tuple-element.36), channel_id=1, source_target_pairs={{0,1},{1,0},{2,3},{3,2},{4,5},{5,4},{6,7},{7,6},{8,9},{9,8},{10,11... | collective-permute-start | bytes 393224 | tf_op jit(solution)/shard_map/ppermute | solution.py:376
  10.8 1.1 %collective-permute-done.3.info_b = s32[4,32]{1,0:T(4,128)S(1)} collective-permute-done((s32[4,32]{1,0:T(4,128)S(1)}, s32[4,32]{1,0:T(4,128)S(1)}, u32[]{:S(2)}, u32[]{:S(2)}) %collective-permute-start.3) | collective-permute-done | bytes 544 | tf_op jit(solution)/shard_map/ppermute | solution.py:367
  11.9 0.9 %shard_map.68 = (bf16[4,512,256]{2,1,0:T(8,128)(2,1)S(1)}, bf16[3,256,512]{2,1,0:T(8,128)(2,1)S(1)}, bf16[9,64,256]{2,1,0:T(8,128)(2,1)S(1)}) custom-call(bf16[256,256]{1,0:T(8,128)(2,1)S(1)} %get-tuple-element.37.grad_a, bf16[256,256]{1,0:T(8,128)(2,1)S(1)} %collective-permute-done.1.grad_b, bf16[256,256]{1,0:T(8,128)(2,1)S(1)} %get-tuple-element.35.act_a, ...), custom_call_target="tpu_custom_call" | custom-call | flops 1000 | bytes 1000 | tf_op jit(solution)/shard_map/pallas_call | solution.py:333
  12.9 1.4 %collective-permute-start.6 = (bf16[9,64,256]{2,1,0:T(8,128)(2,1)S(1)}, bf16[9,64,256]{2,1,0:T(8,128)(2,1)S(1)}, u32[]{:S(2)}, u32[]{:S(2)}) collective-permute-start(bf16[9,64,256]{2,1,0:T(8,128)(2,1)S(1)} %broadcast_select_fusion.3), channel_id=1, source_target_pairs={{0,2},{2,0},{4,6},{6,4},{1,3},{3,1},{5,7},{7,5},{8,10},{10,8},{12,... | collective-permute-start | bytes 884744 | tf_op jit(solution)/shard_map/ppermute | solution.py:358
  14.2 1.4 %shard_map.69 = (bf16[9,64,256]{2,1,0:T(8,128)(2,1)S(1)}, bf16[9,64,256]{2,1,0:T(8,128)(2,1)S(1)}, f32[9,64,256]{2,1,0:T(8,128)S(1)}) custom-call(bf16[4,512,256]{2,1,0:T(8,128)(2,1)S(1)} %get-tuple-element.16.scaled_ref, bf16[3,256,512]{2,1,0:T(8,128)(2,1)S(1)} %get-tuple-element.17.turned), custom_call_target="tpu_custom_call" | custom-call | flops 1000 | bytes 1000 | tf_op jit(solution)/shard_map/pallas_call | solution.py:333
  15.6 5.7 %collective-permute-done.6 = bf16[9,64,256]{2,1,0:T(8,128)(2,1)S(1)} collective-permute-done((bf16[9,64,256]{2,1,0:T(8,128)(2,1)S(1)}, bf16[9,64,256]{2,1,0:T(8,128)(2,1)S(1)}, u32[]{:S(2)}, u32[]{:S(2)}) %collective-permute-start.6) | collective-permute-done | bytes 294944 | tf_op jit(solution)/shard_map/ppermute | solution.py:358
  21.7 0.7 %collective-permute-done.9 = bf16[9,64,256]{2,1,0:T(8,128)(2,1)S(1)} collective-permute-done((bf16[9,64,256]{2,1,0:T(8,128)(2,1)S(1)}, bf16[9,64,256]{2,1,0:T(8,128)(2,1)S(1)}, u32[]{:S(2)}, u32[]{:S(2)}) %collective-permute-start.9) | collective-permute-done | bytes 294944 | tf_op jit(solution)/shard_map/ppermute | solution.py:361
  22.4 1.5 %collective-permute-start.10 = (bf16[9,64,256]{2,1,0:T(8,128)(2,1)S(1)}, bf16[9,64,256]{2,1,0:T(8,128)(2,1)S(1)}, u32[]{:S(2)}, u32[]{:S(2)}) collective-permute-start(bf16[9,64,256]{2,1,0:T(8,128)(2,1)S(1)} %broadcast_select_fusion.2), channel_id=1, source_target_pairs={{0,2},{2,0},{4,6},{6,4},{1,3},{3,1},{5,7},{7,5},{8,10},{10,8},{12,... | collective-permute-start | bytes 884744 | tf_op jit(solution)/shard_map/ppermute | solution.py:358
  23.9 5.2 %collective-permute-done.7 = bf16[9,64,256]{2,1,0:T(8,128)(2,1)S(1)} collective-permute-done((bf16[9,64,256]{2,1,0:T(8,128)(2,1)S(1)}, bf16[9,64,256]{2,1,0:T(8,128)(2,1)S(1)}, u32[]{:S(2)}, u32[]{:S(2)}) %collective-permute-start.7) | collective-permute-done | bytes 294944 | tf_op jit(solution)/shard_map/ppermute | solution.py:361
  29.1 1.1 %collective-permute-done.10 = bf16[9,64,256]{2,1,0:T(8,128)(2,1)S(1)} collective-permute-done((bf16[9,64,256]{2,1,0:T(8,128)(2,1)S(1)}, bf16[9,64,256]{2,1,0:T(8,128)(2,1)S(1)}, u32[]{:S(2)}, u32[]{:S(2)}) %collective-permute-start.10) | collective-permute-done | bytes 294944 | tf_op jit(solution)/shard_map/ppermute | solution.py:358
  30.4 1.6 %shard_map.70.early = f32[512,256]{1,0:T(8,128)S(1)} custom-call(bf16[4,512,256]{2,1,0:T(8,128)(2,1)S(1)} %get-tuple-element.16.scaled_ref, bf16[9,64,256]{2,1,0:T(8,128)(2,1)S(1)} %dynamic-slice_bitcast_fusion.own_ref, bf16[9,64,256]{2,1,0:T(8,128)(2,1)S(1)} %collective-permute-done.4.near_ref, bf16[9,64,256]{2,1,0:T(8,128)(2,1)S(1)} %get-tuple-element.32.mid_ref), custom_call_target="tpu_custom_call" | custom-call | flops 1000 | bytes 1000 | tf_op jit(solution)/shard_map/pallas_call | solution.py:333
  32.0 0.7 %shard_map.71 = (bf16[256,256]{1,0:T(8,128)(2,1)S(1)}, bf16[256,256]{1,0:T(8,128)(2,1)S(1)}) custom-call(bf16[4,512,256]{2,1,0:T(8,128)(2,1)S(1)} %get-tuple-element.16.scaled_ref, bf16[9,64,256]{2,1,0:T(8,128)(2,1)S(1)} %get-tuple-element.31.far_ref, f32[512,256]{1,0:T(8,128)S(1)} %shard_map.70.early, bf16[256,256]{1,0:T(8,128)(2,1)S(1)} %get-tuple-element.37.grad_a, ...), custom_call_target="tpu_custom_call" | custom-call | flops 1000 | bytes 1000 | tf_op jit(solution)/shard_map/pallas_call | solution.py:333
  32.8 2.5 %collective-permute-start.11 = (bf16[256,256]{1,0:T(8,128)(2,1)S(1)}, bf16[256,256]{1,0:T(8,128)(2,1)S(1)}, u32[]{:S(2)}, u32[]{:S(2)}) collective-permute-start(bf16[256,256]{1,0:T(8,128)(2,1)S(1)} %get-tuple-element.26), channel_id=1, source_target_pairs={{0,1},{1,0},{2,3},{3,2},{4,5},{5,4},{6,7},{7,6},{8,9},{9,8},{10,11... | collective-permute-start | bytes 393224 | tf_op jit(solution)/shard_map/ppermute | solution.py:429
  35.3 1.0 %collective-permute-done.11 = bf16[256,256]{1,0:T(8,128)(2,1)S(1)} collective-permute-done((bf16[256,256]{1,0:T(8,128)(2,1)S(1)}, bf16[256,256]{1,0:T(8,128)(2,1)S(1)}, u32[]{:S(2)}, u32[]{:S(2)}) %collective-permute-start.11) | collective-permute-done | bytes 131104 | tf_op jit(solution)/shard_map/ppermute | solution.py:429
  36.3 0.8 %maximum_select_fusion = bf16[32,8,512]{2,1,0:T(8,128)(2,1)} fusion(bf16[32,8,256]{2,1,0:T(8,128)(2,1)S(1)} %bitcast.19, bf16[32,8,256]{2,1,0:T(8,128)(2,1)S(1)} %bitcast.15, pred[]{:T(512)S(6)} %eq.11), kind=kLoop, calls=%fused_computation.7 | loop fusion | flops 1179648 | bytes 524289 | tf_op jit(solution)/shard_map/jit(_where)/select_n | solution.py:432
  37.5 2.6 %collective-permute-start.13 = (bf16[9,64,256]{2,1,0:T(8,128)(2,1)S(1)}, bf16[9,64,256]{2,1,0:T(8,128)(2,1)S(1)}, u32[]{:S(2)}, u32[]{:S(2)}) collective-permute-start(bf16[9,64,256]{2,1,0:T(8,128)(2,1)S(1)} %add_convert_fusion.half_ref), channel_id=1, source_target_pairs={{0,1},{1,0},{2,3},{3,2},{4,5},{5,4},{6,7},{7,6},{8,9},{9,8},{10,11... | collective-permute-start | bytes 884744 | tf_op jit(solution)/shard_map/ppermute | solution.py:440
  40.0 0.9 %shard_map.72.refs_0_ = f32[9,64,512]{2,1,0:T(8,128)} custom-call(s32[1]{0:T(128)} %bitcast.10.core_ref, bf16[9,64,256]{2,1,0:T(8,128)(2,1)S(1)} %add_convert_fusion.half_ref), custom_call_target="tpu_custom_call" | custom-call | flops 1000 | bytes 1000 | tf_op jit(solution)/shard_map/pallas_call | solution.py:313
  40.9 0.3 collective-permute-done.13.half_ref
  41.2 0.9 %shard_map.73 = f32[9,64,512]{2,1,0:T(8,128)} custom-call(s32[1]{0:T(128)} %bitcast.10.core_ref, bf16[9,64,256]{2,1,0:T(8,128)(2,1)S(1)} %collective-permute-done.13.half_ref, f32[9,64,512]{2,1,0:T(8,128)} %shard_map.72.refs_0_), custom_call_target="tpu_custom_call", output_to_operand_aliasing={{}: (2, {})} | custom-call | flops 1000 | bytes 1000 | tf_op jit(solution)/shard_map/pallas_call | solution.py:313
  (27 shorter events, 1.7 us)
Async XLA Ops:
  0.6 1.1 %copy-start = (bf16[1,1,9,64,512]{4,3,2,1,0:T(8,128)(2,1)S(1)}, bf16[1,1,9,64,512]{4,3,2,1,0:T(8,128)(2,1)}, u32[]{:S(2)}) copy-start(bf16[1,1,9,64,512]{4,3,2,1,0:T(8,128)(2,1)} %param.9) | copy-start | bytes 1769476
  0.6 10.0 %copy-start.1 = (s32[1,32,2]{1,2,0:T(2,128)S(1)}, s32[1,32,2]{1,2,0:T(2,128)}, u32[]{:S(2)}) copy-start(s32[1,32,2]{1,2,0:T(2,128)} %param.8) | copy-start | bytes 772
  0.7 10.0 %copy-start.2 = (s32[1,32,2]{1,2,0:T(2,128)S(1)}, s32[1,32,2]{1,2,0:T(2,128)}, u32[]{:S(2)}) copy-start(s32[1,32,2]{1,2,0:T(2,128)} %param.7) | copy-start | bytes 772
  0.7 8.3 %collective-permute-start = (bf16[256,512]{1,0:T(8,128)(2,1)}, bf16[256,512]{1,0:T(8,128)(2,1)S(1)}, u32[]{:S(2)}, u32[]{:S(2)}) collective-permute-start(bf16[256,512]{1,0:T(8,128)(2,1)} %bitcast.22), channel_id=1, source_target_pairs={{8,0},{16,8},{24,16},{0,24},{9,1},{17,9},{25,17},{1,25},{10,2},{18... | collective-permute-start | bytes 786440 | tf_op jit(solution)/shard_map/ppermute | solution.py:364
  1.7 11.1 %collective-permute-start.5 = (bf16[9,64,256]{2,1,0:T(8,128)(2,1)S(1)}, bf16[9,64,256]{2,1,0:T(8,128)(2,1)S(1)}, u32[]{:S(2)}, u32[]{:S(2)}) collective-permute-start(bf16[9,64,256]{2,1,0:T(8,128)(2,1)S(1)} %dynamic-slice_bitcast_fusion.own_ref), channel_id=1, source_target_pairs={{0,1},{1,0},{2,4},{3,5},{4,2},{5,3},{6,7},{7,6},{8,9},{9,8},{10,12... | collective-permute-start | bytes 884744 | tf_op jit(solution)/shard_map/ppermute | solution.py:361
  2.0 10.8 %collective-permute-start.4 = (bf16[9,64,256]{2,1,0:T(8,128)(2,1)S(1)}, bf16[9,64,256]{2,1,0:T(8,128)(2,1)S(1)}, u32[]{:S(2)}, u32[]{:S(2)}) collective-permute-start(bf16[9,64,256]{2,1,0:T(8,128)(2,1)S(1)} %dynamic-slice_bitcast_fusion.own_ref), channel_id=1, source_target_pairs={{0,2},{2,0},{4,6},{6,4},{1,3},{3,1},{5,7},{7,5},{8,10},{10,8},{12,... | collective-permute-start | bytes 884744 | tf_op jit(solution)/shard_map/ppermute | solution.py:358
  4.8 7.1 %collective-permute-start.2 = (bf16[256,256]{1,0:T(8,128)(2,1)S(1)}, bf16[256,256]{1,0:T(8,128)(2,1)S(1)}, u32[]{:S(2)}, u32[]{:S(2)}) collective-permute-start(bf16[256,256]{1,0:T(8,128)(2,1)S(1)} %get-tuple-element.34), channel_id=1, source_target_pairs={{0,1},{1,0},{2,3},{3,2},{4,5},{5,4},{6,7},{7,6},{8,9},{9,8},{10,11... | collective-permute-start | bytes 393224 | tf_op jit(solution)/shard_map/ppermute | solution.py:373
  9.0 2.9 %collective-permute-start.1 = (bf16[256,256]{1,0:T(8,128)(2,1)S(1)}, bf16[256,256]{1,0:T(8,128)(2,1)S(1)}, u32[]{:S(2)}, u32[]{:S(2)}) collective-permute-start(bf16[256,256]{1,0:T(8,128)(2,1)S(1)} %get-tuple-element.36), channel_id=1, source_target_pairs={{0,1},{1,0},{2,3},{3,2},{4,5},{5,4},{6,7},{7,6},{8,9},{9,8},{10,11... | collective-permute-start | bytes 393224 | tf_op jit(solution)/shard_map/ppermute | solution.py:376
  10.7 1.2 %collective-permute-start.3 = (s32[4,32]{1,0:T(4,128)S(1)}, s32[4,32]{1,0:T(4,128)S(1)}, u32[]{:S(2)}, u32[]{:S(2)}) collective-permute-start(s32[4,32]{1,0:T(4,128)S(1)} %pad_add_fusion.info_a), channel_id=1, source_target_pairs={{0,1},{1,0},{2,3},{3,2},{4,5},{5,4},{6,7},{7,6},{8,9},{9,8},{10,11... | collective-permute-start | bytes 1544 | tf_op jit(solution)/shard_map/ppermute | solution.py:367
  12.9 8.5 %collective-permute-start.6 = (bf16[9,64,256]{2,1,0:T(8,128)(2,1)S(1)}, bf16[9,64,256]{2,1,0:T(8,128)(2,1)S(1)}, u32[]{:S(2)}, u32[]{:S(2)}) collective-permute-start(bf16[9,64,256]{2,1,0:T(8,128)(2,1)S(1)} %broadcast_select_fusion.3), channel_id=1, source_target_pairs={{0,2},{2,0},{4,6},{6,4},{1,3},{3,1},{5,7},{7,5},{8,10},{10,8},{12,... | collective-permute-start | bytes 884744 | tf_op jit(solution)/shard_map/ppermute | solution.py:358
  14.2 8.1 %collective-permute-start.9 = (bf16[9,64,256]{2,1,0:T(8,128)(2,1)S(1)}, bf16[9,64,256]{2,1,0:T(8,128)(2,1)S(1)}, u32[]{:S(2)}, u32[]{:S(2)}) collective-permute-start(bf16[9,64,256]{2,1,0:T(8,128)(2,1)S(1)} %collective-permute-done.4.near_ref), channel_id=1, source_target_pairs={{0,1},{1,0},{2,4},{3,5},{4,2},{5,3},{6,7},{7,6},{8,9},{9,8},{10,12... | collective-permute-start | bytes 884744 | tf_op jit(solution)/shard_map/ppermute | solution.py:361
  21.4 7.6 %collective-permute-start.7 = (bf16[9,64,256]{2,1,0:T(8,128)(2,1)S(1)}, bf16[9,64,256]{2,1,0:T(8,128)(2,1)S(1)}, u32[]{:S(2)}, u32[]{:S(2)}) collective-permute-start(bf16[9,64,256]{2,1,0:T(8,128)(2,1)S(1)} %get-tuple-element.33), channel_id=1, source_target_pairs={{0,1},{1,0},{2,4},{3,5},{4,2},{5,3},{6,7},{7,6},{8,9},{9,8},{10,12... | collective-permute-start | bytes 884744 | tf_op jit(solution)/shard_map/ppermute | solution.py:361
  22.4 7.9 %collective-permute-start.10 = (bf16[9,64,256]{2,1,0:T(8,128)(2,1)S(1)}, bf16[9,64,256]{2,1,0:T(8,128)(2,1)S(1)}, u32[]{:S(2)}, u32[]{:S(2)}) collective-permute-start(bf16[9,64,256]{2,1,0:T(8,128)(2,1)S(1)} %broadcast_select_fusion.2), channel_id=1, source_target_pairs={{0,2},{2,0},{4,6},{6,4},{1,3},{3,1},{5,7},{7,5},{8,10},{10,8},{12,... | collective-permute-start | bytes 884744 | tf_op jit(solution)/shard_map/ppermute | solution.py:358
  29.1 8.1 %collective-permute-start.8 = (bf16[9,64,256]{2,1,0:T(8,128)(2,1)S(1)}, bf16[9,64,256]{2,1,0:T(8,128)(2,1)S(1)}, u32[]{:S(2)}, u32[]{:S(2)}) collective-permute-start(bf16[9,64,256]{2,1,0:T(8,128)(2,1)S(1)} %add_select_fusion), channel_id=1, source_target_pairs={{0,2},{2,0},{4,6},{6,4},{1,3},{3,1},{5,7},{7,5},{8,10},{10,8},{12,... | collective-permute-start | bytes 884744 | tf_op jit(solution)/shard_map/ppermute | solution.py:358
  30.3 7.0 %collective-permute-start.12 = (bf16[9,64,256]{2,1,0:T(8,128)(2,1)S(1)}, bf16[9,64,256]{2,1,0:T(8,128)(2,1)S(1)}, u32[]{:S(2)}, u32[]{:S(2)}) collective-permute-start(bf16[9,64,256]{2,1,0:T(8,128)(2,1)S(1)} %get-tuple-element.30), channel_id=1, source_target_pairs={{0,1},{1,0},{2,4},{3,5},{4,2},{5,3},{6,7},{7,6},{8,9},{9,8},{10,12... | collective-permute-start | bytes 884744 | tf_op jit(solution)/shard_map/ppermute | solution.py:361
  32.8 3.5 %collective-permute-start.11 = (bf16[256,256]{1,0:T(8,128)(2,1)S(1)}, bf16[256,256]{1,0:T(8,128)(2,1)S(1)}, u32[]{:S(2)}, u32[]{:S(2)}) collective-permute-start(bf16[256,256]{1,0:T(8,128)(2,1)S(1)} %get-tuple-element.26), channel_id=1, source_target_pairs={{0,1},{1,0},{2,3},{3,2},{4,5},{5,4},{6,7},{7,6},{8,9},{9,8},{10,11... | collective-permute-start | bytes 393224 | tf_op jit(solution)/shard_map/ppermute | solution.py:429
  37.5 3.8 %collective-permute-start.13 = (bf16[9,64,256]{2,1,0:T(8,128)(2,1)S(1)}, bf16[9,64,256]{2,1,0:T(8,128)(2,1)S(1)}, u32[]{:S(2)}, u32[]{:S(2)}) collective-permute-start(bf16[9,64,256]{2,1,0:T(8,128)(2,1)S(1)} %add_convert_fusion.half_ref), channel_id=1, source_target_pairs={{0,1},{1,0},{2,3},{3,2},{4,5},{5,4},{6,7},{7,6},{8,9},{9,8},{10,11... | collective-permute-start | bytes 884744 | tf_op jit(solution)/shard_map/ppermute | solution.py:440

commit v4 on v3

--- a/solution.py
+++ b/solution.py
@@ -165,8 +165,8 @@
 def gate_columns(info_ref, experts):
     rows = [own_gates(info_ref[...], expert) for expert in experts]
     count = rows[0].shape[1]
-    table = jnp.concatenate(rows + [jnp.zeros((8 - len(rows), count), jnp.float32)], axis=0)
-    table = jnp.concatenate([table, jnp.zeros((8, 128 - count), jnp.float32)], axis=1)
+    table = jnp.concatenate(rows + [jnp.zeros((128 - len(rows), count), jnp.float32)], axis=0)
+    table = jnp.concatenate([table, jnp.zeros((128, 128 - count), jnp.float32)], axis=1)
     return table.T[:count]
 
 
@@ -178,13 +178,10 @@
     return [me, me ^ 1, me ^ mid, me ^ far]
 
 
-def prepare_kernel(grad_a, grad_b, act_a, act_b, info_a, info_b, scaled_ref, turned, far_ref, wide, cells):
-    tiles = info_a.shape[1]
-    block = 2 * tiles
-    width = grad_a.shape[1]
-    column = TH * block
-    strips = width // 128
-    for at, ref in enumerate((grad_a, grad_b, act_a, act_b)):
+def rows_by_cell(refs, wide):
+    strips = refs[0].shape[1] // 128
+    tiles = refs[0].shape[0] // (TH * TW)
+    for at, ref in enumerate(refs):
         for strip in range(strips):
             wide[at * strips + strip] = ref[:, pl.ds(strip * 128, 128)].astype(jnp.float32)
 
@@ -192,18 +189,16 @@
         pieces = [wide[at * strips + strip, pl.ds(cell, tiles, stride=TH * TW), :] for strip in range(strips)]
         return jnp.concatenate(pieces, axis=1)
 
-    experts = slot_experts()
-    gates_a = gate_columns(info_a, experts)
-    gates_b = gate_columns(info_b, experts)
+    return cell_rows
+
+
+def turn_kernel(act_a, act_b, turned, wide, cells):
+    width = act_a.shape[1]
+    block = 2 * act_a.shape[0] // (TH * TW)
+    column = TH * block
+    cell_rows = rows_by_cell((act_a, act_b), wide)
     for place, cell in enumerate(cell_order()):
-        part_a = cell_rows(0, cell)
-        part_b = cell_rows(1, cell)
-        for slot in range(4):
-            both = jnp.concatenate(
-                [part_a * gates_a[:, slot : slot + 1], part_b * gates_b[:, slot : slot + 1]], axis=0
-            )
-            scaled_ref[slot, pl.ds(place * block, block), :] = both.astype(jnp.bfloat16)
-        act_rows = jnp.concatenate([cell_rows(2, cell), cell_rows(3, cell)], axis=0)
+        act_rows = jnp.concatenate([cell_rows(0, cell), cell_rows(1, cell)], axis=0)
         cells[pl.ds(place * block, block), :] = act_rows.astype(jnp.bfloat16)
     empty = jnp.zeros((block, width), jnp.bfloat16)
     for col in range(TW):
@@ -211,7 +206,21 @@
         turned[1, :, pl.ds(col * column, column)] = rows.T
         turned[2, :, pl.ds(col * column, column)] = jnp.concatenate([rows[block:], empty], axis=0).T
         turned[0, :, pl.ds(col * column, column)] = jnp.concatenate([empty, rows[:-block]], axis=0).T
-    kernel_gradient(turned, scaled_ref, 3, far_ref)
+
+
+def prepare_kernel(grad_a, grad_b, turned, info_a, info_b, cells, gates, far_ref, wide, scaled):
+    tiles = info_a.shape[1]
+    block = 2 * tiles
+    cell_rows = rows_by_cell((grad_a, grad_b), wide)
+    experts = slot_experts()
+    gates[pl.ds(0, tiles), :] = gate_columns(info_a, experts)
+    gates[pl.ds(tiles, tiles), :] = gate_columns(info_b, experts)
+    far_gate = gates[:, 3:4]
+    for place, cell in enumerate(cell_order()):
+        both = jnp.concatenate([cell_rows(0, cell), cell_rows(1, cell)], axis=0)
+        cells[pl.ds(place * block, block), :] = both.astype(jnp.bfloat16)
+        scaled[0, pl.ds(place * block, block), :] = (both * far_gate).astype(jnp.bfloat16)
+    kernel_gradient(turned, scaled, 0, far_ref)
 
 
 def kernel_gradient(turned, scaled_ref, slot, ref):
@@ -237,7 +246,12 @@
                 ref[tap, :, pl.ds(base, 128)] = piece.astype(ref.dtype)
 
 
-def partial_kernel(scaled_ref, turned, mid_ref, near_ref, own_ref):
+def partial_kernel(cells, gates, turned, scaled_ref, mid_ref, near_ref, own_ref):
+    block = gates.shape[0]
+    for place in range(TH * TW):
+        rows = cells[pl.ds(place * block, block), :].astype(jnp.float32)
+        for slot in range(4):
+            scaled_ref[slot, pl.ds(place * block, block), :] = (rows * gates[:, slot : slot + 1]).astype(jnp.bfloat16)
     for slot, ref in ((2, mid_ref), (1, near_ref), (0, own_ref)):
         kernel_gradient(turned, scaled_ref, slot, ref)
 
@@ -295,9 +309,10 @@
     at = core_ref[0] if side == 0 else 1 - core_ref[0]
     lanes = pl.ds(pl.multiple_of(at * width, width), width)
     copies = []
-    for tap in range(taps):
-        staged[tap] = half_ref[tap].astype(jnp.float32) * scale
-        copies.append(pltpu.make_async_copy(staged.at[tap], out.at[tap, :, lanes], done.at[tap]))
+    for tap in range(0, taps, 3):
+        these = pl.ds(tap, min(3, taps - tap))
+        staged[these] = half_ref[these].astype(jnp.float32) * scale
+        copies.append(pltpu.make_async_copy(staged.at[these], out.at[these, :, lanes], done.at[tap]))
         copies[-1].start()
     for copy in copies:
         copy.wait()
@@ -376,29 +391,44 @@
     grad_b = lax.ppermute(half(grad_rows, 1 - core), "dp", SWAP)
 
     part = jax.ShapeDtypeStruct((taps, group_width, width), jnp.bfloat16)
-    scaled, turned, far_part = local_call(
+    (turned,) = local_call(
+        turn_kernel,
+        (jax.ShapeDtypeStruct((3, width, 2 * rows), jnp.bfloat16),),
+        [
+            pltpu.VMEM((2 * (width // 128), rows, 128), jnp.float32),
+            pltpu.VMEM((2 * rows, width), jnp.bfloat16),
+        ],
+        200_000_000,
+        act_a, act_b,
+    )
+    cells, gates, far_part = local_call(
         prepare_kernel,
         (
-            jax.ShapeDtypeStruct((4, 2 * rows, width), jnp.bfloat16),
-            jax.ShapeDtypeStruct((3, width, 2 * rows), jnp.bfloat16),
+            jax.ShapeDtypeStruct((2 * rows, width), jnp.bfloat16),
+            jax.ShapeDtypeStruct((2 * per_device, 128), jnp.float32),
             part,
         ),
         [
-            pltpu.VMEM((4 * (width // 128), rows, 128), jnp.float32),
-            pltpu.VMEM((2 * rows, width), jnp.bfloat16),
+            pltpu.VMEM((2 * (width // 128), rows, 128), jnp.float32),
+            pltpu.VMEM((1, 2 * rows, width), jnp.bfloat16),
         ],
-        800_000_000,
-        grad_a, grad_b, act_a, act_b, info, info_b,
+        600_000_000,
+        grad_a, grad_b, turned, info, info_b,
     )
     near_weights, far_part = lax.optimization_barrier((near_weights, far_part))
     cross_weights = across(near_weights)
     first_swap = near(jnp.where(inner, inner_weights, far_part))
-    mid_part, near_part, own_part = local_call(
+    scaled, mid_part, near_part, own_part = local_call(
         partial_kernel,
-        (part, part, jax.ShapeDtypeStruct((taps, group_width, width), jnp.float32)),
+        (
+            jax.ShapeDtypeStruct((4, 2 * rows, width), jnp.bfloat16),
+            part,
+            part,
+            jax.ShapeDtypeStruct((taps, group_width, width), jnp.float32),
+        ),
         [],
         1_200_000_000,
-        scaled, turned,
+        cells, gates, turned,
     )
     first_swap, mid_part = lax.optimization_barrier((first_swap, mid_part))
     second_swap = near(jnp.where(inner, cross_weights, mid_part))

time: 42.3 us -> 42.1 us (level)
    ppermute x1, starting transfers between devices: 0.41 us -> 1.02 us  [weights_travel(): act_b = lax.ppermute(half(act_rows, 1 - core), 'dp', SWAP)]
    ppermute x4, starting transfers between devices: 4.74 us -> 4.28 us  [near(): return lax.ppermute(array, 'expert', NEAR_PAIRS)]
    pallas_call x4 -> x5, Pallas kernels: 4.6 us -> 4.86 us  [local_call(): pl.pallas_call(kernel, out_shape=tuple(outs), in_specs=on_vmem(len(operan...]
  transfers between devices with their start and end apart: 14 -> 14, of which waited for: 9 -> 9; matrix products, arithmetic and copies ran while one was open for 5% -> 5% of each run, Pallas kernels for 13% -> 14%
where the time goes in v4:
time: 42.1 us; the launch traced here: 42 us
  waiting for transfers between devices  18.9 us (45%)
  starting transfers between devices  12.8 us (30%)
  Pallas kernels  6.65 us (16%)
  local copies, waits for them, and re-layouts  1.77 us (4%)
  other arithmetic  1.15 us (3%)
  between operations  0.77 us (2%)
    ppermute x4, waiting for transfers between devices, near(): return lax.ppermute(array, 'expert', NEAR_PAIRS)  6.79 us
    ppermute x4, waiting for transfers between devices, across(): return lax.ppermute(array, ('expert', 'dp'), inner_pairs())  6.04 us
    pallas_call x5, Pallas kernels, local_call(): pl.pallas_call(kernel, out_shape=tuple(outs), in_specs=on_vmem(len(operan...  4.86 us
    ppermute x4, starting transfers between devices, near(): return lax.ppermute(array, 'expert', NEAR_PAIRS)  4.28 us
    ppermute x1, waiting for transfers between devices, from_next(): lax.ppermute(array, 'segment', [((s + 1) % sections, s) for s in range(se...  3.9 us
    ppermute x1, starting transfers between devices, weights_travel(): kernel_other = lax.ppermute(kernel_mine, 'dp', SWAP)  2.58 us
    ppermute x1, starting transfers between devices, weights_travel(): grad_back = lax.ppermute(grad_other, 'dp', SWAP)  2.55 us
    pallas_call x2, Pallas kernels, place_half(): pl.pallas_call(functools.partial(place_half_kernel, scale, side), out_sha...  1.8 us
  transfers between devices with their start and end apart: 14, of which 9 were waited for; matrix products, arithmetic and copies ran while one was open for 5% of the time, Pallas kernels for 14%

profile of v4, /device:TPU:19, one launch (start us, length us, event | category | flops | bytes accessed | tf_op | source)
XLA Modules:
  0.0 42.0 jit_solution(233758692684959252)
XLA Ops:
  0.7 0.3 collective-permute-start
  1.0 0.7 %copy-done = bf16[1,1,9,64,512]{4,3,2,1,0:T(8,128)(2,1)S(1)} copy-done((bf16[1,1,9,64,512]{4,3,2,1,0:T(8,128)(2,1)S(1)}, bf16[1,1,9,64,512]{4,3,2,1,0:T(8,128)(2,1)}, u32[]{:S(2)}) %copy-start) | copy-done | bytes 589848
  1.7 1.4 %collective-permute-start.4 = (bf16[9,64,256]{2,1,0:T(8,128)(2,1)S(1)}, bf16[9,64,256]{2,1,0:T(8,128)(2,1)S(1)}, u32[]{:S(2)}, u32[]{:S(2)}) collective-permute-start(bf16[9,64,256]{2,1,0:T(8,128)(2,1)S(1)} %dynamic-slice_bitcast_fusion.own_ref), channel_id=1, source_target_pairs={{0,2},{2,0},{4,6},{6,4},{1,3},{3,1},{5,7},{7,5},{8,10},{10,8},{12,... | collective-permute-start | bytes 884744 | tf_op jit(solution)/shard_map/ppermute | solution.py:373
  3.1 1.0 %constant_dynamic-slice_fusion = (bf16[256,256]{1,0:T(8,128)(2,1)S(1)}, bf16[256,256]{1,0:T(8,128)(2,1)S(1)}) fusion(bf16[256,512]{1,0:T(8,128)(2,1)} %bitcast.18, s32[]{:T(128)S(6)} %select_n.50, s32[]{:T(128)S(6)} %select_n.49), kind=kLoop, calls=%fused_computation.9 | loop fusion | bytes 524296 | tf_op jit(solution)/shard_map/dynamic_slice | solution.py:370
  4.1 1.0 %collective-permute-start.2 = (bf16[256,256]{1,0:T(8,128)(2,1)S(1)}, bf16[256,256]{1,0:T(8,128)(2,1)S(1)}, u32[]{:S(2)}, u32[]{:S(2)}) collective-permute-start(bf16[256,256]{1,0:T(8,128)(2,1)S(1)} %get-tuple-element.36), channel_id=1, source_target_pairs={{0,1},{1,0},{2,3},{3,2},{4,5},{5,4},{6,7},{7,6},{8,9},{9,8},{10,11... | collective-permute-start | bytes 393224 | tf_op jit(solution)/shard_map/ppermute | solution.py:388
  5.1 3.9 %collective-permute-done = bf16[256,512]{1,0:T(8,128)(2,1)S(1)} collective-permute-done((bf16[256,512]{1,0:T(8,128)(2,1)}, bf16[256,512]{1,0:T(8,128)(2,1)S(1)}, u32[]{:S(2)}, u32[]{:S(2)}) %collective-permute-start) | collective-permute-done | bytes 262176 | tf_op jit(solution)/shard_map/ppermute | solution.py:379
  9.0 1.6 %collective-permute-start.1 = (bf16[256,256]{1,0:T(8,128)(2,1)S(1)}, bf16[256,256]{1,0:T(8,128)(2,1)S(1)}, u32[]{:S(2)}, u32[]{:S(2)}) collective-permute-start(bf16[256,256]{1,0:T(8,128)(2,1)S(1)} %get-tuple-element.38), channel_id=1, source_target_pairs={{0,1},{1,0},{2,3},{3,2},{4,5},{5,4},{6,7},{7,6},{8,9},{9,8},{10,11... | collective-permute-start | bytes 393224 | tf_op jit(solution)/shard_map/ppermute | solution.py:391
  11.0 0.8 %collective-permute-done.3.info_b = s32[4,32]{1,0:T(4,128)S(1)} collective-permute-done((s32[4,32]{1,0:T(4,128)S(1)}, s32[4,32]{1,0:T(4,128)S(1)}, u32[]{:S(2)}, u32[]{:S(2)}) %collective-permute-start.3) | collective-permute-done | bytes 544 | tf_op jit(solution)/shard_map/ppermute | solution.py:382
  11.9 0.8 %shard_map.69 = (bf16[512,256]{1,0:T(8,128)(2,1)S(1)}, f32[64,128]{1,0:T(8,128)S(1)}, bf16[9,64,256]{2,1,0:T(8,128)(2,1)S(1)}) custom-call(bf16[256,256]{1,0:T(8,128)(2,1)S(1)} %get-tuple-element.39.grad_a, bf16[256,256]{1,0:T(8,128)(2,1)S(1)} %collective-permute-done.1.grad_b, bf16[3,256,512]{2,1,0:T(8,128)(2,1)S(1)} %shard_map.68.turned, ...), custom_call_target="tpu_custom_call" | custom-call | flops 1000 | bytes 1000 | tf_op jit(solution)/shard_map/pallas_call | solution.py:348
  12.7 1.4 %collective-permute-start.6 = (bf16[9,64,256]{2,1,0:T(8,128)(2,1)S(1)}, bf16[9,64,256]{2,1,0:T(8,128)(2,1)S(1)}, u32[]{:S(2)}, u32[]{:S(2)}) collective-permute-start(bf16[9,64,256]{2,1,0:T(8,128)(2,1)S(1)} %broadcast_select_fusion.3), channel_id=1, source_target_pairs={{0,2},{2,0},{4,6},{6,4},{1,3},{3,1},{5,7},{7,5},{8,10},{10,8},{12,... | collective-permute-start | bytes 884744 | tf_op jit(solution)/shard_map/ppermute | solution.py:373
  14.1 1.5 %shard_map.70 = (bf16[4,512,256]{2,1,0:T(8,128)(2,1)S(1)}, bf16[9,64,256]{2,1,0:T(8,128)(2,1)S(1)}, bf16[9,64,256]{2,1,0:T(8,128)(2,1)S(1)}, f32[9,64,256]{2,1,0:T(8,128)S(1)}) custom-call(bf16[512,256]{1,0:T(8,128)(2,1)S(1)} %get-tuple-element.17.cells, f32[64,128]{1,0:T(8,128)S(1)} %get-tuple-element.18.gates, bf16[3,256,512]{2,1,0:T(8,128)(2,1)S(1)} %shard_map.68.turned), custom_call_target="tpu_custom_call" | custom-call | flops 1000 | bytes 1000 | tf_op jit(solution)/shard_map/pallas_call | solution.py:348
  15.6 5.6 %collective-permute-done.6 = bf16[9,64,256]{2,1,0:T(8,128)(2,1)S(1)} collective-permute-done((bf16[9,64,256]{2,1,0:T(8,128)(2,1)S(1)}, bf16[9,64,256]{2,1,0:T(8,128)(2,1)S(1)}, u32[]{:S(2)}, u32[]{:S(2)}) %collective-permute-start.6) | collective-permute-done | bytes 294944 | tf_op jit(solution)/shard_map/ppermute | solution.py:373
  21.5 0.7 %collective-permute-done.9 = bf16[9,64,256]{2,1,0:T(8,128)(2,1)S(1)} collective-permute-done((bf16[9,64,256]{2,1,0:T(8,128)(2,1)S(1)}, bf16[9,64,256]{2,1,0:T(8,128)(2,1)S(1)}, u32[]{:S(2)}, u32[]{:S(2)}) %collective-permute-start.9) | collective-permute-done | bytes 294944 | tf_op jit(solution)/shard_map/ppermute | solution.py:376
  22.2 1.5 %collective-permute-start.10 = (bf16[9,64,256]{2,1,0:T(8,128)(2,1)S(1)}, bf16[9,64,256]{2,1,0:T(8,128)(2,1)S(1)}, u32[]{:S(2)}, u32[]{:S(2)}) collective-permute-start(bf16[9,64,256]{2,1,0:T(8,128)(2,1)S(1)} %broadcast_select_fusion.2), channel_id=1, source_target_pairs={{0,2},{2,0},{4,6},{6,4},{1,3},{3,1},{5,7},{7,5},{8,10},{10,8},{12,... | collective-permute-start | bytes 884744 | tf_op jit(solution)/shard_map/ppermute | solution.py:373
  23.7 5.2 %collective-permute-done.7 = bf16[9,64,256]{2,1,0:T(8,128)(2,1)S(1)} collective-permute-done((bf16[9,64,256]{2,1,0:T(8,128)(2,1)S(1)}, bf16[9,64,256]{2,1,0:T(8,128)(2,1)S(1)}, u32[]{:S(2)}, u32[]{:S(2)}) %collective-permute-start.7) | collective-permute-done | bytes 294944 | tf_op jit(solution)/shard_map/ppermute | solution.py:376
  29.0 1.1 %collective-permute-done.10 = bf16[9,64,256]{2,1,0:T(8,128)(2,1)S(1)} collective-permute-done((bf16[9,64,256]{2,1,0:T(8,128)(2,1)S(1)}, bf16[9,64,256]{2,1,0:T(8,128)(2,1)S(1)}, u32[]{:S(2)}, u32[]{:S(2)}) %collective-permute-start.10) | collective-permute-done | bytes 294944 | tf_op jit(solution)/shard_map/ppermute | solution.py:373
  30.3 1.6 %shard_map.71.early = f32[512,256]{1,0:T(8,128)S(1)} custom-call(bf16[4,512,256]{2,1,0:T(8,128)(2,1)S(1)} %get-tuple-element.24.scaled_ref, bf16[9,64,256]{2,1,0:T(8,128)(2,1)S(1)} %dynamic-slice_bitcast_fusion.own_ref, bf16[9,64,256]{2,1,0:T(8,128)(2,1)S(1)} %collective-permute-done.4.near_ref, bf16[9,64,256]{2,1,0:T(8,128)(2,1)S(1)} %get-tuple-element.34.mid_ref), custom_call_target="tpu_custom_call" | custom-call | flops 1000 | bytes 1000 | tf_op jit(solution)/shard_map/pallas_call | solution.py:348
  31.9 0.7 %shard_map.72 = (bf16[256,256]{1,0:T(8,128)(2,1)S(1)}, bf16[256,256]{1,0:T(8,128)(2,1)S(1)}) custom-call(bf16[4,512,256]{2,1,0:T(8,128)(2,1)S(1)} %get-tuple-element.24.scaled_ref, bf16[9,64,256]{2,1,0:T(8,128)(2,1)S(1)} %get-tuple-element.33.far_ref, f32[512,256]{1,0:T(8,128)S(1)} %shard_map.71.early, bf16[256,256]{1,0:T(8,128)(2,1)S(1)} %get-tuple-element.39.grad_a, ...), custom_call_target="tpu_custom_call" | custom-call | flops 1000 | bytes 1000 | tf_op jit(solution)/shard_map/pallas_call | solution.py:348
  32.6 2.5 %collective-permute-start.11 = (bf16[256,256]{1,0:T(8,128)(2,1)S(1)}, bf16[256,256]{1,0:T(8,128)(2,1)S(1)}, u32[]{:S(2)}, u32[]{:S(2)}) collective-permute-start(bf16[256,256]{1,0:T(8,128)(2,1)S(1)} %get-tuple-element.28), channel_id=1, source_target_pairs={{0,1},{1,0},{2,3},{3,2},{4,5},{5,4},{6,7},{7,6},{8,9},{9,8},{10,11... | collective-permute-start | bytes 393224 | tf_op jit(solution)/shard_map/ppermute | solution.py:459
  35.2 1.0 %collective-permute-done.11 = bf16[256,256]{1,0:T(8,128)(2,1)S(1)} collective-permute-done((bf16[256,256]{1,0:T(8,128)(2,1)S(1)}, bf16[256,256]{1,0:T(8,128)(2,1)S(1)}, u32[]{:S(2)}, u32[]{:S(2)}) %collective-permute-start.11) | collective-permute-done | bytes 131104 | tf_op jit(solution)/shard_map/ppermute | solution.py:459
  36.2 0.8 %maximum_select_fusion = bf16[32,8,512]{2,1,0:T(8,128)(2,1)} fusion(bf16[32,8,256]{2,1,0:T(8,128)(2,1)S(1)} %bitcast.19, bf16[32,8,256]{2,1,0:T(8,128)(2,1)S(1)} %bitcast.15, pred[]{:T(512)S(6)} %eq.11), kind=kLoop, calls=%fused_computation.7 | loop fusion | flops 1179648 | bytes 524289 | tf_op jit(solution)/shard_map/jit(_where)/select_n | solution.py:462
  37.3 2.6 %collective-permute-start.13 = (bf16[9,64,256]{2,1,0:T(8,128)(2,1)S(1)}, bf16[9,64,256]{2,1,0:T(8,128)(2,1)S(1)}, u32[]{:S(2)}, u32[]{:S(2)}) collective-permute-start(bf16[9,64,256]{2,1,0:T(8,128)(2,1)S(1)} %add_convert_fusion.half_ref), channel_id=1, source_target_pairs={{0,1},{1,0},{2,3},{3,2},{4,5},{5,4},{6,7},{7,6},{8,9},{9,8},{10,11... | collective-permute-start | bytes 884744 | tf_op jit(solution)/shard_map/ppermute | solution.py:470
  39.9 0.9 %shard_map.73.refs_0_ = f32[9,64,512]{2,1,0:T(8,128)} custom-call(s32[1]{0:T(128)} %bitcast.10.core_ref, bf16[9,64,256]{2,1,0:T(8,128)(2,1)S(1)} %add_convert_fusion.half_ref), custom_call_target="tpu_custom_call" | custom-call | flops 1000 | bytes 1000 | tf_op jit(solution)/shard_map/pallas_call | solution.py:328
  41.1 0.9 %shard_map.74 = f32[9,64,512]{2,1,0:T(8,128)} custom-call(s32[1]{0:T(128)} %bitcast.10.core_ref, bf16[9,64,256]{2,1,0:T(8,128)(2,1)S(1)} %collective-permute-done.13.half_ref, f32[9,64,512]{2,1,0:T(8,128)} %shard_map.73.refs_0_), custom_call_target="tpu_custom_call", output_to_operand_aliasing={{}: (2, {})} | custom-call | flops 1000 | bytes 1000 | tf_op jit(solution)/shard_map/pallas_call | solution.py:328
  (28 shorter events, 1.7 us)
Async XLA Ops:
  0.6 1.1 %copy-start = (bf16[1,1,9,64,512]{4,3,2,1,0:T(8,128)(2,1)S(1)}, bf16[1,1,9,64,512]{4,3,2,1,0:T(8,128)(2,1)}, u32[]{:S(2)}) copy-start(bf16[1,1,9,64,512]{4,3,2,1,0:T(8,128)(2,1)} %param.9) | copy-start | bytes 1769476
  0.6 10.0 %copy-start.2 = (s32[1,32,2]{1,2,0:T(2,128)S(1)}, s32[1,32,2]{1,2,0:T(2,128)}, u32[]{:S(2)}) copy-start(s32[1,32,2]{1,2,0:T(2,128)} %param.7) | copy-start | bytes 772
  0.7 10.0 %copy-start.1 = (s32[1,32,2]{1,2,0:T(2,128)S(1)}, s32[1,32,2]{1,2,0:T(2,128)}, u32[]{:S(2)}) copy-start(s32[1,32,2]{1,2,0:T(2,128)} %param.8) | copy-start | bytes 772
  0.7 8.3 %collective-permute-start = (bf16[256,512]{1,0:T(8,128)(2,1)}, bf16[256,512]{1,0:T(8,128)(2,1)S(1)}, u32[]{:S(2)}, u32[]{:S(2)}) collective-permute-start(bf16[256,512]{1,0:T(8,128)(2,1)} %bitcast.22), channel_id=1, source_target_pairs={{8,0},{16,8},{24,16},{0,24},{9,1},{17,9},{25,17},{1,25},{10,2},{18... | collective-permute-start | bytes 786440 | tf_op jit(solution)/shard_map/ppermute | solution.py:379
  1.7 10.9 %collective-permute-start.4 = (bf16[9,64,256]{2,1,0:T(8,128)(2,1)S(1)}, bf16[9,64,256]{2,1,0:T(8,128)(2,1)S(1)}, u32[]{:S(2)}, u32[]{:S(2)}) collective-permute-start(bf16[9,64,256]{2,1,0:T(8,128)(2,1)S(1)} %dynamic-slice_bitcast_fusion.own_ref), channel_id=1, source_target_pairs={{0,2},{2,0},{4,6},{6,4},{1,3},{3,1},{5,7},{7,5},{8,10},{10,8},{12,... | collective-permute-start | bytes 884744 | tf_op jit(solution)/shard_map/ppermute | solution.py:373
  3.1 9.6 %collective-permute-start.5 = (bf16[9,64,256]{2,1,0:T(8,128)(2,1)S(1)}, bf16[9,64,256]{2,1,0:T(8,128)(2,1)S(1)}, u32[]{:S(2)}, u32[]{:S(2)}) collective-permute-start(bf16[9,64,256]{2,1,0:T(8,128)(2,1)S(1)} %dynamic-slice_bitcast_fusion.own_ref), channel_id=1, source_target_pairs={{0,1},{1,0},{2,4},{3,5},{4,2},{5,3},{6,7},{7,6},{8,9},{9,8},{10,12... | collective-permute-start | bytes 884744 | tf_op jit(solution)/shard_map/ppermute | solution.py:376
  4.1 6.7 %collective-permute-start.2 = (bf16[256,256]{1,0:T(8,128)(2,1)S(1)}, bf16[256,256]{1,0:T(8,128)(2,1)S(1)}, u32[]{:S(2)}, u32[]{:S(2)}) collective-permute-start(bf16[256,256]{1,0:T(8,128)(2,1)S(1)} %get-tuple-element.36), channel_id=1, source_target_pairs={{0,1},{1,0},{2,3},{3,2},{4,5},{5,4},{6,7},{7,6},{8,9},{9,8},{10,11... | collective-permute-start | bytes 393224 | tf_op jit(solution)/shard_map/ppermute | solution.py:388
  9.0 2.9 %collective-permute-start.1 = (bf16[256,256]{1,0:T(8,128)(2,1)S(1)}, bf16[256,256]{1,0:T(8,128)(2,1)S(1)}, u32[]{:S(2)}, u32[]{:S(2)}) collective-permute-start(bf16[256,256]{1,0:T(8,128)(2,1)S(1)} %get-tuple-element.38), channel_id=1, source_target_pairs={{0,1},{1,0},{2,3},{3,2},{4,5},{5,4},{6,7},{7,6},{8,9},{9,8},{10,11... | collective-permute-start | bytes 393224 | tf_op jit(solution)/shard_map/ppermute | solution.py:391
  10.7 1.2 %collective-permute-start.3 = (s32[4,32]{1,0:T(4,128)S(1)}, s32[4,32]{1,0:T(4,128)S(1)}, u32[]{:S(2)}, u32[]{:S(2)}) collective-permute-start(s32[4,32]{1,0:T(4,128)S(1)} %pad_add_fusion.info_a), channel_id=1, source_target_pairs={{0,1},{1,0},{2,3},{3,2},{4,5},{5,4},{6,7},{7,6},{8,9},{9,8},{10,11... | collective-permute-start | bytes 1544 | tf_op jit(solution)/shard_map/ppermute | solution.py:382
  12.7 8.5 %collective-permute-start.6 = (bf16[9,64,256]{2,1,0:T(8,128)(2,1)S(1)}, bf16[9,64,256]{2,1,0:T(8,128)(2,1)S(1)}, u32[]{:S(2)}, u32[]{:S(2)}) collective-permute-start(bf16[9,64,256]{2,1,0:T(8,128)(2,1)S(1)} %broadcast_select_fusion.3), channel_id=1, source_target_pairs={{0,2},{2,0},{4,6},{6,4},{1,3},{3,1},{5,7},{7,5},{8,10},{10,8},{12,... | collective-permute-start | bytes 884744 | tf_op jit(solution)/shard_map/ppermute | solution.py:373
  14.1 8.1 %collective-permute-start.9 = (bf16[9,64,256]{2,1,0:T(8,128)(2,1)S(1)}, bf16[9,64,256]{2,1,0:T(8,128)(2,1)S(1)}, u32[]{:S(2)}, u32[]{:S(2)}) collective-permute-start(bf16[9,64,256]{2,1,0:T(8,128)(2,1)S(1)} %collective-permute-done.4.near_ref), channel_id=1, source_target_pairs={{0,1},{1,0},{2,4},{3,5},{4,2},{5,3},{6,7},{7,6},{8,9},{9,8},{10,12... | collective-permute-start | bytes 884744 | tf_op jit(solution)/shard_map/ppermute | solution.py:376
  21.3 7.6 %collective-permute-start.7 = (bf16[9,64,256]{2,1,0:T(8,128)(2,1)S(1)}, bf16[9,64,256]{2,1,0:T(8,128)(2,1)S(1)}, u32[]{:S(2)}, u32[]{:S(2)}) collective-permute-start(bf16[9,64,256]{2,1,0:T(8,128)(2,1)S(1)} %get-tuple-element.35), channel_id=1, source_target_pairs={{0,1},{1,0},{2,4},{3,5},{4,2},{5,3},{6,7},{7,6},{8,9},{9,8},{10,12... | collective-permute-start | bytes 884744 | tf_op jit(solution)/shard_map/ppermute | solution.py:376
  22.2 7.9 %collective-permute-start.10 = (bf16[9,64,256]{2,1,0:T(8,128)(2,1)S(1)}, bf16[9,64,256]{2,1,0:T(8,128)(2,1)S(1)}, u32[]{:S(2)}, u32[]{:S(2)}) collective-permute-start(bf16[9,64,256]{2,1,0:T(8,128)(2,1)S(1)} %broadcast_select_fusion.2), channel_id=1, source_target_pairs={{0,2},{2,0},{4,6},{6,4},{1,3},{3,1},{5,7},{7,5},{8,10},{10,8},{12,... | collective-permute-start | bytes 884744 | tf_op jit(solution)/shard_map/ppermute | solution.py:373
  28.9 8.1 %collective-permute-start.8 = (bf16[9,64,256]{2,1,0:T(8,128)(2,1)S(1)}, bf16[9,64,256]{2,1,0:T(8,128)(2,1)S(1)}, u32[]{:S(2)}, u32[]{:S(2)}) collective-permute-start(bf16[9,64,256]{2,1,0:T(8,128)(2,1)S(1)} %add_select_fusion), channel_id=1, source_target_pairs={{0,2},{2,0},{4,6},{6,4},{1,3},{3,1},{5,7},{7,5},{8,10},{10,8},{12,... | collective-permute-start | bytes 884744 | tf_op jit(solution)/shard_map/ppermute | solution.py:373
  30.2 7.0 %collective-permute-start.12 = (bf16[9,64,256]{2,1,0:T(8,128)(2,1)S(1)}, bf16[9,64,256]{2,1,0:T(8,128)(2,1)S(1)}, u32[]{:S(2)}, u32[]{:S(2)}) collective-permute-start(bf16[9,64,256]{2,1,0:T(8,128)(2,1)S(1)} %get-tuple-element.32), channel_id=1, source_target_pairs={{0,1},{1,0},{2,4},{3,5},{4,2},{5,3},{6,7},{7,6},{8,9},{9,8},{10,12... | collective-permute-start | bytes 884744 | tf_op jit(solution)/shard_map/ppermute | solution.py:376
  32.6 3.5 %collective-permute-start.11 = (bf16[256,256]{1,0:T(8,128)(2,1)S(1)}, bf16[256,256]{1,0:T(8,128)(2,1)S(1)}, u32[]{:S(2)}, u32[]{:S(2)}) collective-permute-start(bf16[256,256]{1,0:T(8,128)(2,1)S(1)} %get-tuple-element.28), channel_id=1, source_target_pairs={{0,1},{1,0},{2,3},{3,2},{4,5},{5,4},{6,7},{7,6},{8,9},{9,8},{10,11... | collective-permute-start | bytes 393224 | tf_op jit(solution)/shard_map/ppermute | solution.py:459
  37.3 3.8 %collective-permute-start.13 = (bf16[9,64,256]{2,1,0:T(8,128)(2,1)S(1)}, bf16[9,64,256]{2,1,0:T(8,128)(2,1)S(1)}, u32[]{:S(2)}, u32[]{:S(2)}) collective-permute-start(bf16[9,64,256]{2,1,0:T(8,128)(2,1)S(1)} %add_convert_fusion.half_ref), channel_id=1, source_target_pairs={{0,1},{1,0},{2,3},{3,2},{4,5},{5,4},{6,7},{7,6},{8,9},{9,8},{10,11... | collective-permute-start | bytes 884744 | tf_op jit(solution)/shard_map/ppermute | solution.py:470

commit v5 on v4

--- a/solution.py
+++ b/solution.py
@@ -336,7 +336,7 @@
         ],
         input_output_aliases={} if begun is None else {2: 0},
         compiler_params=pltpu.CompilerParams(vmem_limit_bytes=VMEM_LIMIT),
-        cost_estimate=pl.CostEstimate(flops=1000, bytes_accessed=1000, transcendentals=0),
+        cost_estimate=pl.CostEstimate(flops=1000, bytes_accessed=600_000, transcendentals=0),
     )(*operands)
 
 
@@ -352,8 +352,12 @@
         out_specs=tuple(on_vmem(len(outs))),
         scratch_shapes=scratch,
         compiler_params=pltpu.CompilerParams(vmem_limit_bytes=VMEM_LIMIT),
-        cost_estimate=pl.CostEstimate(flops=1000, bytes_accessed=1000, transcendentals=0),
+        cost_estimate=pl.CostEstimate(flops=flops, bytes_accessed=1000, transcendentals=0),
     )(*operands)
+
+
+def copy_kernel(source, out):
+    out[...] = source[...]
 
 
 def weights_travel(activations, upstream, routes, gate_codes, weights):
@@ -383,6 +387,13 @@
     grad_rows = from_next(upstream[0].reshape(rows, channels))
     my_weights = half(weights[0, 0], core)
     inner_weights = across(my_weights)
+    (inner_weights,) = local_call(
+        copy_kernel,
+        (jax.ShapeDtypeStruct(inner_weights.shape, inner_weights.dtype),),
+        [],
+        20_000_000_000,
+        inner_weights,
+    )
     act_rows = activations[0].reshape(rows, channels)
     act_a = half(act_rows, core)
     act_b = lax.ppermute(half(act_rows, 1 - core), "dp", SWAP)
@@ -415,7 +426,6 @@
         600_000_000,
         grad_a, grad_b, turned, info, info_b,
     )
-    near_weights, far_part = lax.optimization_barrier((near_weights, far_part))
     cross_weights = across(near_weights)
     first_swap = near(jnp.where(inner, inner_weights, far_part))
     scaled, mid_part, near_part, own_part = local_call(

time: 42.1 us -> 42 us (level)
  waiting for transfers between devices: 18.9 us -> 17.2 us
  other arithmetic: 1.15 us -> 1.84 us
  starting transfers between devices: 12.8 us -> 13.4 us
    ppermute x1, waiting for transfers between devices: 3.9 us -> 2.39 us  [from_next(): lax.ppermute(array, 'segment', [((s + 1) % sections, s) for s in range(se...]
    ppermute x4, waiting for transfers between devices: 6.04 us -> 5.03 us  [across(): return lax.ppermute(array, ('expert', 'dp'), inner_pairs())]
    ppermute x1, waiting for transfers between devices: 0.01 us -> 0.95 us  [weights_travel(): grad_b = lax.ppermute(half(grad_rows, 1 - core), 'dp', SWAP)]
    ppermute x1, waiting for transfers between devices: 0.84 us -> 0.01 us  [weights_travel(): info_b = lax.ppermute(info, 'dp', SWAP)]
    ppermute x4, waiting for transfers between devices: 6.79 us -> 7.56 us  [near(): return lax.ppermute(array, 'expert', NEAR_PAIRS)]
    concatenate x1, other arithmetic: 0.01 us -> 0.7 us  [weights_travel(): info = jnp.concatenate([routes[0].T, gate_codes[0].T], axis=0)]
    ppermute x1, starting transfers between devices: 0.1 us -> 0.71 us  [weights_travel(): info_b = lax.ppermute(info, 'dp', SWAP)]
    pallas_call x5 -> x6, Pallas kernels: 4.86 us -> 4.88 us  [local_call(): pl.pallas_call(kernel, out_shape=tuple(outs), in_specs=on_vmem(len(operan...]
  transfers between devices with their start and end apart: 14 -> 14, of which waited for: 9 -> 10; matrix products, arithmetic and copies ran while one was open for 5% -> 7% of each run, Pallas kernels for 14% -> 14%
where the time goes in v5:
time: 42 us; the launch traced here: 41.7 us
  waiting for transfers between devices  17.2 us (41%)
  starting transfers between devices  13.4 us (32%)
  Pallas kernels  6.68 us (16%)
  other arithmetic  1.84 us (4%)
  local copies, waits for them, and re-layouts  1.78 us (4%)
  between operations  0.76 us (2%)
    ppermute x4, waiting for transfers between devices, near(): return lax.ppermute(array, 'expert', NEAR_PAIRS)  7.56 us
    ppermute x4, waiting for transfers between devices, across(): return lax.ppermute(array, ('expert', 'dp'), inner_pairs())  5.03 us
    pallas_call x6, Pallas kernels, local_call(): pl.pallas_call(kernel, out_shape=tuple(outs), in_specs=on_vmem(len(operan...  4.88 us
    ppermute x4, starting transfers between devices, near(): return lax.ppermute(array, 'expert', NEAR_PAIRS)  4.05 us
    ppermute x1, starting transfers between devices, weights_travel(): grad_back = lax.ppermute(grad_other, 'dp', SWAP)  2.56 us
    ppermute x1, starting transfers between devices, weights_travel(): kernel_other = lax.ppermute(kernel_mine, 'dp', SWAP)  2.53 us
    ppermute x1, waiting for transfers between devices, from_next(): lax.ppermute(array, 'segment', [((s + 1) % sections, s) for s in range(se...  2.39 us
    pallas_call x2, Pallas kernels, place_half(): pl.pallas_call(functools.partial(place_half_kernel, scale, side), out_sha...  1.8 us
  transfers between devices with their start and end apart: 14, of which 10 were waited for; matrix products, arithmetic and copies ran while one was open for 7% of the time, Pallas kernels for 14%

profile of v5, /device:TPU:19, one launch (start us, length us, event | category | flops | bytes accessed | tf_op | source)
XLA Modules:
  0.0 41.7 jit_solution(10153387431189887738)
XLA Ops:
  1.0 0.7 %copy-done = bf16[1,1,9,64,512]{4,3,2,1,0:T(8,128)(2,1)S(1)} copy-done((bf16[1,1,9,64,512]{4,3,2,1,0:T(8,128)(2,1)S(1)}, bf16[1,1,9,64,512]{4,3,2,1,0:T(8,128)(2,1)}, u32[]{:S(2)}) %copy-start) | copy-done | bytes 589848
  2.0 1.0 %constant_dynamic-slice_fusion = (bf16[256,256]{1,0:T(8,128)(2,1)S(1)}, bf16[256,256]{1,0:T(8,128)(2,1)S(1)}) fusion(bf16[256,512]{1,0:T(8,128)(2,1)} %bitcast.18, s32[]{:T(128)S(6)} %select_n.50, s32[]{:T(128)S(6)} %select_n.49), kind=kLoop, calls=%fused_computation.9 | loop fusion | bytes 524296 | tf_op jit(solution)/shard_map/dynamic_slice | solution.py:374
  2.9 1.0 %collective-permute-start.2 = (bf16[256,256]{1,0:T(8,128)(2,1)S(1)}, bf16[256,256]{1,0:T(8,128)(2,1)S(1)}, u32[]{:S(2)}, u32[]{:S(2)}) collective-permute-start(bf16[256,256]{1,0:T(8,128)(2,1)S(1)} %get-tuple-element.32), channel_id=1, source_target_pairs={{0,1},{1,0},{2,3},{3,2},{4,5},{5,4},{6,7},{7,6},{8,9},{9,8},{10,11... | collective-permute-start | bytes 393224 | tf_op jit(solution)/shard_map/ppermute | solution.py:399
  4.0 0.9 %collective-permute-start.8 = (bf16[9,64,256]{2,1,0:T(8,128)(2,1)S(1)}, bf16[9,64,256]{2,1,0:T(8,128)(2,1)S(1)}, u32[]{:S(2)}, u32[]{:S(2)}) collective-permute-start(bf16[9,64,256]{2,1,0:T(8,128)(2,1)S(1)} %dynamic-slice_bitcast_fusion.own_ref), channel_id=1, source_target_pairs={{0,2},{2,0},{4,6},{6,4},{1,3},{3,1},{5,7},{7,5},{8,10},{10,8},{12,... | collective-permute-start | bytes 884744 | tf_op jit(solution)/shard_map/ppermute | solution.py:377
  5.6 0.7 %collective-permute-start.3 = (s32[4,32]{1,0:T(4,128)S(1)}, s32[4,32]{1,0:T(4,128)S(1)}, u32[]{:S(2)}, u32[]{:S(2)}) collective-permute-start(s32[4,32]{1,0:T(4,128)S(1)} %pad_add_fusion.info_a), channel_id=1, source_target_pairs={{0,1},{1,0},{2,3},{3,2},{4,5},{5,4},{6,7},{7,6},{8,9},{9,8},{10,11... | collective-permute-start | bytes 1544 | tf_op jit(solution)/shard_map/ppermute | solution.py:386
  6.6 2.4 %collective-permute-done = bf16[256,512]{1,0:T(8,128)(2,1)S(1)} collective-permute-done((bf16[256,512]{1,0:T(8,128)(2,1)}, bf16[256,512]{1,0:T(8,128)(2,1)S(1)}, u32[]{:S(2)}, u32[]{:S(2)}) %collective-permute-start) | collective-permute-done | bytes 262176 | tf_op jit(solution)/shard_map/ppermute | solution.py:383
  9.0 1.6 %collective-permute-start.1 = (bf16[256,256]{1,0:T(8,128)(2,1)S(1)}, bf16[256,256]{1,0:T(8,128)(2,1)S(1)}, u32[]{:S(2)}, u32[]{:S(2)}) collective-permute-start(bf16[256,256]{1,0:T(8,128)(2,1)S(1)} %get-tuple-element.34), channel_id=1, source_target_pairs={{0,1},{1,0},{2,3},{3,2},{4,5},{5,4},{6,7},{7,6},{8,9},{9,8},{10,11... | collective-permute-start | bytes 393224 | tf_op jit(solution)/shard_map/ppermute | solution.py:402
  10.7 0.9 %collective-permute-done.1.grad_b = bf16[256,256]{1,0:T(8,128)(2,1)S(1)} collective-permute-done((bf16[256,256]{1,0:T(8,128)(2,1)S(1)}, bf16[256,256]{1,0:T(8,128)(2,1)S(1)}, u32[]{:S(2)}, u32[]{:S(2)}) %collective-permute-start.1) | collective-permute-done | bytes 131104 | tf_op jit(solution)/shard_map/ppermute | solution.py:402
  11.6 0.8 %shard_map.69 = (bf16[512,256]{1,0:T(8,128)(2,1)S(1)}, f32[64,128]{1,0:T(8,128)S(1)}, bf16[9,64,256]{2,1,0:T(8,128)(2,1)S(1)}) custom-call(bf16[256,256]{1,0:T(8,128)(2,1)S(1)} %get-tuple-element.35.grad_a, bf16[256,256]{1,0:T(8,128)(2,1)S(1)} %collective-permute-done.1.grad_b, bf16[3,256,512]{2,1,0:T(8,128)(2,1)S(1)} %shard_map.68.turned, ...), custom_call_target="tpu_custom_call" | custom-call | flops 600000000 | bytes 1000 | tf_op jit(solution)/shard_map/pallas_call | solution.py:348
  12.4 1.4 %collective-permute-start.5 = (bf16[9,64,256]{2,1,0:T(8,128)(2,1)S(1)}, bf16[9,64,256]{2,1,0:T(8,128)(2,1)S(1)}, u32[]{:S(2)}, u32[]{:S(2)}) collective-permute-start(bf16[9,64,256]{2,1,0:T(8,128)(2,1)S(1)} %broadcast_select_fusion.3), channel_id=1, source_target_pairs={{0,2},{2,0},{4,6},{6,4},{1,3},{3,1},{5,7},{7,5},{8,10},{10,8},{12,... | collective-permute-start | bytes 884744 | tf_op jit(solution)/shard_map/ppermute | solution.py:377
  13.9 1.5 %shard_map.70 = (bf16[4,512,256]{2,1,0:T(8,128)(2,1)S(1)}, bf16[9,64,256]{2,1,0:T(8,128)(2,1)S(1)}, bf16[9,64,256]{2,1,0:T(8,128)(2,1)S(1)}, f32[9,64,256]{2,1,0:T(8,128)S(1)}) custom-call(bf16[512,256]{1,0:T(8,128)(2,1)S(1)} %get-tuple-element.15.cells, f32[64,128]{1,0:T(8,128)S(1)} %get-tuple-element.16.gates, bf16[3,256,512]{2,1,0:T(8,128)(2,1)S(1)} %shard_map.68.turned), custom_call_target="tpu_custom_call" | custom-call | flops 1200000000 | bytes 1000 | tf_op jit(solution)/shard_map/pallas_call | solution.py:348
  15.4 5.4 %collective-permute-done.5 = bf16[9,64,256]{2,1,0:T(8,128)(2,1)S(1)} collective-permute-done((bf16[9,64,256]{2,1,0:T(8,128)(2,1)S(1)}, bf16[9,64,256]{2,1,0:T(8,128)(2,1)S(1)}, u32[]{:S(2)}, u32[]{:S(2)}) %collective-permute-start.5) | collective-permute-done | bytes 294944 | tf_op jit(solution)/shard_map/ppermute | solution.py:377
  21.7 1.7 %collective-permute-start.10 = (bf16[9,64,256]{2,1,0:T(8,128)(2,1)S(1)}, bf16[9,64,256]{2,1,0:T(8,128)(2,1)S(1)}, u32[]{:S(2)}, u32[]{:S(2)}) collective-permute-start(bf16[9,64,256]{2,1,0:T(8,128)(2,1)S(1)} %broadcast_select_fusion.2), channel_id=1, source_target_pairs={{0,2},{2,0},{4,6},{6,4},{1,3},{3,1},{5,7},{7,5},{8,10},{10,8},{12,... | collective-permute-start | bytes 884744 | tf_op jit(solution)/shard_map/ppermute | solution.py:377
  23.4 1.6 %shard_map.72.early = f32[512,256]{1,0:T(8,128)S(1)} custom-call(bf16[4,512,256]{2,1,0:T(8,128)(2,1)S(1)} %get-tuple-element.21.scaled_ref, bf16[9,64,256]{2,1,0:T(8,128)(2,1)S(1)} %dynamic-slice_bitcast_fusion.own_ref, bf16[9,64,256]{2,1,0:T(8,128)(2,1)S(1)} %collective-permute-done.8.near_ref, bf16[9,64,256]{2,1,0:T(8,128)(2,1)S(1)} %get-tuple-element.30.mid_ref), custom_call_target="tpu_custom_call" | custom-call | flops 1200000000 | bytes 1000 | tf_op jit(solution)/shard_map/pallas_call | solution.py:348
  25.0 3.1 %collective-permute-done.6 = bf16[9,64,256]{2,1,0:T(8,128)(2,1)S(1)} collective-permute-done((bf16[9,64,256]{2,1,0:T(8,128)(2,1)S(1)}, bf16[9,64,256]{2,1,0:T(8,128)(2,1)S(1)}, u32[]{:S(2)}, u32[]{:S(2)}) %collective-permute-start.6) | collective-permute-done | bytes 294944 | tf_op jit(solution)/shard_map/ppermute | solution.py:380
  28.3 1.6 %collective-permute-done.10 = bf16[9,64,256]{2,1,0:T(8,128)(2,1)S(1)} collective-permute-done((bf16[9,64,256]{2,1,0:T(8,128)(2,1)S(1)}, bf16[9,64,256]{2,1,0:T(8,128)(2,1)S(1)}, u32[]{:S(2)}, u32[]{:S(2)}) %collective-permute-start.10) | collective-permute-done | bytes 294944 | tf_op jit(solution)/shard_map/ppermute | solution.py:377
  30.0 0.7 %shard_map.73 = (bf16[256,256]{1,0:T(8,128)(2,1)S(1)}, bf16[256,256]{1,0:T(8,128)(2,1)S(1)}) custom-call(bf16[4,512,256]{2,1,0:T(8,128)(2,1)S(1)} %get-tuple-element.21.scaled_ref, bf16[9,64,256]{2,1,0:T(8,128)(2,1)S(1)} %get-tuple-element.29.far_ref, f32[512,256]{1,0:T(8,128)S(1)} %shard_map.72.early, bf16[256,256]{1,0:T(8,128)(2,1)S(1)} %get-tuple-element.35.grad_a, ...), custom_call_target="tpu_custom_call" | custom-call | flops 500000000 | bytes 1000 | tf_op jit(solution)/shard_map/pallas_call | solution.py:348
  30.7 2.6 %collective-permute-start.11 = (bf16[256,256]{1,0:T(8,128)(2,1)S(1)}, bf16[256,256]{1,0:T(8,128)(2,1)S(1)}, u32[]{:S(2)}, u32[]{:S(2)}) collective-permute-start(bf16[256,256]{1,0:T(8,128)(2,1)S(1)} %get-tuple-element.24), channel_id=1, source_target_pairs={{0,1},{1,0},{2,3},{3,2},{4,5},{5,4},{6,7},{7,6},{8,9},{9,8},{10,11... | collective-permute-start | bytes 393224 | tf_op jit(solution)/shard_map/ppermute | solution.py:469
  33.3 1.0 %collective-permute-done.11 = bf16[256,256]{1,0:T(8,128)(2,1)S(1)} collective-permute-done((bf16[256,256]{1,0:T(8,128)(2,1)S(1)}, bf16[256,256]{1,0:T(8,128)(2,1)S(1)}, u32[]{:S(2)}, u32[]{:S(2)}) %collective-permute-start.11) | collective-permute-done | bytes 131104 | tf_op jit(solution)/shard_map/ppermute | solution.py:469
  34.3 0.8 %maximum_select_fusion = bf16[32,8,512]{2,1,0:T(8,128)(2,1)} fusion(bf16[32,8,256]{2,1,0:T(8,128)(2,1)S(1)} %bitcast.19, bf16[32,8,256]{2,1,0:T(8,128)(2,1)S(1)} %bitcast.15, pred[]{:T(512)S(6)} %eq.11), kind=kLoop, calls=%fused_computation.7 | loop fusion | flops 1179648 | bytes 524289 | tf_op jit(solution)/shard_map/jit(_where)/select_n | solution.py:472
  35.7 1.2 %collective-permute-done.12 = bf16[9,64,256]{2,1,0:T(8,128)(2,1)S(1)} collective-permute-done((bf16[9,64,256]{2,1,0:T(8,128)(2,1)S(1)}, bf16[9,64,256]{2,1,0:T(8,128)(2,1)S(1)}, u32[]{:S(2)}, u32[]{:S(2)}) %collective-permute-start.12) | collective-permute-done | bytes 294944 | tf_op jit(solution)/shard_map/ppermute | solution.py:380
  37.0 2.5 %collective-permute-start.13 = (bf16[9,64,256]{2,1,0:T(8,128)(2,1)S(1)}, bf16[9,64,256]{2,1,0:T(8,128)(2,1)S(1)}, u32[]{:S(2)}, u32[]{:S(2)}) collective-permute-start(bf16[9,64,256]{2,1,0:T(8,128)(2,1)S(1)} %add_convert_fusion.half_ref), channel_id=1, source_target_pairs={{0,1},{1,0},{2,3},{3,2},{4,5},{5,4},{6,7},{7,6},{8,9},{9,8},{10,11... | collective-permute-start | bytes 884744 | tf_op jit(solution)/shard_map/ppermute | solution.py:480
  39.6 0.9 %shard_map.74.refs_0_ = f32[9,64,512]{2,1,0:T(8,128)} custom-call(s32[1]{0:T(128)} %bitcast.10.core_ref, bf16[9,64,256]{2,1,0:T(8,128)(2,1)S(1)} %add_convert_fusion.half_ref), custom_call_target="tpu_custom_call" | custom-call | flops 1000 | bytes 600000 | tf_op jit(solution)/shard_map/pallas_call | solution.py:328
  40.8 0.9 %shard_map.75 = f32[9,64,512]{2,1,0:T(8,128)} custom-call(s32[1]{0:T(128)} %bitcast.10.core_ref, bf16[9,64,256]{2,1,0:T(8,128)(2,1)S(1)} %collective-permute-done.13.half_ref, f32[9,64,512]{2,1,0:T(8,128)} %shard_map.74.refs_0_), custom_call_target="tpu_custom_call", output_to_operand_aliasing={{}: (2, {})} | custom-call | flops 1000 | bytes 600000 | tf_op jit(solution)/shard_map/pallas_call | solution.py:328
  (25 shorter events, 4.0 us)
Async XLA Ops:
  0.6 1.1 %copy-start = (bf16[1,1,9,64,512]{4,3,2,1,0:T(8,128)(2,1)S(1)}, bf16[1,1,9,64,512]{4,3,2,1,0:T(8,128)(2,1)}, u32[]{:S(2)}) copy-start(bf16[1,1,9,64,512]{4,3,2,1,0:T(8,128)(2,1)} %param.9) | copy-start | bytes 1769476
  0.6 8.3 %collective-permute-start = (bf16[256,512]{1,0:T(8,128)(2,1)}, bf16[256,512]{1,0:T(8,128)(2,1)S(1)}, u32[]{:S(2)}, u32[]{:S(2)}) collective-permute-start(bf16[256,512]{1,0:T(8,128)(2,1)} %bitcast.22), channel_id=1, source_target_pairs={{8,0},{16,8},{24,16},{0,24},{9,1},{17,9},{25,17},{1,25},{10,2},{18... | collective-permute-start | bytes 786440 | tf_op jit(solution)/shard_map/ppermute | solution.py:383
  1.7 8.9 %collective-permute-start.4 = (bf16[9,64,256]{2,1,0:T(8,128)(2,1)S(1)}, bf16[9,64,256]{2,1,0:T(8,128)(2,1)S(1)}, u32[]{:S(2)}, u32[]{:S(2)}) collective-permute-start(bf16[9,64,256]{2,1,0:T(8,128)(2,1)S(1)} %dynamic-slice_bitcast_fusion.own_ref), channel_id=1, source_target_pairs={{0,1},{1,0},{2,4},{3,5},{4,2},{5,3},{6,7},{7,6},{8,9},{9,8},{10,12... | collective-permute-start | bytes 884744 | tf_op jit(solution)/shard_map/ppermute | solution.py:380
  2.9 3.4 %collective-permute-start.2 = (bf16[256,256]{1,0:T(8,128)(2,1)S(1)}, bf16[256,256]{1,0:T(8,128)(2,1)S(1)}, u32[]{:S(2)}, u32[]{:S(2)}) collective-permute-start(bf16[256,256]{1,0:T(8,128)(2,1)S(1)} %get-tuple-element.32), channel_id=1, source_target_pairs={{0,1},{1,0},{2,3},{3,2},{4,5},{5,4},{6,7},{7,6},{8,9},{9,8},{10,11... | collective-permute-start | bytes 393224 | tf_op jit(solution)/shard_map/ppermute | solution.py:399
  4.0 9.8 %collective-permute-start.8 = (bf16[9,64,256]{2,1,0:T(8,128)(2,1)S(1)}, bf16[9,64,256]{2,1,0:T(8,128)(2,1)S(1)}, u32[]{:S(2)}, u32[]{:S(2)}) collective-permute-start(bf16[9,64,256]{2,1,0:T(8,128)(2,1)S(1)} %dynamic-slice_bitcast_fusion.own_ref), channel_id=1, source_target_pairs={{0,2},{2,0},{4,6},{6,4},{1,3},{3,1},{5,7},{7,5},{8,10},{10,8},{12,... | collective-permute-start | bytes 884744 | tf_op jit(solution)/shard_map/ppermute | solution.py:377
  5.6 5.0 %collective-permute-start.3 = (s32[4,32]{1,0:T(4,128)S(1)}, s32[4,32]{1,0:T(4,128)S(1)}, u32[]{:S(2)}, u32[]{:S(2)}) collective-permute-start(s32[4,32]{1,0:T(4,128)S(1)} %pad_add_fusion.info_a), channel_id=1, source_target_pairs={{0,1},{1,0},{2,3},{3,2},{4,5},{5,4},{6,7},{7,6},{8,9},{9,8},{10,11... | collective-permute-start | bytes 1544 | tf_op jit(solution)/shard_map/ppermute | solution.py:386
  9.0 2.6 %collective-permute-start.1 = (bf16[256,256]{1,0:T(8,128)(2,1)S(1)}, bf16[256,256]{1,0:T(8,128)(2,1)S(1)}, u32[]{:S(2)}, u32[]{:S(2)}) collective-permute-start(bf16[256,256]{1,0:T(8,128)(2,1)S(1)} %get-tuple-element.34), channel_id=1, source_target_pairs={{0,1},{1,0},{2,3},{3,2},{4,5},{5,4},{6,7},{7,6},{8,9},{9,8},{10,11... | collective-permute-start | bytes 393224 | tf_op jit(solution)/shard_map/ppermute | solution.py:402
  12.4 8.3 %collective-permute-start.5 = (bf16[9,64,256]{2,1,0:T(8,128)(2,1)S(1)}, bf16[9,64,256]{2,1,0:T(8,128)(2,1)S(1)}, u32[]{:S(2)}, u32[]{:S(2)}) collective-permute-start(bf16[9,64,256]{2,1,0:T(8,128)(2,1)S(1)} %broadcast_select_fusion.3), channel_id=1, source_target_pairs={{0,2},{2,0},{4,6},{6,4},{1,3},{3,1},{5,7},{7,5},{8,10},{10,8},{12,... | collective-permute-start | bytes 884744 | tf_op jit(solution)/shard_map/ppermute | solution.py:377
  13.8 7.9 %collective-permute-start.9 = (bf16[9,64,256]{2,1,0:T(8,128)(2,1)S(1)}, bf16[9,64,256]{2,1,0:T(8,128)(2,1)S(1)}, u32[]{:S(2)}, u32[]{:S(2)}) collective-permute-start(bf16[9,64,256]{2,1,0:T(8,128)(2,1)S(1)} %collective-permute-done.8.near_ref), channel_id=1, source_target_pairs={{0,1},{1,0},{2,4},{3,5},{4,2},{5,3},{6,7},{7,6},{8,9},{9,8},{10,12... | collective-permute-start | bytes 884744 | tf_op jit(solution)/shard_map/ppermute | solution.py:380
  20.8 7.4 %collective-permute-start.6 = (bf16[9,64,256]{2,1,0:T(8,128)(2,1)S(1)}, bf16[9,64,256]{2,1,0:T(8,128)(2,1)S(1)}, u32[]{:S(2)}, u32[]{:S(2)}) collective-permute-start(bf16[9,64,256]{2,1,0:T(8,128)(2,1)S(1)} %get-tuple-element.31), channel_id=1, source_target_pairs={{0,1},{1,0},{2,4},{3,5},{4,2},{5,3},{6,7},{7,6},{8,9},{9,8},{10,12... | collective-permute-start | bytes 884744 | tf_op jit(solution)/shard_map/ppermute | solution.py:380
  21.7 8.1 %collective-permute-start.10 = (bf16[9,64,256]{2,1,0:T(8,128)(2,1)S(1)}, bf16[9,64,256]{2,1,0:T(8,128)(2,1)S(1)}, u32[]{:S(2)}, u32[]{:S(2)}) collective-permute-start(bf16[9,64,256]{2,1,0:T(8,128)(2,1)S(1)} %broadcast_select_fusion.2), channel_id=1, source_target_pairs={{0,2},{2,0},{4,6},{6,4},{1,3},{3,1},{5,7},{7,5},{8,10},{10,8},{12,... | collective-permute-start | bytes 884744 | tf_op jit(solution)/shard_map/ppermute | solution.py:377
  28.2 7.5 %collective-permute-start.7 = (bf16[9,64,256]{2,1,0:T(8,128)(2,1)S(1)}, bf16[9,64,256]{2,1,0:T(8,128)(2,1)S(1)}, u32[]{:S(2)}, u32[]{:S(2)}) collective-permute-start(bf16[9,64,256]{2,1,0:T(8,128)(2,1)S(1)} %add_select_fusion), channel_id=1, source_target_pairs={{0,2},{2,0},{4,6},{6,4},{1,3},{3,1},{5,7},{7,5},{8,10},{10,8},{12,... | collective-permute-start | bytes 884744 | tf_op jit(solution)/shard_map/ppermute | solution.py:377
  29.9 7.0 %collective-permute-start.12 = (bf16[9,64,256]{2,1,0:T(8,128)(2,1)S(1)}, bf16[9,64,256]{2,1,0:T(8,128)(2,1)S(1)}, u32[]{:S(2)}, u32[]{:S(2)}) collective-permute-start(bf16[9,64,256]{2,1,0:T(8,128)(2,1)S(1)} %get-tuple-element.28), channel_id=1, source_target_pairs={{0,1},{1,0},{2,4},{3,5},{4,2},{5,3},{6,7},{7,6},{8,9},{9,8},{10,12... | collective-permute-start | bytes 884744 | tf_op jit(solution)/shard_map/ppermute | solution.py:380
  30.7 3.5 %collective-permute-start.11 = (bf16[256,256]{1,0:T(8,128)(2,1)S(1)}, bf16[256,256]{1,0:T(8,128)(2,1)S(1)}, u32[]{:S(2)}, u32[]{:S(2)}) collective-permute-start(bf16[256,256]{1,0:T(8,128)(2,1)S(1)} %get-tuple-element.24), channel_id=1, source_target_pairs={{0,1},{1,0},{2,3},{3,2},{4,5},{5,4},{6,7},{7,6},{8,9},{9,8},{10,11... | collective-permute-start | bytes 393224 | tf_op jit(solution)/shard_map/ppermute | solution.py:469
  37.0 3.7 %collective-permute-start.13 = (bf16[9,64,256]{2,1,0:T(8,128)(2,1)S(1)}, bf16[9,64,256]{2,1,0:T(8,128)(2,1)S(1)}, u32[]{:S(2)}, u32[]{:S(2)}) collective-permute-start(bf16[9,64,256]{2,1,0:T(8,128)(2,1)S(1)} %add_convert_fusion.half_ref), channel_id=1, source_target_pairs={{0,1},{1,0},{2,3},{3,2},{4,5},{5,4},{6,7},{7,6},{8,9},{9,8},{10,11... | collective-permute-start | bytes 884744 | tf_op jit(solution)/shard_map/ppermute | solution.py:480

commit v6 on v5

--- a/solution.py
+++ b/solution.py
@@ -282,17 +282,17 @@
                     )
 
 
-def early_answer_kernel(scaled_ref, own_ref, near_ref, mid_ref, total):
+def early_answer_kernel(scaled_ref, own_ref, near_ref, total):
     total[...] = jnp.zeros_like(total)
-    add_answers(scaled_ref, (0, 1, 2), (own_ref, near_ref, mid_ref), total)
-
-
-def late_answer_kernel(scaled_ref, far_ref, early, grad_a, grad_b, out_a, out_b, total, spread):
+    add_answers(scaled_ref, (0, 1), (own_ref, near_ref), total)
+
+
+def late_answer_kernel(scaled_ref, mid_ref, far_ref, early, grad_a, grad_b, out_a, out_b, total, spread):
     tiles = grad_a.shape[0] // (TH * TW)
     block = 2 * tiles
     strips = grad_a.shape[1] // 128
     total[...] = early[...]
-    add_answers(scaled_ref, (3,), (far_ref,), total)
+    add_answers(scaled_ref, (2, 3), (mid_ref, far_ref), total)
     for at, (grad, out) in enumerate(((grad_a, out_a), (grad_b, out_b))):
         for strip in range(strips):
             lanes = pl.ds(strip * 128, 128)
@@ -453,7 +453,7 @@
         (jax.ShapeDtypeStruct((2 * rows, width), jnp.float32),),
         [],
         1_200_000_000,
-        scaled, my_weights, near_weights, mid_weights,
+        scaled, my_weights, near_weights,
     )
     answer = jax.ShapeDtypeStruct((rows, width), jnp.bfloat16)
     grad_own, grad_other = local_call(
@@ -464,7 +464,7 @@
             pltpu.VMEM((width // 128, rows, 128), jnp.float32),
         ],
         500_000_000,
-        scaled, far_weights, early, grad_a, grad_b,
+        scaled, mid_weights, far_weights, early, grad_a, grad_b,
     )
     grad_back = lax.ppermute(grad_other, "dp", SWAP)
 

time: 42 us -> 42 us (level)
    ppermute x4, waiting for transfers between devices: 7.56 us -> 7.09 us  [near(): return lax.ppermute(array, 'expert', NEAR_PAIRS)]
    ppermute x4, waiting for transfers between devices: 5.03 us -> 5.51 us  [across(): return lax.ppermute(array, ('expert', 'dp'), inner_pairs())]
where the time goes in v6:
time: 42 us; the launch traced here: 41.7 us
  waiting for transfers between devices  17.2 us (41%)
  starting transfers between devices  13.4 us (32%)
  Pallas kernels  6.68 us (16%)
  other arithmetic  1.84 us (4%)
  local copies, waits for them, and re-layouts  1.78 us (4%)
  between operations  0.76 us (2%)
    ppermute x4, waiting for transfers between devices, near(): return lax.ppermute(array, 'expert', NEAR_PAIRS)  7.09 us
    ppermute x4, waiting for transfers between devices, across(): return lax.ppermute(array, ('expert', 'dp'), inner_pairs())  5.51 us
    pallas_call x6, Pallas kernels, local_call(): pl.pallas_call(kernel, out_shape=tuple(outs), in_specs=on_vmem(len(operan...  4.88 us
    ppermute x4, starting transfers between devices, near(): return lax.ppermute(array, 'expert', NEAR_PAIRS)  4.05 us
    ppermute x1, starting transfers between devices, weights_travel(): grad_back = lax.ppermute(grad_other, 'dp', SWAP)  2.56 us
    ppermute x1, starting transfers between devices, weights_travel(): kernel_other = lax.ppermute(kernel_mine, 'dp', SWAP)  2.53 us
    ppermute x1, waiting for transfers between devices, from_next(): lax.ppermute(array, 'segment', [((s + 1) % sections, s) for s in range(se...  2.39 us
    pallas_call x2, Pallas kernels, place_half(): pl.pallas_call(functools.partial(place_half_kernel, scale, side), out_sha...  1.8 us
  transfers between devices with their start and end apart: 14, of which 10 were waited for; matrix products, arithmetic and copies ran while one was open for 7% of the time, Pallas kernels for 14%

profile of v6, /device:TPU:19, one launch (start us, length us, event | category | flops | bytes accessed | tf_op | source)
XLA Modules:
  0.0 41.7 jit_solution(14117906670026423937)
XLA Ops:
  1.0 0.7 %copy-done = bf16[1,1,9,64,512]{4,3,2,1,0:T(8,128)(2,1)S(1)} copy-done((bf16[1,1,9,64,512]{4,3,2,1,0:T(8,128)(2,1)S(1)}, bf16[1,1,9,64,512]{4,3,2,1,0:T(8,128)(2,1)}, u32[]{:S(2)}) %copy-start) | copy-done | bytes 589848
  2.0 1.0 %constant_dynamic-slice_fusion = (bf16[256,256]{1,0:T(8,128)(2,1)S(1)}, bf16[256,256]{1,0:T(8,128)(2,1)S(1)}) fusion(bf16[256,512]{1,0:T(8,128)(2,1)} %bitcast.18, s32[]{:T(128)S(6)} %select_n.50, s32[]{:T(128)S(6)} %select_n.49), kind=kLoop, calls=%fused_computation.9 | loop fusion | bytes 524296 | tf_op jit(solution)/shard_map/dynamic_slice | solution.py:374
  2.9 1.0 %collective-permute-start.2 = (bf16[256,256]{1,0:T(8,128)(2,1)S(1)}, bf16[256,256]{1,0:T(8,128)(2,1)S(1)}, u32[]{:S(2)}, u32[]{:S(2)}) collective-permute-start(bf16[256,256]{1,0:T(8,128)(2,1)S(1)} %get-tuple-element.32), channel_id=1, source_target_pairs={{0,1},{1,0},{2,3},{3,2},{4,5},{5,4},{6,7},{7,6},{8,9},{9,8},{10,11... | collective-permute-start | bytes 393224 | tf_op jit(solution)/shard_map/ppermute | solution.py:399
  4.0 0.9 %collective-permute-start.8 = (bf16[9,64,256]{2,1,0:T(8,128)(2,1)S(1)}, bf16[9,64,256]{2,1,0:T(8,128)(2,1)S(1)}, u32[]{:S(2)}, u32[]{:S(2)}) collective-permute-start(bf16[9,64,256]{2,1,0:T(8,128)(2,1)S(1)} %dynamic-slice_bitcast_fusion.own_ref), channel_id=1, source_target_pairs={{0,2},{2,0},{4,6},{6,4},{1,3},{3,1},{5,7},{7,5},{8,10},{10,8},{12,... | collective-permute-start | bytes 884744 | tf_op jit(solution)/shard_map/ppermute | solution.py:377
  5.6 0.7 %collective-permute-start.3 = (s32[4,32]{1,0:T(4,128)S(1)}, s32[4,32]{1,0:T(4,128)S(1)}, u32[]{:S(2)}, u32[]{:S(2)}) collective-permute-start(s32[4,32]{1,0:T(4,128)S(1)} %pad_add_fusion.info_a), channel_id=1, source_target_pairs={{0,1},{1,0},{2,3},{3,2},{4,5},{5,4},{6,7},{7,6},{8,9},{9,8},{10,11... | collective-permute-start | bytes 1544 | tf_op jit(solution)/shard_map/ppermute | solution.py:386
  6.6 2.4 %collective-permute-done = bf16[256,512]{1,0:T(8,128)(2,1)S(1)} collective-permute-done((bf16[256,512]{1,0:T(8,128)(2,1)}, bf16[256,512]{1,0:T(8,128)(2,1)S(1)}, u32[]{:S(2)}, u32[]{:S(2)}) %collective-permute-start) | collective-permute-done | bytes 262176 | tf_op jit(solution)/shard_map/ppermute | solution.py:383
  9.0 1.6 %collective-permute-start.1 = (bf16[256,256]{1,0:T(8,128)(2,1)S(1)}, bf16[256,256]{1,0:T(8,128)(2,1)S(1)}, u32[]{:S(2)}, u32[]{:S(2)}) collective-permute-start(bf16[256,256]{1,0:T(8,128)(2,1)S(1)} %get-tuple-element.34), channel_id=1, source_target_pairs={{0,1},{1,0},{2,3},{3,2},{4,5},{5,4},{6,7},{7,6},{8,9},{9,8},{10,11... | collective-permute-start | bytes 393224 | tf_op jit(solution)/shard_map/ppermute | solution.py:402
  10.7 0.9 %collective-permute-done.1.grad_b = bf16[256,256]{1,0:T(8,128)(2,1)S(1)} collective-permute-done((bf16[256,256]{1,0:T(8,128)(2,1)S(1)}, bf16[256,256]{1,0:T(8,128)(2,1)S(1)}, u32[]{:S(2)}, u32[]{:S(2)}) %collective-permute-start.1) | collective-permute-done | bytes 131104 | tf_op jit(solution)/shard_map/ppermute | solution.py:402
  11.6 0.8 %shard_map.69 = (bf16[512,256]{1,0:T(8,128)(2,1)S(1)}, f32[64,128]{1,0:T(8,128)S(1)}, bf16[9,64,256]{2,1,0:T(8,128)(2,1)S(1)}) custom-call(bf16[256,256]{1,0:T(8,128)(2,1)S(1)} %get-tuple-element.35.grad_a, bf16[256,256]{1,0:T(8,128)(2,1)S(1)} %collective-permute-done.1.grad_b, bf16[3,256,512]{2,1,0:T(8,128)(2,1)S(1)} %shard_map.68.turned, ...), custom_call_target="tpu_custom_call" | custom-call | flops 600000000 | bytes 1000 | tf_op jit(solution)/shard_map/pallas_call | solution.py:348
  12.4 1.4 %collective-permute-start.5 = (bf16[9,64,256]{2,1,0:T(8,128)(2,1)S(1)}, bf16[9,64,256]{2,1,0:T(8,128)(2,1)S(1)}, u32[]{:S(2)}, u32[]{:S(2)}) collective-permute-start(bf16[9,64,256]{2,1,0:T(8,128)(2,1)S(1)} %broadcast_select_fusion.3), channel_id=1, source_target_pairs={{0,2},{2,0},{4,6},{6,4},{1,3},{3,1},{5,7},{7,5},{8,10},{10,8},{12,... | collective-permute-start | bytes 884744 | tf_op jit(solution)/shard_map/ppermute | solution.py:377
  13.9 1.5 %shard_map.70 = (bf16[4,512,256]{2,1,0:T(8,128)(2,1)S(1)}, bf16[9,64,256]{2,1,0:T(8,128)(2,1)S(1)}, bf16[9,64,256]{2,1,0:T(8,128)(2,1)S(1)}, f32[9,64,256]{2,1,0:T(8,128)S(1)}) custom-call(bf16[512,256]{1,0:T(8,128)(2,1)S(1)} %get-tuple-element.15.cells, f32[64,128]{1,0:T(8,128)S(1)} %get-tuple-element.16.gates, bf16[3,256,512]{2,1,0:T(8,128)(2,1)S(1)} %shard_map.68.turned), custom_call_target="tpu_custom_call" | custom-call | flops 1200000000 | bytes 1000 | tf_op jit(solution)/shard_map/pallas_call | solution.py:348
  15.4 5.4 %collective-permute-done.5 = bf16[9,64,256]{2,1,0:T(8,128)(2,1)S(1)} collective-permute-done((bf16[9,64,256]{2,1,0:T(8,128)(2,1)S(1)}, bf16[9,64,256]{2,1,0:T(8,128)(2,1)S(1)}, u32[]{:S(2)}, u32[]{:S(2)}) %collective-permute-start.5) | collective-permute-done | bytes 294944 | tf_op jit(solution)/shard_map/ppermute | solution.py:377
  21.7 1.7 %collective-permute-start.10 = (bf16[9,64,256]{2,1,0:T(8,128)(2,1)S(1)}, bf16[9,64,256]{2,1,0:T(8,128)(2,1)S(1)}, u32[]{:S(2)}, u32[]{:S(2)}) collective-permute-start(bf16[9,64,256]{2,1,0:T(8,128)(2,1)S(1)} %broadcast_select_fusion.1), channel_id=1, source_target_pairs={{0,2},{2,0},{4,6},{6,4},{1,3},{3,1},{5,7},{7,5},{8,10},{10,8},{12,... | collective-permute-start | bytes 884744 | tf_op jit(solution)/shard_map/ppermute | solution.py:377
  23.4 1.1 %shard_map.72.early = f32[512,256]{1,0:T(8,128)S(1)} custom-call(bf16[4,512,256]{2,1,0:T(8,128)(2,1)S(1)} %get-tuple-element.21.scaled_ref, bf16[9,64,256]{2,1,0:T(8,128)(2,1)S(1)} %dynamic-slice_bitcast_fusion.own_ref, bf16[9,64,256]{2,1,0:T(8,128)(2,1)S(1)} %collective-permute-done.8.near_ref), custom_call_target="tpu_custom_call" | custom-call | flops 1200000000 | bytes 1000 | tf_op jit(solution)/shard_map/pallas_call | solution.py:348
  24.5 3.6 %collective-permute-done.6 = bf16[9,64,256]{2,1,0:T(8,128)(2,1)S(1)} collective-permute-done((bf16[9,64,256]{2,1,0:T(8,128)(2,1)S(1)}, bf16[9,64,256]{2,1,0:T(8,128)(2,1)S(1)}, u32[]{:S(2)}, u32[]{:S(2)}) %collective-permute-start.6) | collective-permute-done | bytes 294944 | tf_op jit(solution)/shard_map/ppermute | solution.py:380
  28.3 1.6 %collective-permute-done.10 = bf16[9,64,256]{2,1,0:T(8,128)(2,1)S(1)} collective-permute-done((bf16[9,64,256]{2,1,0:T(8,128)(2,1)S(1)}, bf16[9,64,256]{2,1,0:T(8,128)(2,1)S(1)}, u32[]{:S(2)}, u32[]{:S(2)}) %collective-permute-start.10) | collective-permute-done | bytes 294944 | tf_op jit(solution)/shard_map/ppermute | solution.py:377
  30.0 1.2 %shard_map.73 = (bf16[256,256]{1,0:T(8,128)(2,1)S(1)}, bf16[256,256]{1,0:T(8,128)(2,1)S(1)}) custom-call(bf16[4,512,256]{2,1,0:T(8,128)(2,1)S(1)} %get-tuple-element.21.scaled_ref, bf16[9,64,256]{2,1,0:T(8,128)(2,1)S(1)} %get-tuple-element.30.mid_ref, bf16[9,64,256]{2,1,0:T(8,128)(2,1)S(1)} %get-tuple-element.29.far_ref, f32[512,256]{1,0:T(8,128)S(1)} %shard_map.72.early, ...), custom_call_target="tpu_custom_call" | custom-call | flops 500000000 | bytes 1000 | tf_op jit(solution)/shard_map/pallas_call | solution.py:348
  31.2 2.6 %collective-permute-start.11 = (bf16[256,256]{1,0:T(8,128)(2,1)S(1)}, bf16[256,256]{1,0:T(8,128)(2,1)S(1)}, u32[]{:S(2)}, u32[]{:S(2)}) collective-permute-start(bf16[256,256]{1,0:T(8,128)(2,1)S(1)} %get-tuple-element.24), channel_id=1, source_target_pairs={{0,1},{1,0},{2,3},{3,2},{4,5},{5,4},{6,7},{7,6},{8,9},{9,8},{10,11... | collective-permute-start | bytes 393224 | tf_op jit(solution)/shard_map/ppermute | solution.py:469
  33.8 1.0 %collective-permute-done.11 = bf16[256,256]{1,0:T(8,128)(2,1)S(1)} collective-permute-done((bf16[256,256]{1,0:T(8,128)(2,1)S(1)}, bf16[256,256]{1,0:T(8,128)(2,1)S(1)}, u32[]{:S(2)}, u32[]{:S(2)}) %collective-permute-start.11) | collective-permute-done | bytes 131104 | tf_op jit(solution)/shard_map/ppermute | solution.py:469
  34.7 0.8 %maximum_select_fusion = bf16[32,8,512]{2,1,0:T(8,128)(2,1)} fusion(bf16[32,8,256]{2,1,0:T(8,128)(2,1)S(1)} %bitcast.19, bf16[32,8,256]{2,1,0:T(8,128)(2,1)S(1)} %bitcast.15, pred[]{:T(512)S(6)} %eq.11), kind=kLoop, calls=%fused_computation.7 | loop fusion | flops 1179648 | bytes 524289 | tf_op jit(solution)/shard_map/jit(_where)/select_n | solution.py:472
  35.7 1.2 %collective-permute-done.12 = bf16[9,64,256]{2,1,0:T(8,128)(2,1)S(1)} collective-permute-done((bf16[9,64,256]{2,1,0:T(8,128)(2,1)S(1)}, bf16[9,64,256]{2,1,0:T(8,128)(2,1)S(1)}, u32[]{:S(2)}, u32[]{:S(2)}) %collective-permute-start.12) | collective-permute-done | bytes 294944 | tf_op jit(solution)/shard_map/ppermute | solution.py:380
  37.0 2.5 %collective-permute-start.13 = (bf16[9,64,256]{2,1,0:T(8,128)(2,1)S(1)}, bf16[9,64,256]{2,1,0:T(8,128)(2,1)S(1)}, u32[]{:S(2)}, u32[]{:S(2)}) collective-permute-start(bf16[9,64,256]{2,1,0:T(8,128)(2,1)S(1)} %add_convert_fusion.half_ref), channel_id=1, source_target_pairs={{0,1},{1,0},{2,3},{3,2},{4,5},{5,4},{6,7},{7,6},{8,9},{9,8},{10,11... | collective-permute-start | bytes 884744 | tf_op jit(solution)/shard_map/ppermute | solution.py:480
  39.6 0.9 %shard_map.74.refs_0_ = f32[9,64,512]{2,1,0:T(8,128)} custom-call(s32[1]{0:T(128)} %bitcast.10.core_ref, bf16[9,64,256]{2,1,0:T(8,128)(2,1)S(1)} %add_convert_fusion.half_ref), custom_call_target="tpu_custom_call" | custom-call | flops 1000 | bytes 600000 | tf_op jit(solution)/shard_map/pallas_call | solution.py:328
  40.8 0.9 %shard_map.75 = f32[9,64,512]{2,1,0:T(8,128)} custom-call(s32[1]{0:T(128)} %bitcast.10.core_ref, bf16[9,64,256]{2,1,0:T(8,128)(2,1)S(1)} %collective-permute-done.13.half_ref, f32[9,64,512]{2,1,0:T(8,128)} %shard_map.74.refs_0_), custom_call_target="tpu_custom_call", output_to_operand_aliasing={{}: (2, {})} | custom-call | flops 1000 | bytes 600000 | tf_op jit(solution)/shard_map/pallas_call | solution.py:328
  (25 shorter events, 3.5 us)
Async XLA Ops:
  0.6 1.1 %copy-start = (bf16[1,1,9,64,512]{4,3,2,1,0:T(8,128)(2,1)S(1)}, bf16[1,1,9,64,512]{4,3,2,1,0:T(8,128)(2,1)}, u32[]{:S(2)}) copy-start(bf16[1,1,9,64,512]{4,3,2,1,0:T(8,128)(2,1)} %param.9) | copy-start | bytes 1769476
  0.6 8.3 %collective-permute-start = (bf16[256,512]{1,0:T(8,128)(2,1)}, bf16[256,512]{1,0:T(8,128)(2,1)S(1)}, u32[]{:S(2)}, u32[]{:S(2)}) collective-permute-start(bf16[256,512]{1,0:T(8,128)(2,1)} %bitcast.22), channel_id=1, source_target_pairs={{8,0},{16,8},{24,16},{0,24},{9,1},{17,9},{25,17},{1,25},{10,2},{18... | collective-permute-start | bytes 786440 | tf_op jit(solution)/shard_map/ppermute | solution.py:383
  1.7 8.9 %collective-permute-start.4 = (bf16[9,64,256]{2,1,0:T(8,128)(2,1)S(1)}, bf16[9,64,256]{2,1,0:T(8,128)(2,1)S(1)}, u32[]{:S(2)}, u32[]{:S(2)}) collective-permute-start(bf16[9,64,256]{2,1,0:T(8,128)(2,1)S(1)} %dynamic-slice_bitcast_fusion.own_ref), channel_id=1, source_target_pairs={{0,1},{1,0},{2,4},{3,5},{4,2},{5,3},{6,7},{7,6},{8,9},{9,8},{10,12... | collective-permute-start | bytes 884744 | tf_op jit(solution)/shard_map/ppermute | solution.py:380
  2.9 3.4 %collective-permute-start.2 = (bf16[256,256]{1,0:T(8,128)(2,1)S(1)}, bf16[256,256]{1,0:T(8,128)(2,1)S(1)}, u32[]{:S(2)}, u32[]{:S(2)}) collective-permute-start(bf16[256,256]{1,0:T(8,128)(2,1)S(1)} %get-tuple-element.32), channel_id=1, source_target_pairs={{0,1},{1,0},{2,3},{3,2},{4,5},{5,4},{6,7},{7,6},{8,9},{9,8},{10,11... | collective-permute-start | bytes 393224 | tf_op jit(solution)/shard_map/ppermute | solution.py:399
  4.0 9.8 %collective-permute-start.8 = (bf16[9,64,256]{2,1,0:T(8,128)(2,1)S(1)}, bf16[9,64,256]{2,1,0:T(8,128)(2,1)S(1)}, u32[]{:S(2)}, u32[]{:S(2)}) collective-permute-start(bf16[9,64,256]{2,1,0:T(8,128)(2,1)S(1)} %dynamic-slice_bitcast_fusion.own_ref), channel_id=1, source_target_pairs={{0,2},{2,0},{4,6},{6,4},{1,3},{3,1},{5,7},{7,5},{8,10},{10,8},{12,... | collective-permute-start | bytes 884744 | tf_op jit(solution)/shard_map/ppermute | solution.py:377
  5.6 5.0 %collective-permute-start.3 = (s32[4,32]{1,0:T(4,128)S(1)}, s32[4,32]{1,0:T(4,128)S(1)}, u32[]{:S(2)}, u32[]{:S(2)}) collective-permute-start(s32[4,32]{1,0:T(4,128)S(1)} %pad_add_fusion.info_a), channel_id=1, source_target_pairs={{0,1},{1,0},{2,3},{3,2},{4,5},{5,4},{6,7},{7,6},{8,9},{9,8},{10,11... | collective-permute-start | bytes 1544 | tf_op jit(solution)/shard_map/ppermute | solution.py:386
  9.0 2.6 %collective-permute-start.1 = (bf16[256,256]{1,0:T(8,128)(2,1)S(1)}, bf16[256,256]{1,0:T(8,128)(2,1)S(1)}, u32[]{:S(2)}, u32[]{:S(2)}) collective-permute-start(bf16[256,256]{1,0:T(8,128)(2,1)S(1)} %get-tuple-element.34), channel_id=1, source_target_pairs={{0,1},{1,0},{2,3},{3,2},{4,5},{5,4},{6,7},{7,6},{8,9},{9,8},{10,11... | collective-permute-start | bytes 393224 | tf_op jit(solution)/shard_map/ppermute | solution.py:402
  12.4 8.3 %collective-permute-start.5 = (bf16[9,64,256]{2,1,0:T(8,128)(2,1)S(1)}, bf16[9,64,256]{2,1,0:T(8,128)(2,1)S(1)}, u32[]{:S(2)}, u32[]{:S(2)}) collective-permute-start(bf16[9,64,256]{2,1,0:T(8,128)(2,1)S(1)} %broadcast_select_fusion.3), channel_id=1, source_target_pairs={{0,2},{2,0},{4,6},{6,4},{1,3},{3,1},{5,7},{7,5},{8,10},{10,8},{12,... | collective-permute-start | bytes 884744 | tf_op jit(solution)/shard_map/ppermute | solution.py:377
  13.8 7.9 %collective-permute-start.9 = (bf16[9,64,256]{2,1,0:T(8,128)(2,1)S(1)}, bf16[9,64,256]{2,1,0:T(8,128)(2,1)S(1)}, u32[]{:S(2)}, u32[]{:S(2)}) collective-permute-start(bf16[9,64,256]{2,1,0:T(8,128)(2,1)S(1)} %collective-permute-done.8.near_ref), channel_id=1, source_target_pairs={{0,1},{1,0},{2,4},{3,5},{4,2},{5,3},{6,7},{7,6},{8,9},{9,8},{10,12... | collective-permute-start | bytes 884744 | tf_op jit(solution)/shard_map/ppermute | solution.py:380
  20.8 7.4 %collective-permute-start.6 = (bf16[9,64,256]{2,1,0:T(8,128)(2,1)S(1)}, bf16[9,64,256]{2,1,0:T(8,128)(2,1)S(1)}, u32[]{:S(2)}, u32[]{:S(2)}) collective-permute-start(bf16[9,64,256]{2,1,0:T(8,128)(2,1)S(1)} %get-tuple-element.31), channel_id=1, source_target_pairs={{0,1},{1,0},{2,4},{3,5},{4,2},{5,3},{6,7},{7,6},{8,9},{9,8},{10,12... | collective-permute-start | bytes 884744 | tf_op jit(solution)/shard_map/ppermute | solution.py:380
  21.7 8.1 %collective-permute-start.10 = (bf16[9,64,256]{2,1,0:T(8,128)(2,1)S(1)}, bf16[9,64,256]{2,1,0:T(8,128)(2,1)S(1)}, u32[]{:S(2)}, u32[]{:S(2)}) collective-permute-start(bf16[9,64,256]{2,1,0:T(8,128)(2,1)S(1)} %broadcast_select_fusion.1), channel_id=1, source_target_pairs={{0,2},{2,0},{4,6},{6,4},{1,3},{3,1},{5,7},{7,5},{8,10},{10,8},{12,... | collective-permute-start | bytes 884744 | tf_op jit(solution)/shard_map/ppermute | solution.py:377
  28.2 7.5 %collective-permute-start.7 = (bf16[9,64,256]{2,1,0:T(8,128)(2,1)S(1)}, bf16[9,64,256]{2,1,0:T(8,128)(2,1)S(1)}, u32[]{:S(2)}, u32[]{:S(2)}) collective-permute-start(bf16[9,64,256]{2,1,0:T(8,128)(2,1)S(1)} %add_select_fusion), channel_id=1, source_target_pairs={{0,2},{2,0},{4,6},{6,4},{1,3},{3,1},{5,7},{7,5},{8,10},{10,8},{12,... | collective-permute-start | bytes 884744 | tf_op jit(solution)/shard_map/ppermute | solution.py:377
  29.9 7.0 %collective-permute-start.12 = (bf16[9,64,256]{2,1,0:T(8,128)(2,1)S(1)}, bf16[9,64,256]{2,1,0:T(8,128)(2,1)S(1)}, u32[]{:S(2)}, u32[]{:S(2)}) collective-permute-start(bf16[9,64,256]{2,1,0:T(8,128)(2,1)S(1)} %get-tuple-element.28), channel_id=1, source_target_pairs={{0,1},{1,0},{2,4},{3,5},{4,2},{5,3},{6,7},{7,6},{8,9},{9,8},{10,12... | collective-permute-start | bytes 884744 | tf_op jit(solution)/shard_map/ppermute | solution.py:380
  31.2 3.5 %collective-permute-start.11 = (bf16[256,256]{1,0:T(8,128)(2,1)S(1)}, bf16[256,256]{1,0:T(8,128)(2,1)S(1)}, u32[]{:S(2)}, u32[]{:S(2)}) collective-permute-start(bf16[256,256]{1,0:T(8,128)(2,1)S(1)} %get-tuple-element.24), channel_id=1, source_target_pairs={{0,1},{1,0},{2,3},{3,2},{4,5},{5,4},{6,7},{7,6},{8,9},{9,8},{10,11... | collective-permute-start | bytes 393224 | tf_op jit(solution)/shard_map/ppermute | solution.py:469
  37.0 3.7 %collective-permute-start.13 = (bf16[9,64,256]{2,1,0:T(8,128)(2,1)S(1)}, bf16[9,64,256]{2,1,0:T(8,128)(2,1)S(1)}, u32[]{:S(2)}, u32[]{:S(2)}) collective-permute-start(bf16[9,64,256]{2,1,0:T(8,128)(2,1)S(1)} %add_convert_fusion.half_ref), channel_id=1, source_target_pairs={{0,1},{1,0},{2,3},{3,2},{4,5},{5,4},{6,7},{7,6},{8,9},{9,8},{10,11... | collective-permute-start | bytes 884744 | tf_op jit(solution)/shard_map/ppermute | solution.py:480

commit v7 on v5

--- a/solution.py
+++ b/solution.py
@@ -336,7 +336,7 @@
         ],
         input_output_aliases={} if begun is None else {2: 0},
         compiler_params=pltpu.CompilerParams(vmem_limit_bytes=VMEM_LIMIT),
-        cost_estimate=pl.CostEstimate(flops=1000, bytes_accessed=600_000, transcendentals=0),
+        cost_estimate=pl.CostEstimate(flops=1000, bytes_accessed=1000, transcendentals=0),
     )(*operands)
 
 
@@ -391,7 +391,7 @@
         copy_kernel,
         (jax.ShapeDtypeStruct(inner_weights.shape, inner_weights.dtype),),
         [],
-        20_000_000_000,
+        8_000_000_000,
         inner_weights,
     )
     act_rows = activations[0].reshape(rows, channels)

time: 42 us -> 42 us (level)
  no operation moved by 1% of the time
where the time goes in v7:
time: 42 us; the launch traced here: 41.7 us
  waiting for transfers between devices  17.2 us (41%)
  starting transfers between devices  13.4 us (32%)
  Pallas kernels  6.68 us (16%)
  other arithmetic  1.84 us (4%)
  local copies, waits for them, and re-layouts  1.78 us (4%)
  between operations  0.76 us (2%)
    ppermute x4, waiting for transfers between devices, near(): return lax.ppermute(array, 'expert', NEAR_PAIRS)  7.56 us
    ppermute x4, waiting for transfers between devices, across(): return lax.ppermute(array, ('expert', 'dp'), inner_pairs())  5.03 us
    pallas_call x6, Pallas kernels, local_call(): pl.pallas_call(kernel, out_shape=tuple(outs), in_specs=on_vmem(len(operan...  4.88 us
    ppermute x4, starting transfers between devices, near(): return lax.ppermute(array, 'expert', NEAR_PAIRS)  4.05 us
    ppermute x1, starting transfers between devices, weights_travel(): grad_back = lax.ppermute(grad_other, 'dp', SWAP)  2.56 us
    ppermute x1, starting transfers between devices, weights_travel(): kernel_other = lax.ppermute(kernel_mine, 'dp', SWAP)  2.53 us
    ppermute x1, waiting for transfers between devices, from_next(): lax.ppermute(array, 'segment', [((s + 1) % sections, s) for s in range(se...  2.39 us
    pallas_call x2, Pallas kernels, place_half(): pl.pallas_call(functools.partial(place_half_kernel, scale, side), out_sha...  1.8 us
  transfers between devices with their start and end apart: 14, of which 10 were waited for; matrix products, arithmetic and copies ran while one was open for 7% of the time, Pallas kernels for 14%

profile of v7, /device:TPU:19, one launch (start us, length us, event | category | flops | bytes accessed | tf_op | source)
XLA Modules:
  0.0 41.7 jit_solution(10153387431189887738)
XLA Ops:
  1.0 0.7 %copy-done = bf16[1,1,9,64,512]{4,3,2,1,0:T(8,128)(2,1)S(1)} copy-done((bf16[1,1,9,64,512]{4,3,2,1,0:T(8,128)(2,1)S(1)}, bf16[1,1,9,64,512]{4,3,2,1,0:T(8,128)(2,1)}, u32[]{:S(2)}) %copy-start) | copy-done | bytes 589848
  2.0 1.0 %constant_dynamic-slice_fusion = (bf16[256,256]{1,0:T(8,128)(2,1)S(1)}, bf16[256,256]{1,0:T(8,128)(2,1)S(1)}) fusion(bf16[256,512]{1,0:T(8,128)(2,1)} %bitcast.18, s32[]{:T(128)S(6)} %select_n.50, s32[]{:T(128)S(6)} %select_n.49), kind=kLoop, calls=%fused_computation.9 | loop fusion | bytes 524296 | tf_op jit(solution)/shard_map/dynamic_slice | solution.py:374
  2.9 1.0 %collective-permute-start.2 = (bf16[256,256]{1,0:T(8,128)(2,1)S(1)}, bf16[256,256]{1,0:T(8,128)(2,1)S(1)}, u32[]{:S(2)}, u32[]{:S(2)}) collective-permute-start(bf16[256,256]{1,0:T(8,128)(2,1)S(1)} %get-tuple-element.32), channel_id=1, source_target_pairs={{0,1},{1,0},{2,3},{3,2},{4,5},{5,4},{6,7},{7,6},{8,9},{9,8},{10,11... | collective-permute-start | bytes 393224 | tf_op jit(solution)/shard_map/ppermute | solution.py:399
  4.0 0.9 %collective-permute-start.8 = (bf16[9,64,256]{2,1,0:T(8,128)(2,1)S(1)}, bf16[9,64,256]{2,1,0:T(8,128)(2,1)S(1)}, u32[]{:S(2)}, u32[]{:S(2)}) collective-permute-start(bf16[9,64,256]{2,1,0:T(8,128)(2,1)S(1)} %dynamic-slice_bitcast_fusion.own_ref), channel_id=1, source_target_pairs={{0,2},{2,0},{4,6},{6,4},{1,3},{3,1},{5,7},{7,5},{8,10},{10,8},{12,... | collective-permute-start | bytes 884744 | tf_op jit(solution)/shard_map/ppermute | solution.py:377
  5.6 0.7 %collective-permute-start.3 = (s32[4,32]{1,0:T(4,128)S(1)}, s32[4,32]{1,0:T(4,128)S(1)}, u32[]{:S(2)}, u32[]{:S(2)}) collective-permute-start(s32[4,32]{1,0:T(4,128)S(1)} %pad_add_fusion.info_a), channel_id=1, source_target_pairs={{0,1},{1,0},{2,3},{3,2},{4,5},{5,4},{6,7},{7,6},{8,9},{9,8},{10,11... | collective-permute-start | bytes 1544 | tf_op jit(solution)/shard_map/ppermute | solution.py:386
  6.6 2.4 %collective-permute-done = bf16[256,512]{1,0:T(8,128)(2,1)S(1)} collective-permute-done((bf16[256,512]{1,0:T(8,128)(2,1)}, bf16[256,512]{1,0:T(8,128)(2,1)S(1)}, u32[]{:S(2)}, u32[]{:S(2)}) %collective-permute-start) | collective-permute-done | bytes 262176 | tf_op jit(solution)/shard_map/ppermute | solution.py:383
  9.0 1.6 %collective-permute-start.1 = (bf16[256,256]{1,0:T(8,128)(2,1)S(1)}, bf16[256,256]{1,0:T(8,128)(2,1)S(1)}, u32[]{:S(2)}, u32[]{:S(2)}) collective-permute-start(bf16[256,256]{1,0:T(8,128)(2,1)S(1)} %get-tuple-element.34), channel_id=1, source_target_pairs={{0,1},{1,0},{2,3},{3,2},{4,5},{5,4},{6,7},{7,6},{8,9},{9,8},{10,11... | collective-permute-start | bytes 393224 | tf_op jit(solution)/shard_map/ppermute | solution.py:402
  10.7 0.9 %collective-permute-done.1.grad_b = bf16[256,256]{1,0:T(8,128)(2,1)S(1)} collective-permute-done((bf16[256,256]{1,0:T(8,128)(2,1)S(1)}, bf16[256,256]{1,0:T(8,128)(2,1)S(1)}, u32[]{:S(2)}, u32[]{:S(2)}) %collective-permute-start.1) | collective-permute-done | bytes 131104 | tf_op jit(solution)/shard_map/ppermute | solution.py:402
  11.6 0.8 %shard_map.69 = (bf16[512,256]{1,0:T(8,128)(2,1)S(1)}, f32[64,128]{1,0:T(8,128)S(1)}, bf16[9,64,256]{2,1,0:T(8,128)(2,1)S(1)}) custom-call(bf16[256,256]{1,0:T(8,128)(2,1)S(1)} %get-tuple-element.35.grad_a, bf16[256,256]{1,0:T(8,128)(2,1)S(1)} %collective-permute-done.1.grad_b, bf16[3,256,512]{2,1,0:T(8,128)(2,1)S(1)} %shard_map.68.turned, ...), custom_call_target="tpu_custom_call" | custom-call | flops 600000000 | bytes 1000 | tf_op jit(solution)/shard_map/pallas_call | solution.py:348
  12.4 1.4 %collective-permute-start.5 = (bf16[9,64,256]{2,1,0:T(8,128)(2,1)S(1)}, bf16[9,64,256]{2,1,0:T(8,128)(2,1)S(1)}, u32[]{:S(2)}, u32[]{:S(2)}) collective-permute-start(bf16[9,64,256]{2,1,0:T(8,128)(2,1)S(1)} %broadcast_select_fusion.3), channel_id=1, source_target_pairs={{0,2},{2,0},{4,6},{6,4},{1,3},{3,1},{5,7},{7,5},{8,10},{10,8},{12,... | collective-permute-start | bytes 884744 | tf_op jit(solution)/shard_map/ppermute | solution.py:377
  13.9 1.5 %shard_map.70 = (bf16[4,512,256]{2,1,0:T(8,128)(2,1)S(1)}, bf16[9,64,256]{2,1,0:T(8,128)(2,1)S(1)}, bf16[9,64,256]{2,1,0:T(8,128)(2,1)S(1)}, f32[9,64,256]{2,1,0:T(8,128)S(1)}) custom-call(bf16[512,256]{1,0:T(8,128)(2,1)S(1)} %get-tuple-element.15.cells, f32[64,128]{1,0:T(8,128)S(1)} %get-tuple-element.16.gates, bf16[3,256,512]{2,1,0:T(8,128)(2,1)S(1)} %shard_map.68.turned), custom_call_target="tpu_custom_call" | custom-call | flops 1200000000 | bytes 1000 | tf_op jit(solution)/shard_map/pallas_call | solution.py:348
  15.4 5.4 %collective-permute-done.5 = bf16[9,64,256]{2,1,0:T(8,128)(2,1)S(1)} collective-permute-done((bf16[9,64,256]{2,1,0:T(8,128)(2,1)S(1)}, bf16[9,64,256]{2,1,0:T(8,128)(2,1)S(1)}, u32[]{:S(2)}, u32[]{:S(2)}) %collective-permute-start.5) | collective-permute-done | bytes 294944 | tf_op jit(solution)/shard_map/ppermute | solution.py:377
  21.7 1.7 %collective-permute-start.10 = (bf16[9,64,256]{2,1,0:T(8,128)(2,1)S(1)}, bf16[9,64,256]{2,1,0:T(8,128)(2,1)S(1)}, u32[]{:S(2)}, u32[]{:S(2)}) collective-permute-start(bf16[9,64,256]{2,1,0:T(8,128)(2,1)S(1)} %broadcast_select_fusion.2), channel_id=1, source_target_pairs={{0,2},{2,0},{4,6},{6,4},{1,3},{3,1},{5,7},{7,5},{8,10},{10,8},{12,... | collective-permute-start | bytes 884744 | tf_op jit(solution)/shard_map/ppermute | solution.py:377
  23.4 1.6 %shard_map.72.early = f32[512,256]{1,0:T(8,128)S(1)} custom-call(bf16[4,512,256]{2,1,0:T(8,128)(2,1)S(1)} %get-tuple-element.21.scaled_ref, bf16[9,64,256]{2,1,0:T(8,128)(2,1)S(1)} %dynamic-slice_bitcast_fusion.own_ref, bf16[9,64,256]{2,1,0:T(8,128)(2,1)S(1)} %collective-permute-done.8.near_ref, bf16[9,64,256]{2,1,0:T(8,128)(2,1)S(1)} %get-tuple-element.30.mid_ref), custom_call_target="tpu_custom_call" | custom-call | flops 1200000000 | bytes 1000 | tf_op jit(solution)/shard_map/pallas_call | solution.py:348
  25.0 3.1 %collective-permute-done.6 = bf16[9,64,256]{2,1,0:T(8,128)(2,1)S(1)} collective-permute-done((bf16[9,64,256]{2,1,0:T(8,128)(2,1)S(1)}, bf16[9,64,256]{2,1,0:T(8,128)(2,1)S(1)}, u32[]{:S(2)}, u32[]{:S(2)}) %collective-permute-start.6) | collective-permute-done | bytes 294944 | tf_op jit(solution)/shard_map/ppermute | solution.py:380
  28.3 1.6 %collective-permute-done.10 = bf16[9,64,256]{2,1,0:T(8,128)(2,1)S(1)} collective-permute-done((bf16[9,64,256]{2,1,0:T(8,128)(2,1)S(1)}, bf16[9,64,256]{2,1,0:T(8,128)(2,1)S(1)}, u32[]{:S(2)}, u32[]{:S(2)}) %collective-permute-start.10) | collective-permute-done | bytes 294944 | tf_op jit(solution)/shard_map/ppermute | solution.py:377
  30.0 0.7 %shard_map.73 = (bf16[256,256]{1,0:T(8,128)(2,1)S(1)}, bf16[256,256]{1,0:T(8,128)(2,1)S(1)}) custom-call(bf16[4,512,256]{2,1,0:T(8,128)(2,1)S(1)} %get-tuple-element.21.scaled_ref, bf16[9,64,256]{2,1,0:T(8,128)(2,1)S(1)} %get-tuple-element.29.far_ref, f32[512,256]{1,0:T(8,128)S(1)} %shard_map.72.early, bf16[256,256]{1,0:T(8,128)(2,1)S(1)} %get-tuple-element.35.grad_a, ...), custom_call_target="tpu_custom_call" | custom-call | flops 500000000 | bytes 1000 | tf_op jit(solution)/shard_map/pallas_call | solution.py:348
  30.7 2.6 %collective-permute-start.11 = (bf16[256,256]{1,0:T(8,128)(2,1)S(1)}, bf16[256,256]{1,0:T(8,128)(2,1)S(1)}, u32[]{:S(2)}, u32[]{:S(2)}) collective-permute-start(bf16[256,256]{1,0:T(8,128)(2,1)S(1)} %get-tuple-element.24), channel_id=1, source_target_pairs={{0,1},{1,0},{2,3},{3,2},{4,5},{5,4},{6,7},{7,6},{8,9},{9,8},{10,11... | collective-permute-start | bytes 393224 | tf_op jit(solution)/shard_map/ppermute | solution.py:469
  33.3 1.0 %collective-permute-done.11 = bf16[256,256]{1,0:T(8,128)(2,1)S(1)} collective-permute-done((bf16[256,256]{1,0:T(8,128)(2,1)S(1)}, bf16[256,256]{1,0:T(8,128)(2,1)S(1)}, u32[]{:S(2)}, u32[]{:S(2)}) %collective-permute-start.11) | collective-permute-done | bytes 131104 | tf_op jit(solution)/shard_map/ppermute | solution.py:469
  34.3 0.8 %maximum_select_fusion = bf16[32,8,512]{2,1,0:T(8,128)(2,1)} fusion(bf16[32,8,256]{2,1,0:T(8,128)(2,1)S(1)} %bitcast.19, bf16[32,8,256]{2,1,0:T(8,128)(2,1)S(1)} %bitcast.15, pred[]{:T(512)S(6)} %eq.11), kind=kLoop, calls=%fused_computation.7 | loop fusion | flops 1179648 | bytes 524289 | tf_op jit(solution)/shard_map/jit(_where)/select_n | solution.py:472
  35.7 1.2 %collective-permute-done.12 = bf16[9,64,256]{2,1,0:T(8,128)(2,1)S(1)} collective-permute-done((bf16[9,64,256]{2,1,0:T(8,128)(2,1)S(1)}, bf16[9,64,256]{2,1,0:T(8,128)(2,1)S(1)}, u32[]{:S(2)}, u32[]{:S(2)}) %collective-permute-start.12) | collective-permute-done | bytes 294944 | tf_op jit(solution)/shard_map/ppermute | solution.py:380
  37.0 2.5 %collective-permute-start.13 = (bf16[9,64,256]{2,1,0:T(8,128)(2,1)S(1)}, bf16[9,64,256]{2,1,0:T(8,128)(2,1)S(1)}, u32[]{:S(2)}, u32[]{:S(2)}) collective-permute-start(bf16[9,64,256]{2,1,0:T(8,128)(2,1)S(1)} %add_convert_fusion.half_ref), channel_id=1, source_target_pairs={{0,1},{1,0},{2,3},{3,2},{4,5},{5,4},{6,7},{7,6},{8,9},{9,8},{10,11... | collective-permute-start | bytes 884744 | tf_op jit(solution)/shard_map/ppermute | solution.py:480
  39.6 0.9 %shard_map.74.refs_0_ = f32[9,64,512]{2,1,0:T(8,128)} custom-call(s32[1]{0:T(128)} %bitcast.10.core_ref, bf16[9,64,256]{2,1,0:T(8,128)(2,1)S(1)} %add_convert_fusion.half_ref), custom_call_target="tpu_custom_call" | custom-call | flops 1000 | bytes 1000 | tf_op jit(solution)/shard_map/pallas_call | solution.py:328
  40.8 0.9 %shard_map.75 = f32[9,64,512]{2,1,0:T(8,128)} custom-call(s32[1]{0:T(128)} %bitcast.10.core_ref, bf16[9,64,256]{2,1,0:T(8,128)(2,1)S(1)} %collective-permute-done.13.half_ref, f32[9,64,512]{2,1,0:T(8,128)} %shard_map.74.refs_0_), custom_call_target="tpu_custom_call", output_to_operand_aliasing={{}: (2, {})} | custom-call | flops 1000 | bytes 1000 | tf_op jit(solution)/shard_map/pallas_call | solution.py:328
  (25 shorter events, 4.0 us)
Async XLA Ops:
  0.6 1.1 %copy-start = (bf16[1,1,9,64,512]{4,3,2,1,0:T(8,128)(2,1)S(1)}, bf16[1,1,9,64,512]{4,3,2,1,0:T(8,128)(2,1)}, u32[]{:S(2)}) copy-start(bf16[1,1,9,64,512]{4,3,2,1,0:T(8,128)(2,1)} %param.9) | copy-start | bytes 1769476
  0.6 8.3 %collective-permute-start = (bf16[256,512]{1,0:T(8,128)(2,1)}, bf16[256,512]{1,0:T(8,128)(2,1)S(1)}, u32[]{:S(2)}, u32[]{:S(2)}) collective-permute-start(bf16[256,512]{1,0:T(8,128)(2,1)} %bitcast.22), channel_id=1, source_target_pairs={{8,0},{16,8},{24,16},{0,24},{9,1},{17,9},{25,17},{1,25},{10,2},{18... | collective-permute-start | bytes 786440 | tf_op jit(solution)/shard_map/ppermute | solution.py:383
  1.7 8.9 %collective-permute-start.4 = (bf16[9,64,256]{2,1,0:T(8,128)(2,1)S(1)}, bf16[9,64,256]{2,1,0:T(8,128)(2,1)S(1)}, u32[]{:S(2)}, u32[]{:S(2)}) collective-permute-start(bf16[9,64,256]{2,1,0:T(8,128)(2,1)S(1)} %dynamic-slice_bitcast_fusion.own_ref), channel_id=1, source_target_pairs={{0,1},{1,0},{2,4},{3,5},{4,2},{5,3},{6,7},{7,6},{8,9},{9,8},{10,12... | collective-permute-start | bytes 884744 | tf_op jit(solution)/shard_map/ppermute | solution.py:380
  2.9 3.4 %collective-permute-start.2 = (bf16[256,256]{1,0:T(8,128)(2,1)S(1)}, bf16[256,256]{1,0:T(8,128)(2,1)S(1)}, u32[]{:S(2)}, u32[]{:S(2)}) collective-permute-start(bf16[256,256]{1,0:T(8,128)(2,1)S(1)} %get-tuple-element.32), channel_id=1, source_target_pairs={{0,1},{1,0},{2,3},{3,2},{4,5},{5,4},{6,7},{7,6},{8,9},{9,8},{10,11... | collective-permute-start | bytes 393224 | tf_op jit(solution)/shard_map/ppermute | solution.py:399
  4.0 9.8 %collective-permute-start.8 = (bf16[9,64,256]{2,1,0:T(8,128)(2,1)S(1)}, bf16[9,64,256]{2,1,0:T(8,128)(2,1)S(1)}, u32[]{:S(2)}, u32[]{:S(2)}) collective-permute-start(bf16[9,64,256]{2,1,0:T(8,128)(2,1)S(1)} %dynamic-slice_bitcast_fusion.own_ref), channel_id=1, source_target_pairs={{0,2},{2,0},{4,6},{6,4},{1,3},{3,1},{5,7},{7,5},{8,10},{10,8},{12,... | collective-permute-start | bytes 884744 | tf_op jit(solution)/shard_map/ppermute | solution.py:377
  5.6 5.0 %collective-permute-start.3 = (s32[4,32]{1,0:T(4,128)S(1)}, s32[4,32]{1,0:T(4,128)S(1)}, u32[]{:S(2)}, u32[]{:S(2)}) collective-permute-start(s32[4,32]{1,0:T(4,128)S(1)} %pad_add_fusion.info_a), channel_id=1, source_target_pairs={{0,1},{1,0},{2,3},{3,2},{4,5},{5,4},{6,7},{7,6},{8,9},{9,8},{10,11... | collective-permute-start | bytes 1544 | tf_op jit(solution)/shard_map/ppermute | solution.py:386
  9.0 2.6 %collective-permute-start.1 = (bf16[256,256]{1,0:T(8,128)(2,1)S(1)}, bf16[256,256]{1,0:T(8,128)(2,1)S(1)}, u32[]{:S(2)}, u32[]{:S(2)}) collective-permute-start(bf16[256,256]{1,0:T(8,128)(2,1)S(1)} %get-tuple-element.34), channel_id=1, source_target_pairs={{0,1},{1,0},{2,3},{3,2},{4,5},{5,4},{6,7},{7,6},{8,9},{9,8},{10,11... | collective-permute-start | bytes 393224 | tf_op jit(solution)/shard_map/ppermute | solution.py:402
  12.4 8.3 %collective-permute-start.5 = (bf16[9,64,256]{2,1,0:T(8,128)(2,1)S(1)}, bf16[9,64,256]{2,1,0:T(8,128)(2,1)S(1)}, u32[]{:S(2)}, u32[]{:S(2)}) collective-permute-start(bf16[9,64,256]{2,1,0:T(8,128)(2,1)S(1)} %broadcast_select_fusion.3), channel_id=1, source_target_pairs={{0,2},{2,0},{4,6},{6,4},{1,3},{3,1},{5,7},{7,5},{8,10},{10,8},{12,... | collective-permute-start | bytes 884744 | tf_op jit(solution)/shard_map/ppermute | solution.py:377
  13.8 7.9 %collective-permute-start.9 = (bf16[9,64,256]{2,1,0:T(8,128)(2,1)S(1)}, bf16[9,64,256]{2,1,0:T(8,128)(2,1)S(1)}, u32[]{:S(2)}, u32[]{:S(2)}) collective-permute-start(bf16[9,64,256]{2,1,0:T(8,128)(2,1)S(1)} %collective-permute-done.8.near_ref), channel_id=1, source_target_pairs={{0,1},{1,0},{2,4},{3,5},{4,2},{5,3},{6,7},{7,6},{8,9},{9,8},{10,12... | collective-permute-start | bytes 884744 | tf_op jit(solution)/shard_map/ppermute | solution.py:380
  20.8 7.4 %collective-permute-start.6 = (bf16[9,64,256]{2,1,0:T(8,128)(2,1)S(1)}, bf16[9,64,256]{2,1,0:T(8,128)(2,1)S(1)}, u32[]{:S(2)}, u32[]{:S(2)}) collective-permute-start(bf16[9,64,256]{2,1,0:T(8,128)(2,1)S(1)} %get-tuple-element.31), channel_id=1, source_target_pairs={{0,1},{1,0},{2,4},{3,5},{4,2},{5,3},{6,7},{7,6},{8,9},{9,8},{10,12... | collective-permute-start | bytes 884744 | tf_op jit(solution)/shard_map/ppermute | solution.py:380
  21.7 8.1 %collective-permute-start.10 = (bf16[9,64,256]{2,1,0:T(8,128)(2,1)S(1)}, bf16[9,64,256]{2,1,0:T(8,128)(2,1)S(1)}, u32[]{:S(2)}, u32[]{:S(2)}) collective-permute-start(bf16[9,64,256]{2,1,0:T(8,128)(2,1)S(1)} %broadcast_select_fusion.2), channel_id=1, source_target_pairs={{0,2},{2,0},{4,6},{6,4},{1,3},{3,1},{5,7},{7,5},{8,10},{10,8},{12,... | collective-permute-start | bytes 884744 | tf_op jit(solution)/shard_map/ppermute | solution.py:377
  28.2 7.5 %collective-permute-start.7 = (bf16[9,64,256]{2,1,0:T(8,128)(2,1)S(1)}, bf16[9,64,256]{2,1,0:T(8,128)(2,1)S(1)}, u32[]{:S(2)}, u32[]{:S(2)}) collective-permute-start(bf16[9,64,256]{2,1,0:T(8,128)(2,1)S(1)} %add_select_fusion), channel_id=1, source_target_pairs={{0,2},{2,0},{4,6},{6,4},{1,3},{3,1},{5,7},{7,5},{8,10},{10,8},{12,... | collective-permute-start | bytes 884744 | tf_op jit(solution)/shard_map/ppermute | solution.py:377
  29.9 7.0 %collective-permute-start.12 = (bf16[9,64,256]{2,1,0:T(8,128)(2,1)S(1)}, bf16[9,64,256]{2,1,0:T(8,128)(2,1)S(1)}, u32[]{:S(2)}, u32[]{:S(2)}) collective-permute-start(bf16[9,64,256]{2,1,0:T(8,128)(2,1)S(1)} %get-tuple-element.28), channel_id=1, source_target_pairs={{0,1},{1,0},{2,4},{3,5},{4,2},{5,3},{6,7},{7,6},{8,9},{9,8},{10,12... | collective-permute-start | bytes 884744 | tf_op jit(solution)/shard_map/ppermute | solution.py:380
  30.7 3.5 %collective-permute-start.11 = (bf16[256,256]{1,0:T(8,128)(2,1)S(1)}, bf16[256,256]{1,0:T(8,128)(2,1)S(1)}, u32[]{:S(2)}, u32[]{:S(2)}) collective-permute-start(bf16[256,256]{1,0:T(8,128)(2,1)S(1)} %get-tuple-element.24), channel_id=1, source_target_pairs={{0,1},{1,0},{2,3},{3,2},{4,5},{5,4},{6,7},{7,6},{8,9},{9,8},{10,11... | collective-permute-start | bytes 393224 | tf_op jit(solution)/shard_map/ppermute | solution.py:469
  37.0 3.7 %collective-permute-start.13 = (bf16[9,64,256]{2,1,0:T(8,128)(2,1)S(1)}, bf16[9,64,256]{2,1,0:T(8,128)(2,1)S(1)}, u32[]{:S(2)}, u32[]{:S(2)}) collective-permute-start(bf16[9,64,256]{2,1,0:T(8,128)(2,1)S(1)} %add_convert_fusion.half_ref), channel_id=1, source_target_pairs={{0,1},{1,0},{2,3},{3,2},{4,5},{5,4},{6,7},{7,6},{8,9},{9,8},{10,11... | collective-permute-start | bytes 884744 | tf_op jit(solution)/shard_map/ppermute | solution.py:480
